TPU v7x, 32 devices: a whole 2x2x4 slice. The times are simulated.
32 devices in a mesh: feat: 4 (over y, x), ex: 8 (over z, core).
Axes of the slice: x: 2, y: 2, z: 4, core: 2. Of those that a mesh axis runs over, the one named last changes fastest.
Arguments:
- train_grads: bfloat16 [1024, 262144], P('ex', 'feat')
- target_grads: bfloat16 [256, 262144], P('ex', 'feat')
- signs: int32 [32, 8192], replicated, may hold values from -1 to 1, as said below
- block_order: int32 [32], replicated, may hold values from 0 to 31, each once
Outputs:
- train_features: bfloat16 [1024, 8192], P('ex', 'feat')
- cosines: float32 [1024, 8, 32], P('ex', None, 'feat')
Inputs may be any that keep to these rules, and one draw needn't show every extreme that they name: `signs`: every entry is +1 or -1.
All inputs are finite; a program needn't handle non-finite values.
Results may differ from a plain program's by a relative error of at most 0.013.
Values may be sent and summed in bfloat16 or wider, within the bound.
No kernel may reach another device: no remote copies, remote signals or barrier semaphores. Data moves between devices by JAX's collectives and lax.ppermute only.
A program may use at most 64 MiB of HBM per device.

v0:
```python
import math

import jax
import jax.numpy as jnp
from jax import lax
from jax.sharding import PartitionSpec as P

HIN = 512


def sign_table(order_size):
    positions = jnp.arange(order_size, dtype=jnp.int32)
    parity = jnp.zeros((order_size, order_size), jnp.int32)
    for bit_place in range(order_size.bit_length() - 1):
        parity = parity + (positions[:, None] >> bit_place & 1) * (
            positions[None, :] >> bit_place & 1
        )
    return jnp.where(parity % 2 == 0, 1.0, -1.0).astype(jnp.float32)


def normalize(projected):
    widened = projected.astype(jnp.float32)
    row_scale = lax.rsqrt(jnp.mean(widened * widened, axis=-1, keepdims=True) + 1e-06)
    return (widened * row_scale).astype(jnp.bfloat16)


def local(train_grads, target_grads, signs, block_order):
    proj_width = signs.shape[1]
    block_total = signs.shape[0]
    blocks_here = train_grads.shape[1] // proj_width
    feat_count = lax.axis_size("feat")
    feat_index = lax.axis_index("feat")
    inner_size = HIN
    outer_size = proj_width // inner_size
    inner_table = sign_table(inner_size).astype(jnp.bfloat16)
    outer_table = sign_table(outer_size)
    positions_here = feat_index * blocks_here + jnp.arange(blocks_here, dtype=jnp.int32)
    selector = (block_order[None, :] == positions_here[:, None]).astype(jnp.float32)
    local_signs = jnp.dot(selector, signs.astype(jnp.float32)).astype(jnp.bfloat16)
    local_signs = local_signs.reshape(blocks_here, outer_size, inner_size)
    full_scale = 1.0 / math.sqrt(block_total * proj_width)

    def project_terms(gradients):
        row_count = gradients.shape[0]
        signed_blocks = (
            gradients.reshape(row_count, blocks_here, outer_size, inner_size) * local_signs[None]
        )
        inner_done = jnp.einsum(
            "rtoi,ij->roj", signed_blocks, inner_table, preferred_element_type=jnp.float32
        )
        outer_done = jnp.einsum(
            "roj,ok->rkj", inner_done, outer_table, precision=lax.Precision.HIGHEST
        )
        return outer_done.reshape(row_count, proj_width) * full_scale

    train_terms = project_terms(train_grads)
    target_terms = project_terms(target_grads)
    per_device = target_grads.shape[0] // feat_count
    dims_here = proj_width // feat_count
    group_count = lax.axis_size("ex")
    train_rows = train_grads.shape[0]
    train_sum, target_sum = lax.psum((train_terms, target_terms), "feat")
    train_full = train_sum.astype(jnp.bfloat16)
    target_full = target_sum.astype(jnp.bfloat16)
    target_mine = lax.dynamic_slice_in_dim(target_full, feat_index * per_device, per_device, 0)
    train_normed = normalize(train_full)
    train_features = lax.dynamic_slice_in_dim(train_normed, feat_index * dims_here, dims_here, 1)
    products = (
        jnp.einsum(
            "rp,kp->rk",
            train_normed,
            lax.all_gather(normalize(target_mine), "ex", axis=0, tiled=True),
            preferred_element_type=jnp.float32,
        )
        / proj_width
    )
    cosines = products.reshape(train_rows, group_count, per_device)
    return (train_features, cosines)


def solution(mesh):
    placed = (P("ex", "feat"), P("ex", "feat"), P(), P())
    return jax.shard_map(
        local,
        mesh=mesh,
        in_specs=placed,
        out_specs=(P("ex", "feat"), P("ex", None, "feat")),
        check_vma=False,
    )
```

profile of v0, /device:TPU:0, one launch (start us, length us, event | category | flops | bytes accessed | tf_op | source)
XLA Modules:
  0.0 260.9 jit_solution(10348885813472967452)
XLA Ops:
  7.2 0.0 all-gather.2.cloned.1.call-start
  7.3 1.5 convolution_convert_fusion
  8.8 12.1 %copy.8 = bf16[16,8,128,512]{3,2,1,0:T(8,128)(2,1)S(1)} copy(bf16[16,8,128,512]{3,1,2,0:T(8,128)(2,1)} %bitcast.32) | data formatting | bytes 33554432
  21.0 7.5 %convert_reduce_fusion = bf16[128,16,512]{2,1,0:T(8,128)(2,1)S(1)} fusion(bf16[128,8,16,512]{3,2,1,0:T(8,128)(2,1)S(1)} %bitcast.30, bf16[8,16,512]{2,1,0:T(8,128)(2,1)S(1)} %copy.6), kind=kLoop, calls=%fused_computation | loop fusion | flops 40894464 | bytes 19005440 | tf_op jit(solution)/shard_map/rtoi,ij->roj/reduce_sum | solution.py:48
  28.5 1.9 fusion.11
  30.4 3.8 %convolution_multiply_fusion = f32[16,128,512]{2,0,1:T(8,128)S(1)} fusion(f32[128,16,512]{2,1,0:T(8,128)S(1)} %fusion.11, s32[16]{0:T(128)S(1)} %get-tuple-element.12, s32[16]{0:T(128)S(1)} %get-tuple-element.13, s32[16]{0:T(128)S(1)} %get-tuple-element.14, s32[16]{0:T(128)S(1)} %get-tuple-element.15), kind=kOutput, calls=%fused_computation.7 | convolution fusion | flops 202380288 | bytes 8388864 | tf_op jit(solution)/shard_map/roj,ok->rkj/dot_general | solution.py:51
  34.2 0.0 copy-start.1
  34.2 5.4 %copy.9 = f32[16,8,16,512]{3,1,2,0:T(8,128)} copy(f32[16,8,16,512]{3,2,1,0:T(8,128)S(1)} %bitcast.34) | data formatting | bytes 8388608
  39.6 0.0 copy-done.1
  39.6 1.5 copy.10
  41.1 1.0 convert_reduce_fusion.1
  42.1 1.7 fusion.9
  43.8 1.1 convolution_multiply_fusion.1
  44.9 0.6 copy.11
  45.5 180.1 %all-reduce.2 = (bf16[128,8192]{1,0:T(8,128)(2,1)S(1)}, bf16[32,8192]{1,0:T(8,128)(2,1)}) all-reduce(f32[128,8192]{1,0:T(8,128)} %bitcast.31, f32[32,8192]{1,0:T(8,128)S(1)} %bitcast.35), channel_id=1, replica_groups=mesh['feat'=4,'ex'=8] {'feat'}, use_global_device_ids=true, to_apply=%region_1.2 | all-reduce | flops 1310720 | bytes 7864320 | tf_op jit(solution)/shard_map/psum | solution.py:62
  225.6 0.0 copy-start
  225.6 1.2 fusion.7
  226.9 1.6 fusion.8
  228.5 0.0 all-gather.2.cloned.1.call-update
  228.5 0.5 fusion
  229.0 0.0 copy-done
  229.1 2.0 fusion.1
  231.1 0.8 constant_dynamic-slice_fusion
  231.9 19.4 %all-gather.2.cloned.1.call-done = bf16[64,8192]{1,0:T(8,128)(2,1)} async-done(((bf16[8,8192]{1,0:T(8,128)(2,1)}), bf16[64,8192]{1,0:T(8,128)(2,1)}) %all-gather.2.cloned.1.call-update) | async-done | bytes 1048592 | tf_op jit(solution)/shard_map/all_gather | solution.py:72
  251.3 2.7 %fusion.2 = f32[128,8,8]{0,2,1:T(8,128)} fusion(bf16[128,8192]{1,0:T(8,128)(2,1)S(1)} %fusion.1, bf16[64,8192]{1,0:T(8,128)(2,1)} %all-gather.2.cloned.1.call-done), kind=kOutput, calls=%fused_computation.13 | convolution fusion | flops 134225920 | bytes 3178496 | tf_op jit(solution)/shard_map/rp,kp->rk/dot_general | solution.py:69
  (11 shorter events, 0.1 us)
Async XLA Ops:
  7.2 244.2 %all-gather.2.cloned.1.call-start = ((), (), s32[]{:S(2)}) async-start(), calls=%async_computation | async-start | bytes 1179648 | tf_op jit(solution)/shard_map/all_gather | solution.py:72
  34.2 5.4 %copy-start.1 = (bf16[32,65536]{1,0:T(8,128)(2,1)S(1)}, bf16[32,65536]{1,0:T(8,128)(2,1)}, u32[]{:S(2)}) copy-start(bf16[32,65536]{1,0:T(8,128)(2,1)} %param.5) | copy-start | bytes 12582916
  225.6 3.4 %copy-start = (bf16[128,8192]{1,0:T(8,128)(2,1)}, bf16[128,8192]{1,0:T(8,128)(2,1)S(1)}, u32[]{:S(2)}) copy-start(bf16[128,8192]{1,0:T(8,128)(2,1)S(1)} %get-tuple-element.2) | copy-start | bytes 6291460
Sparse Core Ops, SparseCore 0:
  228.7 22.6 all-gather.1
where the time goes:
time: 261 us
  blocking collectives  180 us (69%)
  local copies, waits for them, and re-layouts  20.6 us (8%)
  waiting for transfers between devices  19.4 us (7%)
  between operations  14.2 us (5%)
  other arithmetic  14 us (5%)
  matrix products  12.6 us (5%)
    psum x1, blocking collectives, local(): train_sum, target_sum = lax.psum((train_terms, target_terms), 'feat')  180 us
    unnamed x8, local copies, waits for them, and re-layouts  19.7 us
    all_gather x1, waiting for transfers between devices, local(): lax.all_gather(normalize(target_mine), 'ex', axis=0, tiled=True)  19.4 us
    reduce_sum x2, other arithmetic, project_terms(): jnp.einsum('rtoi,ij->roj', signed_blocks, inner_table, preferred_element_...  8.5 us
  transfers between devices with their start and end apart: 1, of which 1 were waited for; matrix products, arithmetic and copies ran while one was open for 1% of the time, Pallas kernels for 0%

commit v1 on v0

v1 whole, which is shorter than its diff:
```python
import functools
import math

import jax
import jax.numpy as jnp
import numpy as np
from jax import lax
from jax.experimental import pallas as pl
from jax.experimental.pallas import tpu as pltpu
from jax.sharding import PartitionSpec as P

ROWS = 16
LANES = 256
CHUNKS = (48, 80)
EPS = 1e-06
MIB = 1 << 20
HBM = pl.BlockSpec(memory_space=pltpu.HBM)
SMEM = pl.BlockSpec(memory_space=pltpu.SMEM)
VMEM = pl.BlockSpec(memory_space=pltpu.VMEM)
ANY = pl.BlockSpec(memory_space=pl.ANY)


def sign_matrix(order):
    matrix = np.ones((1, 1), np.float32)
    while matrix.shape[0] < order:
        matrix = np.block([[matrix, matrix], [matrix, -matrix]])
    return matrix


def butterfly(parts):
    parts, half = list(parts), 1
    while half < len(parts):
        for i in range(len(parts)):
            if not i & half:
                a, b = parts[i], parts[i | half]
                parts[i], parts[i | half] = a + b, a - b
        half *= 2
    return parts


def wide(value):
    return value.astype(jnp.float32)


def narrow(value):
    return value.astype(jnp.bfloat16)


def diagonal(size):
    return lax.broadcasted_iota(jnp.int32, (size, size), 0) == lax.broadcasted_iota(jnp.int32, (size, size), 1)


def as_row(column):
    return jnp.sum(jnp.where(diagonal(column.shape[0]), column, 0.0), axis=0, keepdims=True)


def as_column(row):
    return jnp.sum(jnp.where(diagonal(row.shape[1]), row, 0.0), axis=1, keepdims=True)


def call(kernel, out_shape, operands, specs, name, limit=16, scratch=(), after=None, flops=10**10):
    body = kernel
    if after is not None:
        place = len(operands)
        operands, specs = [*operands, after], [*specs, ANY]

        def body(*refs):
            kernel(*refs[:place], *refs[place + 1 :])

    return pl.pallas_call(
        body,
        out_shape=out_shape,
        in_specs=specs,
        out_specs=jax.tree.map(lambda unused: VMEM, out_shape),
        scratch_shapes=scratch,
        compiler_params=pltpu.CompilerParams(vmem_limit_bytes=limit * MIB),
        cost_estimate=pl.CostEstimate(flops=flops, bytes_accessed=0, transcendentals=0),
        name=name,
    )(*operands)


def fetch(first, gradients_ref, held, sems):
    tiles, blocks = sems.shape
    width = held.shape[2] // blocks
    copies = []
    for i in range(tiles):
        row = []
        for p in range(blocks):
            span = pl.ds(p * width, width)
            copy = pltpu.make_async_copy(
                gradients_ref.at[pl.ds(first + i * ROWS, ROWS), span], held.at[i, :, span], sems.at[i, p]
            )
            copy.start()
            row.append(copy)
        copies.append(row)
    return copies


def reverse_bits(number, count):
    return sum((number >> i & 1) << (count - 1 - i) for i in range(count))


def outer_terms(feat_count, core, spread, tiles, store, make_sign=None):
    blocks, unused, width = spread.shape
    inner = width // feat_count
    lanes = min(LANES, inner)
    count = feat_count.bit_length() - 1
    places = [
        pl.multiple_of(jnp.where(core == 0, h, reverse_bits(h, count)) * inner, inner) for h in range(feat_count)
    ]

    @pl.loop(0, inner // lanes)
    def step(c):
        start = pl.multiple_of(c * lanes, lanes)
        for i, tile in enumerate(tiles):
            sums = []
            for h in range(feat_count):
                span = pl.ds(pl.multiple_of(places[h] + start, lanes), lanes)
                if make_sign is not None and i == 0:
                    for p in range(blocks):
                        spread[p, :, span] = make_sign(p, span)
                total = None
                for p in range(blocks):
                    piece = tile[:, pl.ds(pl.multiple_of(p * width + places[h] + start, lanes), lanes)]
                    term = wide(piece * spread[p, :, span])
                    total = term if total is None else total + term
                sums.append(total)
            for d, value in enumerate(butterfly(sums)):
                store(d, pl.ds(i * ROWS, ROWS), pl.ds(start, lanes), narrow(value))


def first_kernel(feat_count, feat_ref, core_ref, order_hbm, signs_hbm, gradients_ref, *refs):
    outs, (spread, held, sems, order, signs, mine, place, few) = refs[:feat_count], refs[feat_count:]
    order_copy = pltpu.make_async_copy(order_hbm, order, few.at[0])
    order_copy.start()
    copies = fetch(0, gradients_ref, held, sems)
    feat = feat_ref[0]
    blocks, unused, width = spread.shape
    inner = width // feat_count
    order_copy.wait()
    for b in range(order.shape[0]):
        place[order[b]] = b
    sign_copies = []
    for p in range(blocks):
        row = place[feat * blocks + p]
        sign_copies.append(pltpu.make_async_copy(signs_hbm.at[pl.ds(row, 1)], signs.at[pl.ds(p, 1)], few.at[1 + p]))
        sign_copies[-1].start()
    for copy in sign_copies:
        copy.wait()
    for h in range(feat_count):
        bits = feat & h
        odd = 0
        for shift in range(feat_count.bit_length() - 1):
            odd = odd ^ ((bits >> shift) & 1)
        span = pl.ds(h * inner, inner)
        mine[:, span] = wide(signs[:, span] * (1 - 2 * odd))

    def make_sign(p, span):
        return narrow(jnp.broadcast_to(mine[pl.ds(p, 1), span], (ROWS, span.size)))

    def store(d, rows, lanes, value):
        outs[d][rows, lanes] = value

    for tile in copies:
        for copy in tile:
            copy.wait()
    tiles = [held.at[i] for i in range(held.shape[0])]
    outer_terms(feat_count, core_ref[0], spread, tiles, store, make_sign)


def first_terms(feat_count, feat, core, block_order, signs, gradients):
    rows, columns = gradients.shape
    total, width = signs.shape
    blocks = columns // width
    part = jax.ShapeDtypeStruct((rows, width // feat_count), jnp.bfloat16)
    *parts, table = call(
        functools.partial(first_kernel, feat_count),
        [part] * feat_count + [jax.ShapeDtypeStruct((blocks, ROWS, width), jnp.bfloat16)],
        [feat, core, block_order, signs, gradients],
        [SMEM, SMEM, HBM, HBM, HBM],
        "first_terms",
        flops=2 * 10**10,
        limit=7,
        scratch=[
            pltpu.VMEM((rows // ROWS, ROWS, columns), jnp.bfloat16),
            pltpu.SemaphoreType.DMA((rows // ROWS, blocks)),
            pltpu.SMEM((total,), jnp.int32),
            pltpu.VMEM((blocks, width), jnp.int32),
            pltpu.VMEM((blocks, width), jnp.float32),
            pltpu.SMEM((total,), jnp.int32),
            pltpu.SemaphoreType.DMA((1 + blocks,)),
        ],
    )
    return parts, table


def halving_places(bits):
    count = len(bits)
    numbers = [sum((d >> bit & 1) << (count - 1 - i) for i, bit in enumerate(bits)) for d in range(1 << count)]
    return [divmod(number, 1 << (count - 1)) for number in numbers]


def terms_kernel(first, places, core_ref, spread, gradients_ref, *outs):
    def store(d, rows, lanes, value):
        half, place = places[d]
        outs[half][place, rows, lanes] = value

    tiles = [gradients_ref.at[pl.ds(first + i, ROWS)] for i in range(0, outs[0].shape[1], ROWS)]
    outer_terms(len(places), core_ref[0], spread, tiles, store)


def terms(bits, core, table, gradients, first, rows, after):
    blocks, unused, width = table.shape
    feat_count = 1 << len(bits)
    columns = gradients.shape[1]
    part = jax.ShapeDtypeStruct((feat_count // 2, rows, width // feat_count), jnp.bfloat16)
    return call(
        functools.partial(terms_kernel, first, halving_places(bits)),
        [part, part],
        [core, table, gradients],
        [SMEM, VMEM, VMEM],
        "terms",
        limit=4,
        after=after,
    )


def add_parts(refs, low, high):
    total = wide(refs[0][low:high])
    for ref in refs[1:]:
        total = total + wide(ref[low:high])
    return total


def middle_kernel(low, high, *refs):
    refs[-1][...] = add_parts(refs[:-1], low, high).astype(refs[-1].dtype)


def middle(parts, low, high, after):
    return call(
        functools.partial(middle_kernel, low, high),
        jax.ShapeDtypeStruct((high - low, *parts[0].shape[1:]), parts[0].dtype),
        parts,
        [VMEM] * len(parts),
        "middle",
        limit=16,
        after=after,
    )


def combine_kernel(*refs):
    refs[-1][...] = narrow(add_parts(refs[:-1], 0, refs[-1].shape[0]))


def combine(parts, after):
    return call(
        combine_kernel,
        jax.ShapeDtypeStruct(parts[0].shape, jnp.bfloat16),
        parts,
        [VMEM] * len(parts),
        "combine",
        limit=16,
        after=after,
    )


def inner_part(scale, table, t1):
    side = table.shape[0]
    parts = butterfly(
        [
            jnp.dot(t1[:, c : c + side], table, preferred_element_type=jnp.float32)
            for c in range(0, t1.shape[1], side)
        ]
    )
    return narrow(jnp.concatenate(parts, axis=1) * scale)


def inner_table(width):
    return jnp.asarray(sign_matrix(min(256, width)), jnp.bfloat16)


def stack_kernel(feat_count, per, feat_ref, *refs):
    parts, out_ref = refs[:-1], refs[-1]
    feat = feat_ref[0]
    rows, inner = parts[0].shape
    count = rows * len(parts)
    columns = []
    for i, part in enumerate(parts):
        value = part[...]
        out_ref[pl.ds(i * rows, rows), :] = value
        columns.append(square_sums(value))
    place = lax.broadcasted_iota(jnp.int32, (count, count), 1)
    source = lax.broadcasted_iota(jnp.int32, (count, count), 0)
    share = count // feat_count
    d, left = place // share, place % share
    wanted = (left // per) * rows + (d ^ feat) * per + left % per
    norms = jnp.sum(jnp.where(source == wanted, jnp.concatenate(columns, axis=0), 0.0), axis=0, keepdims=True)
    pieces = []
    for unused in range(3):
        piece = narrow(norms)
        norms = norms - wide(piece)
        pieces.append(wide(piece))
    pieces = jnp.concatenate([*pieces, jnp.zeros((ROWS - 3, count), jnp.float32)], axis=0)
    out_ref[pl.ds(count, ROWS), pl.ds(0, count)] = narrow(pieces)
    if inner > count:
        out_ref[pl.ds(count, ROWS), pl.ds(count, inner - count)] = jnp.zeros((ROWS, inner - count), jnp.bfloat16)


def stack_targets(feat_count, per, feat, parts, after):
    rows, inner = parts[0].shape
    return call(
        functools.partial(stack_kernel, feat_count, per),
        jax.ShapeDtypeStruct((rows * len(parts) + ROWS, inner), jnp.bfloat16),
        [feat, *parts],
        [SMEM] + [VMEM] * len(parts),
        "stack_targets",
        after=after,
    )


def square_sums(value):
    value = wide(value)
    return jnp.sum(value * value, axis=1, keepdims=True)


def join_kernel(counts, *refs):
    parts, (t1_ref, norms_ref) = refs[: sum(counts)], refs[sum(counts) :]
    row, norms = 0, []
    for count in counts:
        chunk, parts = parts[:count], parts[count:]
        total = narrow(add_parts(chunk, 0, 1)[0])
        t1_ref[pl.ds(row, total.shape[0]), :] = total
        row += total.shape[0]
        norms.append(square_sums(total))
    norms = as_row(jnp.concatenate(norms, axis=0))
    norms_ref[...] = jnp.concatenate([norms, jnp.zeros((7, row), jnp.float32)], axis=0)


def join(chunks):
    parts = [part for chunk in chunks for part in chunk]
    rows = sum(chunk[0].shape[1] for chunk in chunks)
    return call(
        functools.partial(join_kernel, [len(chunk) for chunk in chunks]),
        [
            jax.ShapeDtypeStruct((rows, parts[0].shape[2]), jnp.bfloat16),
            jax.ShapeDtypeStruct((8, rows), jnp.float32),
        ],
        parts,
        [VMEM] * len(parts),
        "join",
    )


def gram_kernel(per, feat_ref, t1_ref, norms_ref, mine_ref, other_ref, *refs):
    outs, products = refs[:-1], refs[-1]
    feat = feat_ref[0]
    rows = t1_ref.shape[0]
    height = mine_ref.shape[0] - ROWS
    share = height // len(outs)
    target_norms = []
    for i, ref in enumerate((mine_ref, other_ref)):
        products[pl.ds(i * height, height), :] = lax.dot_general(
            ref[pl.ds(0, height), :], t1_ref[...], (((1,), (1,)), ((), ())), preferred_element_type=jnp.float32
        )
        pieces = wide(ref[pl.ds(height, ROWS), pl.ds(0, height)])
        target_norms.append(pieces[0:1] + pieces[1:2] + pieces[2:3])
    for d, out in enumerate(outs):
        for i in range(0, 2 * share, per):
            first = pl.multiple_of((i * len(outs)) + (d ^ feat) * per, per)
            out[pl.ds(i, per), :] = products[pl.ds(first, per), :]
        span = slice(d * share, (d + 1) * share)
        here = jnp.concatenate(
            [x[:, span] for x in target_norms] + [jnp.zeros((1, rows - 2 * share), jnp.float32)], axis=1
        )
        out[pl.ds(2 * share, 8), :] = jnp.concatenate([norms_ref[0:1, :], here, jnp.zeros((6, rows), jnp.float32)], axis=0)


def gram(feat_count, per, feat, t1, norms, mine, other):
    total = 2 * (mine.shape[0] - ROWS)
    rows = t1.shape[0]
    return call(
        functools.partial(gram_kernel, per),
        [jax.ShapeDtypeStruct((total // feat_count + 8, rows), jnp.float32)] * feat_count,
        [feat, t1, norms, mine, other],
        [SMEM] + [VMEM] * 4,
        "gram",
        scratch=[pltpu.VMEM((total, rows), jnp.float32)],
    )


def inner_kernel(scale, table_ref, t1_ref, out_ref):
    out_ref[...] = inner_part(scale, table_ref[...], t1_ref[...])


def inner_transform(scale, table, t1):
    return call(
        functools.partial(inner_kernel, scale),
        jax.ShapeDtypeStruct(t1.shape, jnp.bfloat16),
        [table, t1],
        [VMEM, VMEM],
        "inner_transform",
        limit=16,
    )


def finish_kernel(mean_scale, per, ex_ref, projected_ref, *refs):
    parts, (features_ref, cosines_ref) = refs[:-2], refs[-2:]
    count = cosines_ref.shape[0]
    share = count // 2
    sums = parts[0][...]
    for part in parts[1:]:
        sums = sums + part[...]
    train_scale = lax.rsqrt(sums[count : count + 1] * mean_scale + EPS)
    target_scale = lax.rsqrt(sums[count + 1 : count + 2, :count] * mean_scale + EPS)
    cosines = sums[:count] * train_scale * as_column(target_scale) * mean_scale
    for i in range(count // per):
        group = ex_ref[0] ^ (i * 2 if i * per < share else i * 2 - count // per + 1)
        cosines_ref[pl.ds(pl.multiple_of(group * per, per), per), :] = cosines[i * per : (i + 1) * per]
    features_ref[...] = narrow(wide(projected_ref[...]) * as_column(train_scale))


def finish(mean_scale, per, ex, projected, parts):
    return call(
        functools.partial(finish_kernel, mean_scale, per),
        [
            jax.ShapeDtypeStruct(projected.shape, jnp.bfloat16),
            jax.ShapeDtypeStruct((parts[0].shape[0] - 8, projected.shape[0]), jnp.float32),
        ],
        [ex, projected, *parts],
        [SMEM] + [VMEM] * (1 + len(parts)),
        "finish",
    )


def swap(value, axis, distance):
    return lax.ppermute(value, axis, [(i, i ^ distance) for i in range(lax.axis_size(axis))])


def local(train_grads, target_grads, signs, block_order):
    train_grads, target_grads, signs, block_order = (
        pltpu.with_memory_space_constraint(value, pltpu.HBM)
        for value in (train_grads, target_grads, signs, block_order)
    )
    train_grads = pltpu.with_memory_space_constraint(train_grads, pltpu.VMEM)
    block_total, width = signs.shape
    feat_count = lax.axis_size("feat")
    groups = lax.axis_size("ex")
    feat = lax.axis_index("feat").astype(jnp.int32).reshape(1)
    ex = lax.axis_index("ex").astype(jnp.int32)
    train_rows, target_rows = train_grads.shape[0], target_grads.shape[0]
    per = target_rows // feat_count
    inner = width // feat_count
    mean_scale = 1.0 / (block_total * width * feat_count)
    scale = 1.0 / math.sqrt(block_total * width)
    table256 = inner_table(inner)
    bits = list(range(feat_count.bit_length() - 1))
    assert sum(CHUNKS) == train_rows

    core = (ex % 2).reshape(1)

    def turn(value, d):
        other = reverse_bits(d, len(bits))
        pairs = [
            (f * groups + e, (f ^ (d if e % 2 == 0 else other)) * groups + e)
            for f in range(feat_count)
            for e in range(groups)
        ]
        return lax.ppermute(value, ("feat", "ex"), pairs)

    target_parts, table = first_terms(feat_count, feat, core, block_order, signs, target_grads)
    own = pltpu.with_memory_space_constraint(target_parts[0], pltpu.VMEM)
    got = [own] + [turn(target_parts[d], d) for d in range(1, feat_count)]

    orders = [bits if i % 2 == 0 else bits[::-1] for i in range(len(CHUNKS))]
    firsts = [sum(CHUNKS[:i]) for i in range(len(CHUNKS))]

    def start(i, after):
        keep, send = terms(orders[i], core, table, train_grads, firsts[i], CHUNKS[i], after)
        return [keep, turn(send, 1 << orders[i][0])], send

    def proceed(order, parts, after):
        for bit in order[1:]:
            high = parts[-1].shape[0]
            send = after = middle(parts, high // 2, high, after)
            parts = [*parts, turn(send, 1 << bit)]
        return parts, after

    state = [None] * len(CHUNKS)
    state[0], mark = start(0, None)
    state[1], mark = start(1, mark)
    own = combine(got, mark)
    around = [own] + [swap(own, "ex", d) for d in range(2, groups, 2)]
    state[0], mark = proceed(orders[0], state[0], own)
    state[1], mark = proceed(orders[1], state[1], mark)
    mine = stack_targets(feat_count, per, feat, around, mark)
    other = swap(mine, "ex", 1)
    t1, norms = join(state)
    sums = gram(feat_count, per, feat, t1, norms, mine, other)
    far = sorted(range(1, feat_count), key=lambda d: -d.bit_count())
    sums = [sums[0]] + [swap(sums[d], "feat", d) for d in far]
    projected = inner_transform(scale, table256, t1)
    features, cosines = finish(mean_scale, per, ex.reshape(1), projected, sums)
    return features, cosines.reshape(groups, per, train_rows).transpose(2, 0, 1)


def solution(mesh):
    placed = (P("ex", "feat"), P("ex", "feat"), P(), P())
    return jax.shard_map(
        local,
        mesh=mesh,
        in_specs=placed,
        out_specs=(P("ex", "feat"), P("ex", None, "feat")),
        check_vma=False,
    )
```

time: 261 us -> 42.8 us (0.16)
  blocking collectives: 180 us -> 0 us
  local copies, waits for them, and re-layouts: 20.6 us -> 0.01 us
  starting transfers between devices: 0.04 us -> 20.1 us
  other arithmetic: 14 us -> 0 us
  between operations: 14.2 us -> 0.76 us
  matrix products: 12.6 us -> 0 us
  Pallas kernels: 0 us -> 10.7 us
  waiting for transfers between devices: 19.4 us -> 11.1 us
    psum x1 -> x0, blocking collectives: 180 us -> none  [local(): train_sum, target_sum = lax.psum((train_terms, target_terms), 'feat')]
    ppermute x0 -> x14, starting transfers between devices: none -> 20.1 us  [the longest x7 12 us: turn(): return lax.ppermute(value, ('feat', 'ex'), pairs)]
    unnamed x8 -> x4, local copies, waits for them, and re-layouts: 19.7 us -> 0.01 us
    all_gather x1 -> x0, waiting for transfers between devices: 19.4 us -> none  [local(): lax.all_gather(normalize(target_mine), 'ex', axis=0, tiled=True)]
    dot_general x6 -> x0, matrix products: 12.6 us -> none  [the longest x2 4.81 us: project_terms(): jnp.einsum('roj,ok->rkj', inner_done, outer_table, precision=lax.Precisio...]
    ppermute x0 -> x14, waiting for transfers between devices: none -> 11.1 us  [the longest x7 5.61 us: swap(): lax.ppermute(value, axis, [(i, i ^ distance) for i in range(lax.axis_size...]
    pallas_call x0 -> x11, Pallas kernels: none -> 10.7 us  [call(): pl.pallas_call(body, out_shape=out_shape, in_specs=specs, out_specs=jax.t...]
    reduce_sum x4 -> x0, other arithmetic: 10.2 us -> none  [the longest x2 8.5 us: project_terms(): jnp.einsum('rtoi,ij->roj', signed_blocks, inner_table, preferred_element_...]
  transfers between devices with their start and end apart: 1 -> 14, of which waited for: 1 -> 6; matrix products, arithmetic and copies ran while one was open for 1% -> 0% of each run, Pallas kernels for 0% -> 13%
where the time goes in v1:
time: 42.8 us; the launch traced here: 42.7 us
  starting transfers between devices  20.1 us (47%)
  waiting for transfers between devices  11.1 us (26%)
  Pallas kernels  10.7 us (25%)
  between operations  0.76 us (2%)
    ppermute x7, starting transfers between devices, turn(): return lax.ppermute(value, ('feat', 'ex'), pairs)  12 us
    pallas_call x11, Pallas kernels, call(): pl.pallas_call(body, out_shape=out_shape, in_specs=specs, out_specs=jax.t...  10.7 us
    ppermute x7, starting transfers between devices, swap(): lax.ppermute(value, axis, [(i, i ^ distance) for i in range(lax.axis_size...  8.08 us
    ppermute x7, waiting for transfers between devices, swap(): lax.ppermute(value, axis, [(i, i ^ distance) for i in range(lax.axis_size...  5.61 us
    ppermute x7, waiting for transfers between devices, turn(): return lax.ppermute(value, ('feat', 'ex'), pairs)  5.52 us
  transfers between devices with their start and end apart: 14, of which 6 were waited for; matrix products, arithmetic and copies ran while one was open for 0% of the time, Pallas kernels for 13%

profile of v1, /device:TPU:0, one launch (start us, length us, event | category | flops | bytes accessed | tf_op | source)
XLA Modules:
  0.0 42.7 jit_solution(10022961867936127453)
XLA Ops:
  0.6 0.0 copy-start
  0.7 3.9 %first_terms.1 = (bf16[32,2048]{1,0:T(8,128)(2,1)S(1)}, bf16[32,2048]{1,0:T(8,128)(2,1)S(1)}, bf16[32,2048]{1,0:T(8,128)(2,1)S(1)}, bf16[32,2048]{1,0:T(8,128)(2,1)S(1)}, bf16[8,16,8192]{2,1,0:T(8,128)(2,1)S(1)}) custom-call(s32[1]{0:T(128)} %bitcast.2.feat_ref.refs_0_, s32[1]{0:T(128)} %bitcast.1.core_ref.refs_0_, s32[32]{0:T(128)} %order_hbm.1, ...), custom_call_target="tpu_custom_call" | custom-call | flops 20000000000 | tf_op jit(solution)/shard_map/first_terms/pallas_call | solution.py:70
  4.5 3.0 %collective-permute-start.1 = (bf16[32,2048]{1,0:T(8,128)(2,1)S(1)}, bf16[32,2048]{1,0:T(8,128)(2,1)S(1)}, u32[]{:S(2)}, u32[]{:S(2)}) collective-permute-start(bf16[32,2048]{1,0:T(8,128)(2,1)S(1)} %get-tuple-element.23), channel_id=1, source_target_pairs={{0,8},{1,17},{2,10},{3,19},{4,12},{5,21},{6,14},{7,23},{8,0},{9,25... | collective-permute-start | bytes 393224 | tf_op jit(solution)/shard_map/ppermute | solution.py:468
  7.5 1.5 %collective-permute-start.2 = (bf16[32,2048]{1,0:T(8,128)(2,1)S(1)}, bf16[32,2048]{1,0:T(8,128)(2,1)S(1)}, u32[]{:S(2)}, u32[]{:S(2)}) collective-permute-start(bf16[32,2048]{1,0:T(8,128)(2,1)S(1)} %get-tuple-element.24), channel_id=1, source_target_pairs={{0,16},{1,9},{2,18},{3,11},{4,20},{5,13},{6,22},{7,15},{8,24},{9,1... | collective-permute-start | bytes 393224 | tf_op jit(solution)/shard_map/ppermute | solution.py:468
  9.1 0.0 collective-permute-start.3
  9.1 0.0 copy-done
  9.1 1.6 %terms.2 = (bf16[2,48,2048]{2,1,0:T(8,128)(2,1)S(1)}, bf16[2,48,2048]{2,1,0:T(8,128)(2,1)S(1)}) custom-call(s32[1]{0:T(128)} %bitcast.1.core_ref.refs_0_, bf16[8,16,8192]{2,1,0:T(8,128)(2,1)S(1)} %get-tuple-element.19.spread.refs_1_, bf16[128,65536]{1,0:T(8,128)(2,1)S(1)} %copy-done), custom_call_target="tpu_custom_call" | custom-call | flops 10000000000 | tf_op jit(solution)/shard_map/terms/pallas_call | solution.py:70
  10.7 2.0 %collective-permute-start = (bf16[2,48,2048]{2,1,0:T(8,128)(2,1)S(1)}, bf16[2,48,2048]{2,1,0:T(8,128)(2,1)S(1)}, u32[]{:S(2)}, u32[]{:S(2)}) collective-permute-start(bf16[2,48,2048]{2,1,0:T(8,128)(2,1)S(1)} %get-tuple-element.21.refs_3_), channel_id=1, source_target_pairs={{0,8},{1,17},{2,10},{3,19},{4,12},{5,21},{6,14},{7,23},{8,0},{9,25... | collective-permute-start | bytes 1179656 | tf_op jit(solution)/shard_map/ppermute | solution.py:468
  12.7 2.5 %terms.3 = (bf16[2,80,2048]{2,1,0:T(8,128)(2,1)S(1)}, bf16[2,80,2048]{2,1,0:T(8,128)(2,1)S(1)}) custom-call(s32[1]{0:T(128)} %bitcast.1.core_ref.refs_0_, bf16[8,16,8192]{2,1,0:T(8,128)(2,1)S(1)} %get-tuple-element.19.spread.refs_1_, bf16[128,65536]{1,0:T(8,128)(2,1)S(1)} %copy-done, bf16[2,48,2048]{2,1,0:T(8,128)(2,1)S(1)} %get-tuple-element.21.refs_3_), custom_call_target="tpu_custom_call" | custom-call | flops 10000000000 | tf_op jit(solution)/shard_map/terms/pallas_call | solution.py:70
  15.2 1.6 %collective-permute-start.5 = (bf16[2,80,2048]{2,1,0:T(8,128)(2,1)S(1)}, bf16[2,80,2048]{2,1,0:T(8,128)(2,1)S(1)}, u32[]{:S(2)}, u32[]{:S(2)}) collective-permute-start(bf16[2,80,2048]{2,1,0:T(8,128)(2,1)S(1)} %get-tuple-element.26.refs_4_), channel_id=1, source_target_pairs={{0,16},{1,9},{2,18},{3,11},{4,20},{5,13},{6,22},{7,15},{8,24},{9,1... | collective-permute-start | bytes 1966088 | tf_op jit(solution)/shard_map/ppermute | solution.py:468
  16.8 0.0 collective-permute-done.1.refs_1_
  16.8 0.0 collective-permute-done.2.refs_2_
  16.8 0.0 collective-permute-done.3.refs_3_
  16.8 0.1 combine.1.refs_2_.refs_1_
  16.9 3.7 %collective-permute-start.9 = (bf16[32,2048]{1,0:T(8,128)(2,1)S(1)}, bf16[32,2048]{1,0:T(8,128)(2,1)S(1)}, u32[]{:S(2)}, u32[]{:S(2)}) collective-permute-start(bf16[32,2048]{1,0:T(8,128)(2,1)S(1)} %combine.1.refs_2_.refs_1_), channel_id=1, source_target_pairs={{0,6},{1,7},{2,4},{3,5},{4,2},{5,3},{6,0},{7,1},{8,14},{9,15},{10,... | collective-permute-start | bytes 393224 | tf_op jit(solution)/shard_map/ppermute | solution.py:436
  20.5 0.0 collective-permute-start.8
  20.5 0.8 %collective-permute-start.7 = (bf16[32,2048]{1,0:T(8,128)(2,1)S(1)}, bf16[32,2048]{1,0:T(8,128)(2,1)S(1)}, u32[]{:S(2)}, u32[]{:S(2)}) collective-permute-start(bf16[32,2048]{1,0:T(8,128)(2,1)S(1)} %combine.1.refs_2_.refs_1_), channel_id=1, source_target_pairs={{0,2},{1,3},{2,0},{3,1},{4,6},{5,7},{6,4},{7,5},{8,10},{9,11},{10,... | collective-permute-start | bytes 393224 | tf_op jit(solution)/shard_map/ppermute | solution.py:436
  21.3 0.0 collective-permute-done.refs_1_
  21.4 2.4 %collective-permute-start.4 = (bf16[1,48,2048]{2,1,0:T(8,128)(2,1)S(1)}, bf16[1,48,2048]{2,1,0:T(8,128)(2,1)S(1)}, u32[]{:S(2)}, u32[]{:S(2)}) collective-permute-start(bf16[1,48,2048]{2,1,0:T(8,128)(2,1)S(1)} %middle.2.refs_2_), channel_id=1, source_target_pairs={{0,16},{1,9},{2,18},{3,11},{4,20},{5,13},{6,22},{7,15},{8,24},{9,1... | collective-permute-start | bytes 589832 | tf_op jit(solution)/shard_map/ppermute | solution.py:468
  23.8 2.8 %collective-permute-done.5.refs_1_.refs_4_ = bf16[2,80,2048]{2,1,0:T(8,128)(2,1)S(1)} collective-permute-done((bf16[2,80,2048]{2,1,0:T(8,128)(2,1)S(1)}, bf16[2,80,2048]{2,1,0:T(8,128)(2,1)S(1)}, u32[]{:S(2)}, u32[]{:S(2)}) %collective-permute-start.5) | collective-permute-done | bytes 655392 | tf_op jit(solution)/shard_map/ppermute | solution.py:468
  26.6 0.1 middle.3.refs_5_
  26.6 1.5 %collective-permute-start.6 = (bf16[1,80,2048]{2,1,0:T(8,128)(2,1)S(1)}, bf16[1,80,2048]{2,1,0:T(8,128)(2,1)S(1)}, u32[]{:S(2)}, u32[]{:S(2)}) collective-permute-start(bf16[1,80,2048]{2,1,0:T(8,128)(2,1)S(1)} %middle.3.refs_5_), channel_id=1, source_target_pairs={{0,8},{1,17},{2,10},{3,19},{4,12},{5,21},{6,14},{7,23},{8,0},{9,25... | collective-permute-start | bytes 983048 | tf_op jit(solution)/shard_map/ppermute | solution.py:468
  28.1 0.0 collective-permute-done.9.refs_4_
  28.1 2.6 %collective-permute-done.8.refs_3_ = bf16[32,2048]{1,0:T(8,128)(2,1)S(1)} collective-permute-done((bf16[32,2048]{1,0:T(8,128)(2,1)S(1)}, bf16[32,2048]{1,0:T(8,128)(2,1)S(1)}, u32[]{:S(2)}, u32[]{:S(2)}) %collective-permute-start.8) | collective-permute-done | bytes 131104 | tf_op jit(solution)/shard_map/ppermute | solution.py:436
  30.7 0.0 collective-permute-done.7.refs_2_
  30.7 0.3 stack_targets.1.mine_ref
  31.0 0.1 collective-permute-start.10
  31.1 0.0 collective-permute-done.4.refs_2_
  31.1 2.7 %collective-permute-done.6.refs_5_ = bf16[1,80,2048]{2,1,0:T(8,128)(2,1)S(1)} collective-permute-done((bf16[1,80,2048]{2,1,0:T(8,128)(2,1)S(1)}, bf16[1,80,2048]{2,1,0:T(8,128)(2,1)S(1)}, u32[]{:S(2)}, u32[]{:S(2)}) %collective-permute-start.6) | collective-permute-done | bytes 327712 | tf_op jit(solution)/shard_map/ppermute | solution.py:468
  33.8 0.4 join.1
  34.2 0.0 collective-permute-done.10.other_ref
  34.2 0.0 copy-start.1
  34.2 0.5 %gram.1 = (f32[72,128]{1,0:T(8,128)S(1)}, f32[72,128]{1,0:T(8,128)S(1)}, f32[72,128]{1,0:T(8,128)S(1)}, f32[72,128]{1,0:T(8,128)S(1)}) custom-call(s32[1]{0:T(128)} %bitcast.2.feat_ref.refs_0_, bf16[128,2048]{1,0:T(8,128)(2,1)S(1)} %get-tuple-element.28.t1_ref, f32[8,128]{1,0:T(8,128)S(1)} %get-tuple-element.29.norms_ref, ...), custom_call_target="tpu_custom_call" | custom-call | flops 10000000000 | tf_op jit(solution)/shard_map/gram/pallas_call | solution.py:70
  34.7 2.4 %collective-permute-start.11 = (f32[72,128]{1,0:T(8,128)S(1)}, f32[72,128]{1,0:T(8,128)S(1)}, u32[]{:S(2)}, u32[]{:S(2)}) collective-permute-start(f32[72,128]{1,0:T(8,128)S(1)} %get-tuple-element.31), channel_id=1, source_target_pairs={{0,24},{8,16},{16,8},{24,0},{1,25},{9,17},{17,9},{25,1},{2,26},{10... | collective-permute-start | bytes 110600 | tf_op jit(solution)/shard_map/ppermute | solution.py:436
  37.1 0.7 %collective-permute-start.12 = (f32[72,128]{1,0:T(8,128)S(1)}, f32[72,128]{1,0:T(8,128)S(1)}, u32[]{:S(2)}, u32[]{:S(2)}) collective-permute-start(f32[72,128]{1,0:T(8,128)S(1)} %get-tuple-element.32), channel_id=1, source_target_pairs={{0,8},{8,0},{16,24},{24,16},{1,9},{9,1},{17,25},{25,17},{2,10},{10... | collective-permute-start | bytes 110600 | tf_op jit(solution)/shard_map/ppermute | solution.py:436
  37.8 0.5 %collective-permute-start.13 = (f32[72,128]{1,0:T(8,128)S(1)}, f32[72,128]{1,0:T(8,128)S(1)}, u32[]{:S(2)}, u32[]{:S(2)}) collective-permute-start(f32[72,128]{1,0:T(8,128)S(1)} %get-tuple-element.33), channel_id=1, source_target_pairs={{0,16},{8,24},{16,0},{24,8},{1,17},{9,25},{17,1},{25,9},{2,18},{10... | collective-permute-start | bytes 110600 | tf_op jit(solution)/shard_map/ppermute | solution.py:436
  38.3 0.0 copy-done.1
  38.3 0.4 inner_transform.1.projected_ref
  38.7 1.0 %collective-permute-done.11.refs_1_ = f32[72,128]{1,0:T(8,128)S(1)} collective-permute-done((f32[72,128]{1,0:T(8,128)S(1)}, f32[72,128]{1,0:T(8,128)S(1)}, u32[]{:S(2)}, u32[]{:S(2)}) %collective-permute-start.11) | collective-permute-done | bytes 36896 | tf_op jit(solution)/shard_map/ppermute | solution.py:436
  39.6 1.4 %collective-permute-done.12.refs_2_ = f32[72,128]{1,0:T(8,128)S(1)} collective-permute-done((f32[72,128]{1,0:T(8,128)S(1)}, f32[72,128]{1,0:T(8,128)S(1)}, u32[]{:S(2)}, u32[]{:S(2)}) %collective-permute-start.12) | collective-permute-done | bytes 36896 | tf_op jit(solution)/shard_map/ppermute | solution.py:436
  41.0 0.7 %collective-permute-done.13.refs_3_ = f32[72,128]{1,0:T(8,128)S(1)} collective-permute-done((f32[72,128]{1,0:T(8,128)S(1)}, f32[72,128]{1,0:T(8,128)S(1)}, u32[]{:S(2)}, u32[]{:S(2)}) %collective-permute-start.13) | collective-permute-done | bytes 36896 | tf_op jit(solution)/shard_map/ppermute | solution.py:436
  41.7 1.0 %finish.1 = (bf16[128,2048]{1,0:T(8,128)(2,1)}, f32[64,128]{1,0:T(8,128)}) custom-call(s32[1]{0:T(128)} %bitcast.ex_ref, bf16[128,2048]{1,0:T(8,128)(2,1)S(1)} %inner_transform.1.projected_ref, f32[72,128]{1,0:T(8,128)S(1)} %get-tuple-element.30.refs_0_, f32[72,128]{1,0:T(8,128)S(1)} %collective-permute-done.11.refs_1_, ...), custom_call_target="tpu_custom_call" | custom-call | flops 10000000000 | tf_op jit(solution)/shard_map/finish/pallas_call | solution.py:70
  (1 shorter events, 0.0 us)
Async XLA Ops:
  0.6 8.4 %copy-start = (bf16[128,65536]{1,0:T(8,128)(2,1)S(1)}, bf16[128,65536]{1,0:T(8,128)(2,1)}, u32[]{:S(2)}) copy-start(bf16[128,65536]{1,0:T(8,128)(2,1)} %refs_2_.1) | copy-start | bytes 50331652
  4.5 12.2 %collective-permute-start.1 = (bf16[32,2048]{1,0:T(8,128)(2,1)S(1)}, bf16[32,2048]{1,0:T(8,128)(2,1)S(1)}, u32[]{:S(2)}, u32[]{:S(2)}) collective-permute-start(bf16[32,2048]{1,0:T(8,128)(2,1)S(1)} %get-tuple-element.23), channel_id=1, source_target_pairs={{0,8},{1,17},{2,10},{3,19},{4,12},{5,21},{6,14},{7,23},{8,0},{9,25... | collective-permute-start | bytes 393224 | tf_op jit(solution)/shard_map/ppermute | solution.py:468
  7.5 9.2 %collective-permute-start.2 = (bf16[32,2048]{1,0:T(8,128)(2,1)S(1)}, bf16[32,2048]{1,0:T(8,128)(2,1)S(1)}, u32[]{:S(2)}, u32[]{:S(2)}) collective-permute-start(bf16[32,2048]{1,0:T(8,128)(2,1)S(1)} %get-tuple-element.24), channel_id=1, source_target_pairs={{0,16},{1,9},{2,18},{3,11},{4,20},{5,13},{6,22},{7,15},{8,24},{9,1... | collective-permute-start | bytes 393224 | tf_op jit(solution)/shard_map/ppermute | solution.py:468
  9.1 7.7 %collective-permute-start.3 = (bf16[32,2048]{1,0:T(8,128)(2,1)S(1)}, bf16[32,2048]{1,0:T(8,128)(2,1)S(1)}, u32[]{:S(2)}, u32[]{:S(2)}) collective-permute-start(bf16[32,2048]{1,0:T(8,128)(2,1)S(1)} %get-tuple-element.25), channel_id=1, source_target_pairs={{0,24},{1,25},{2,26},{3,27},{4,28},{5,29},{6,30},{7,31},{8,16},{9,... | collective-permute-start | bytes 393224 | tf_op jit(solution)/shard_map/ppermute | solution.py:468
  10.7 10.6 %collective-permute-start = (bf16[2,48,2048]{2,1,0:T(8,128)(2,1)S(1)}, bf16[2,48,2048]{2,1,0:T(8,128)(2,1)S(1)}, u32[]{:S(2)}, u32[]{:S(2)}) collective-permute-start(bf16[2,48,2048]{2,1,0:T(8,128)(2,1)S(1)} %get-tuple-element.21.refs_3_), channel_id=1, source_target_pairs={{0,8},{1,17},{2,10},{3,19},{4,12},{5,21},{6,14},{7,23},{8,0},{9,25... | collective-permute-start | bytes 1179656 | tf_op jit(solution)/shard_map/ppermute | solution.py:468
  15.2 11.4 %collective-permute-start.5 = (bf16[2,80,2048]{2,1,0:T(8,128)(2,1)S(1)}, bf16[2,80,2048]{2,1,0:T(8,128)(2,1)S(1)}, u32[]{:S(2)}, u32[]{:S(2)}) collective-permute-start(bf16[2,80,2048]{2,1,0:T(8,128)(2,1)S(1)} %get-tuple-element.26.refs_4_), channel_id=1, source_target_pairs={{0,16},{1,9},{2,18},{3,11},{4,20},{5,13},{6,22},{7,15},{8,24},{9,1... | collective-permute-start | bytes 1966088 | tf_op jit(solution)/shard_map/ppermute | solution.py:468
  16.9 11.3 %collective-permute-start.9 = (bf16[32,2048]{1,0:T(8,128)(2,1)S(1)}, bf16[32,2048]{1,0:T(8,128)(2,1)S(1)}, u32[]{:S(2)}, u32[]{:S(2)}) collective-permute-start(bf16[32,2048]{1,0:T(8,128)(2,1)S(1)} %combine.1.refs_2_.refs_1_), channel_id=1, source_target_pairs={{0,6},{1,7},{2,4},{3,5},{4,2},{5,3},{6,0},{7,1},{8,14},{9,15},{10,... | collective-permute-start | bytes 393224 | tf_op jit(solution)/shard_map/ppermute | solution.py:436
  20.5 10.2 %collective-permute-start.8 = (bf16[32,2048]{1,0:T(8,128)(2,1)S(1)}, bf16[32,2048]{1,0:T(8,128)(2,1)S(1)}, u32[]{:S(2)}, u32[]{:S(2)}) collective-permute-start(bf16[32,2048]{1,0:T(8,128)(2,1)S(1)} %combine.1.refs_2_.refs_1_), channel_id=1, source_target_pairs={{0,4},{1,5},{2,6},{3,7},{4,0},{5,1},{6,2},{7,3},{8,12},{9,13},{10,... | collective-permute-start | bytes 393224 | tf_op jit(solution)/shard_map/ppermute | solution.py:436
  20.5 10.2 %collective-permute-start.7 = (bf16[32,2048]{1,0:T(8,128)(2,1)S(1)}, bf16[32,2048]{1,0:T(8,128)(2,1)S(1)}, u32[]{:S(2)}, u32[]{:S(2)}) collective-permute-start(bf16[32,2048]{1,0:T(8,128)(2,1)S(1)} %combine.1.refs_2_.refs_1_), channel_id=1, source_target_pairs={{0,2},{1,3},{2,0},{3,1},{4,6},{5,7},{6,4},{7,5},{8,10},{9,11},{10,... | collective-permute-start | bytes 393224 | tf_op jit(solution)/shard_map/ppermute | solution.py:436
  21.4 9.7 %collective-permute-start.4 = (bf16[1,48,2048]{2,1,0:T(8,128)(2,1)S(1)}, bf16[1,48,2048]{2,1,0:T(8,128)(2,1)S(1)}, u32[]{:S(2)}, u32[]{:S(2)}) collective-permute-start(bf16[1,48,2048]{2,1,0:T(8,128)(2,1)S(1)} %middle.2.refs_2_), channel_id=1, source_target_pairs={{0,16},{1,9},{2,18},{3,11},{4,20},{5,13},{6,22},{7,15},{8,24},{9,1... | collective-permute-start | bytes 589832 | tf_op jit(solution)/shard_map/ppermute | solution.py:468
  26.6 7.1 %collective-permute-start.6 = (bf16[1,80,2048]{2,1,0:T(8,128)(2,1)S(1)}, bf16[1,80,2048]{2,1,0:T(8,128)(2,1)S(1)}, u32[]{:S(2)}, u32[]{:S(2)}) collective-permute-start(bf16[1,80,2048]{2,1,0:T(8,128)(2,1)S(1)} %middle.3.refs_5_), channel_id=1, source_target_pairs={{0,8},{1,17},{2,10},{3,19},{4,12},{5,21},{6,14},{7,23},{8,0},{9,25... | collective-permute-start | bytes 983048 | tf_op jit(solution)/shard_map/ppermute | solution.py:468
  31.0 3.2 %collective-permute-start.10 = (bf16[144,2048]{1,0:T(8,128)(2,1)S(1)}, bf16[144,2048]{1,0:T(8,128)(2,1)S(1)}, u32[]{:S(2)}, u32[]{:S(2)}) collective-permute-start(bf16[144,2048]{1,0:T(8,128)(2,1)S(1)} %stack_targets.1.mine_ref), channel_id=1, source_target_pairs={{0,1},{1,0},{2,3},{3,2},{4,5},{5,4},{6,7},{7,6},{8,9},{9,8},{10,11... | collective-permute-start | bytes 1769480 | tf_op jit(solution)/shard_map/ppermute | solution.py:436
  34.2 4.0 %copy-start.1 = (bf16[256,256]{1,0:T(8,128)(2,1)S(1)}, bf16[256,256]{1,0:T(8,128)(2,1)}, u32[]{:S(2)}) copy-start(bf16[256,256]{1,0:T(8,128)(2,1)} %constant.23.clone.table_ref) | copy-start | bytes 393220
  34.7 4.9 %collective-permute-start.11 = (f32[72,128]{1,0:T(8,128)S(1)}, f32[72,128]{1,0:T(8,128)S(1)}, u32[]{:S(2)}, u32[]{:S(2)}) collective-permute-start(f32[72,128]{1,0:T(8,128)S(1)} %get-tuple-element.31), channel_id=1, source_target_pairs={{0,24},{8,16},{16,8},{24,0},{1,25},{9,17},{17,9},{25,1},{2,26},{10... | collective-permute-start | bytes 110600 | tf_op jit(solution)/shard_map/ppermute | solution.py:436
  37.1 4.0 %collective-permute-start.12 = (f32[72,128]{1,0:T(8,128)S(1)}, f32[72,128]{1,0:T(8,128)S(1)}, u32[]{:S(2)}, u32[]{:S(2)}) collective-permute-start(f32[72,128]{1,0:T(8,128)S(1)} %get-tuple-element.32), channel_id=1, source_target_pairs={{0,8},{8,0},{16,24},{24,16},{1,9},{9,1},{17,25},{25,17},{2,10},{10... | collective-permute-start | bytes 110600 | tf_op jit(solution)/shard_map/ppermute | solution.py:436
  37.8 4.0 %collective-permute-start.13 = (f32[72,128]{1,0:T(8,128)S(1)}, f32[72,128]{1,0:T(8,128)S(1)}, u32[]{:S(2)}, u32[]{:S(2)}) collective-permute-start(f32[72,128]{1,0:T(8,128)S(1)} %get-tuple-element.33), channel_id=1, source_target_pairs={{0,16},{8,24},{16,0},{24,8},{1,17},{9,25},{17,1},{25,9},{2,18},{10... | collective-permute-start | bytes 110600 | tf_op jit(solution)/shard_map/ppermute | solution.py:436

commit v2 on v1

--- a/solution.py
+++ b/solution.py
@@ -129,8 +129,9 @@
                 store(d, pl.ds(i * ROWS, ROWS), pl.ds(start, lanes), narrow(value))
 
 
-def first_kernel(feat_count, feat_ref, core_ref, order_hbm, signs_hbm, gradients_ref, *refs):
-    outs, (spread, held, sems, order, signs, mine, place, few) = refs[:feat_count], refs[feat_count:]
+def first_kernel(places, feat_ref, core_ref, order_hbm, signs_hbm, gradients_ref, *refs):
+    outs, (spread, held, sems, order, signs, mine, place, few) = refs[:2], refs[2:]
+    feat_count = len(places)
     order_copy = pltpu.make_async_copy(order_hbm, order, few.at[0])
     order_copy.start()
     copies = fetch(0, gradients_ref, held, sems)
@@ -159,7 +160,8 @@
         return narrow(jnp.broadcast_to(mine[pl.ds(p, 1), span], (ROWS, span.size)))
 
     def store(d, rows, lanes, value):
-        outs[d][rows, lanes] = value
+        half, number = places[d]
+        outs[half][number, rows, lanes] = value
 
     for tile in copies:
         for copy in tile:
@@ -168,14 +170,15 @@
     outer_terms(feat_count, core_ref[0], spread, tiles, store, make_sign)
 
 
-def first_terms(feat_count, feat, core, block_order, signs, gradients):
+def first_terms(bits, feat, core, block_order, signs, gradients):
+    feat_count = 1 << len(bits)
     rows, columns = gradients.shape
     total, width = signs.shape
     blocks = columns // width
-    part = jax.ShapeDtypeStruct((rows, width // feat_count), jnp.bfloat16)
-    *parts, table = call(
-        functools.partial(first_kernel, feat_count),
-        [part] * feat_count + [jax.ShapeDtypeStruct((blocks, ROWS, width), jnp.bfloat16)],
+    part = jax.ShapeDtypeStruct((feat_count // 2, rows, width // feat_count), jnp.bfloat16)
+    return call(
+        functools.partial(first_kernel, halving_places(bits)),
+        [part, part] + [jax.ShapeDtypeStruct((blocks, ROWS, width), jnp.bfloat16)],
         [feat, core, block_order, signs, gradients],
         [SMEM, SMEM, HBM, HBM, HBM],
         "first_terms",
@@ -191,7 +194,6 @@
             pltpu.SemaphoreType.DMA((1 + blocks,)),
         ],
     )
-    return parts, table
 
 
 def halving_places(bits):
@@ -249,13 +251,13 @@
 
 
 def combine_kernel(*refs):
-    refs[-1][...] = narrow(add_parts(refs[:-1], 0, refs[-1].shape[0]))
+    refs[-1][...] = narrow(add_parts(refs[:-1], 0, 1)[0])
 
 
 def combine(parts, after):
     return call(
         combine_kernel,
-        jax.ShapeDtypeStruct(parts[0].shape, jnp.bfloat16),
+        jax.ShapeDtypeStruct(parts[0].shape[1:], jnp.bfloat16),
         parts,
         [VMEM] * len(parts),
         "combine",
@@ -295,12 +297,7 @@
     d, left = place // share, place % share
     wanted = (left // per) * rows + (d ^ feat) * per + left % per
     norms = jnp.sum(jnp.where(source == wanted, jnp.concatenate(columns, axis=0), 0.0), axis=0, keepdims=True)
-    pieces = []
-    for unused in range(3):
-        piece = narrow(norms)
-        norms = norms - wide(piece)
-        pieces.append(wide(piece))
-    pieces = jnp.concatenate([*pieces, jnp.zeros((ROWS - 3, count), jnp.float32)], axis=0)
+    pieces = jnp.concatenate([*pieces_of(norms), jnp.zeros((ROWS - 3, count), jnp.float32)], axis=0)
     out_ref[pl.ds(count, ROWS), pl.ds(0, count)] = narrow(pieces)
     if inner > count:
         out_ref[pl.ds(count, ROWS), pl.ds(count, inner - count)] = jnp.zeros((ROWS, inner - count), jnp.bfloat16)
@@ -316,6 +313,15 @@
         "stack_targets",
         after=after,
     )
+
+
+def pieces_of(row):
+    pieces = []
+    for unused in range(3):
+        piece = wide(narrow(row))
+        row = row - piece
+        pieces.append(piece)
+    return pieces
 
 
 def square_sums(value):
@@ -365,14 +371,19 @@
         pieces = wide(ref[pl.ds(height, ROWS), pl.ds(0, height)])
         target_norms.append(pieces[0:1] + pieces[1:2] + pieces[2:3])
     for d, out in enumerate(outs):
+        blocks = []
         for i in range(0, 2 * share, per):
             first = pl.multiple_of((i * len(outs)) + (d ^ feat) * per, per)
-            out[pl.ds(i, per), :] = products[pl.ds(first, per), :]
+            blocks.append(products[pl.ds(first, per), :])
         span = slice(d * share, (d + 1) * share)
         here = jnp.concatenate(
             [x[:, span] for x in target_norms] + [jnp.zeros((1, rows - 2 * share), jnp.float32)], axis=1
         )
-        out[pl.ds(2 * share, 8), :] = jnp.concatenate([norms_ref[0:1, :], here, jnp.zeros((6, rows), jnp.float32)], axis=0)
+        sums = [norms_ref[0:1, :], here]
+        if d > 0:
+            sums = [piece for row in sums for piece in pieces_of(row)]
+        sums.append(jnp.zeros((out.shape[0] - 2 * share - len(sums), rows), jnp.float32))
+        out[...] = jnp.concatenate([*blocks, *sums], axis=0).astype(out.dtype)
 
 
 def gram(feat_count, per, feat, t1, norms, mine, other):
@@ -380,7 +391,8 @@
     rows = t1.shape[0]
     return call(
         functools.partial(gram_kernel, per),
-        [jax.ShapeDtypeStruct((total // feat_count + 8, rows), jnp.float32)] * feat_count,
+        [jax.ShapeDtypeStruct((total // feat_count + 8, rows), jnp.float32)]
+        + [jax.ShapeDtypeStruct((total // feat_count + ROWS, rows), jnp.bfloat16)] * (feat_count - 1),
         [feat, t1, norms, mine, other],
         [SMEM] + [VMEM] * 4,
         "gram",
@@ -408,11 +420,16 @@
     count = cosines_ref.shape[0]
     share = count // 2
     sums = parts[0][...]
+    products, train_sums, target_sums = sums[:count], sums[count : count + 1], sums[count + 1 : count + 2]
     for part in parts[1:]:
-        sums = sums + part[...]
-    train_scale = lax.rsqrt(sums[count : count + 1] * mean_scale + EPS)
-    target_scale = lax.rsqrt(sums[count + 1 : count + 2, :count] * mean_scale + EPS)
-    cosines = sums[:count] * train_scale * as_column(target_scale) * mean_scale
+        got = wide(part[...])
+        products = products + got[:count]
+        for i in range(count, count + 3):
+            train_sums = train_sums + got[i : i + 1]
+            target_sums = target_sums + got[i + 3 : i + 4]
+    train_scale = lax.rsqrt(train_sums * mean_scale + EPS)
+    target_scale = lax.rsqrt(target_sums[:, :count] * mean_scale + EPS)
+    cosines = products * train_scale * as_column(target_scale) * mean_scale
     for i in range(count // per):
         group = ex_ref[0] ^ (i * 2 if i * per < share else i * 2 - count // per + 1)
         cosines_ref[pl.ds(pl.multiple_of(group * per, per), per), :] = cosines[i * per : (i + 1) * per]
@@ -467,9 +484,8 @@
         ]
         return lax.ppermute(value, ("feat", "ex"), pairs)
 
-    target_parts, table = first_terms(feat_count, feat, core, block_order, signs, target_grads)
-    own = pltpu.with_memory_space_constraint(target_parts[0], pltpu.VMEM)
-    got = [own] + [turn(target_parts[d], d) for d in range(1, feat_count)]
+    keep, send, table = first_terms(bits, feat, core, block_order, signs, target_grads)
+    got = [pltpu.with_memory_space_constraint(keep, pltpu.VMEM), turn(send, 1 << bits[0])]
 
     orders = [bits if i % 2 == 0 else bits[::-1] for i in range(len(CHUNKS))]
     firsts = [sum(CHUNKS[:i]) for i in range(len(CHUNKS))]
@@ -487,6 +503,7 @@
 
     state = [None] * len(CHUNKS)
     state[0], mark = start(0, None)
+    got, mark = proceed(bits, got, mark)
     state[1], mark = start(1, mark)
     own = combine(got, mark)
     around = [own] + [swap(own, "ex", d) for d in range(2, groups, 2)]

time: 42.8 us -> 42.3 us (0.988)
  starting transfers between devices: 20.1 us -> 19.5 us
    ppermute x7 -> x6, starting transfers between devices: 12 us -> 11.3 us  [turn(): return lax.ppermute(value, ('feat', 'ex'), pairs)]
    ppermute x7 -> x6, waiting for transfers between devices: 5.52 us -> 5.21 us  [turn(): return lax.ppermute(value, ('feat', 'ex'), pairs)]
    pallas_call x11 -> x12, Pallas kernels: 10.7 us -> 10.7 us  [call(): pl.pallas_call(body, out_shape=out_shape, in_specs=specs, out_specs=jax.t...]
  transfers between devices with their start and end apart: 14 -> 13, of which waited for: 6 -> 8; matrix products, arithmetic and copies ran while one was open for 0% -> 0% of each run, Pallas kernels for 13% -> 13%
where the time goes in v2:
time: 42.3 us; the launch traced here: 42.1 us
  starting transfers between devices  19.5 us (46%)
  waiting for transfers between devices  10.9 us (26%)
  Pallas kernels  10.7 us (25%)
  between operations  0.74 us (2%)
    ppermute x6, starting transfers between devices, turn(): return lax.ppermute(value, ('feat', 'ex'), pairs)  11.3 us
    pallas_call x12, Pallas kernels, call(): pl.pallas_call(body, out_shape=out_shape, in_specs=specs, out_specs=jax.t...  10.7 us
    ppermute x7, starting transfers between devices, swap(): lax.ppermute(value, axis, [(i, i ^ distance) for i in range(lax.axis_size...  8.14 us
    ppermute x7, waiting for transfers between devices, swap(): lax.ppermute(value, axis, [(i, i ^ distance) for i in range(lax.axis_size...  5.68 us
    ppermute x6, waiting for transfers between devices, turn(): return lax.ppermute(value, ('feat', 'ex'), pairs)  5.21 us
  transfers between devices with their start and end apart: 13, of which 8 were waited for; matrix products, arithmetic and copies ran while one was open for 0% of the time, Pallas kernels for 13%

profile of v2, /device:TPU:0, one launch (start us, length us, event | category | flops | bytes accessed | tf_op | source)
XLA Modules:
  0.0 42.1 jit_solution(1640917393969682777)
XLA Ops:
  0.6 0.0 copy-start
  0.7 3.7 %first_terms.1 = (bf16[2,32,2048]{2,1,0:T(8,128)(2,1)S(1)}, bf16[2,32,2048]{2,1,0:T(8,128)(2,1)S(1)}, bf16[8,16,8192]{2,1,0:T(8,128)(2,1)S(1)}) custom-call(s32[1]{0:T(128)} %bitcast.2.feat_ref.refs_0_, s32[1]{0:T(128)} %bitcast.1.core_ref.refs_0_, s32[32]{0:T(128)} %order_hbm.1, s32[32,8192]{1,0:T(8,128)} %signs_hbm.1, bf16[32,65536]{1,0:T(8,128)(2,1)} %gradients_ref.2), custom_call_target="tpu_custom_call" | custom-call | flops 20000000000 | tf_op jit(solution)/shard_map/first_terms/pallas_call | solution.py:70
  4.4 3.0 %collective-permute-start.1 = (bf16[2,32,2048]{2,1,0:T(8,128)(2,1)S(1)}, bf16[2,32,2048]{2,1,0:T(8,128)(2,1)S(1)}, u32[]{:S(2)}, u32[]{:S(2)}) collective-permute-start(bf16[2,32,2048]{2,1,0:T(8,128)(2,1)S(1)} %get-tuple-element.21), channel_id=1, source_target_pairs={{0,8},{1,17},{2,10},{3,19},{4,12},{5,21},{6,14},{7,23},{8,0},{9,25... | collective-permute-start | bytes 786440 | tf_op jit(solution)/shard_map/ppermute | solution.py:485
  7.4 0.4 copy-done
  7.7 1.6 %terms.2 = (bf16[2,48,2048]{2,1,0:T(8,128)(2,1)S(1)}, bf16[2,48,2048]{2,1,0:T(8,128)(2,1)S(1)}) custom-call(s32[1]{0:T(128)} %bitcast.1.core_ref.refs_0_, bf16[8,16,8192]{2,1,0:T(8,128)(2,1)S(1)} %get-tuple-element.17.spread.refs_1_, bf16[128,65536]{1,0:T(8,128)(2,1)S(1)} %copy-done), custom_call_target="tpu_custom_call" | custom-call | flops 10000000000 | tf_op jit(solution)/shard_map/terms/pallas_call | solution.py:70
  9.4 3.0 %collective-permute-start = (bf16[2,48,2048]{2,1,0:T(8,128)(2,1)S(1)}, bf16[2,48,2048]{2,1,0:T(8,128)(2,1)S(1)}, u32[]{:S(2)}, u32[]{:S(2)}) collective-permute-start(bf16[2,48,2048]{2,1,0:T(8,128)(2,1)S(1)} %get-tuple-element.19.refs_2_), channel_id=1, source_target_pairs={{0,8},{1,17},{2,10},{3,19},{4,12},{5,21},{6,14},{7,23},{8,0},{9,25... | collective-permute-start | bytes 1179656 | tf_op jit(solution)/shard_map/ppermute | solution.py:485
  12.4 0.0 collective-permute-done.1.refs_1_
  12.4 1.6 %collective-permute-start.2 = (bf16[1,32,2048]{2,1,0:T(8,128)(2,1)S(1)}, bf16[1,32,2048]{2,1,0:T(8,128)(2,1)S(1)}, u32[]{:S(2)}, u32[]{:S(2)}) collective-permute-start(bf16[1,32,2048]{2,1,0:T(8,128)(2,1)S(1)} %middle.3.refs_3_), channel_id=1, source_target_pairs={{0,16},{1,9},{2,18},{3,11},{4,20},{5,13},{6,22},{7,15},{8,24},{9,1... | collective-permute-start | bytes 393224 | tf_op jit(solution)/shard_map/ppermute | solution.py:485
  14.0 2.5 %terms.3 = (bf16[2,80,2048]{2,1,0:T(8,128)(2,1)S(1)}, bf16[2,80,2048]{2,1,0:T(8,128)(2,1)S(1)}) custom-call(s32[1]{0:T(128)} %bitcast.1.core_ref.refs_0_, bf16[8,16,8192]{2,1,0:T(8,128)(2,1)S(1)} %get-tuple-element.17.spread.refs_1_, bf16[128,65536]{1,0:T(8,128)(2,1)S(1)} %copy-done, bf16[1,32,2048]{2,1,0:T(8,128)(2,1)S(1)} %middle.3.refs_3_), custom_call_target="tpu_custom_call" | custom-call | flops 10000000000 | tf_op jit(solution)/shard_map/terms/pallas_call | solution.py:70
  16.5 0.6 %collective-permute-start.4 = (bf16[2,80,2048]{2,1,0:T(8,128)(2,1)S(1)}, bf16[2,80,2048]{2,1,0:T(8,128)(2,1)S(1)}, u32[]{:S(2)}, u32[]{:S(2)}) collective-permute-start(bf16[2,80,2048]{2,1,0:T(8,128)(2,1)S(1)} %get-tuple-element.22.refs_3_), channel_id=1, source_target_pairs={{0,16},{1,9},{2,18},{3,11},{4,20},{5,13},{6,22},{7,15},{8,24},{9,1... | collective-permute-start | bytes 1966088 | tf_op jit(solution)/shard_map/ppermute | solution.py:485
  17.1 1.6 %collective-permute-done.2.refs_2_ = bf16[1,32,2048]{2,1,0:T(8,128)(2,1)S(1)} collective-permute-done((bf16[1,32,2048]{2,1,0:T(8,128)(2,1)S(1)}, bf16[1,32,2048]{2,1,0:T(8,128)(2,1)S(1)}, u32[]{:S(2)}, u32[]{:S(2)}) %collective-permute-start.2) | collective-permute-done | bytes 131104 | tf_op jit(solution)/shard_map/ppermute | solution.py:485
  18.7 0.1 combine.1.refs_2_.refs_1_
  18.7 3.9 %collective-permute-start.8 = (bf16[32,2048]{1,0:T(8,128)(2,1)S(1)}, bf16[32,2048]{1,0:T(8,128)(2,1)S(1)}, u32[]{:S(2)}, u32[]{:S(2)}) collective-permute-start(bf16[32,2048]{1,0:T(8,128)(2,1)S(1)} %combine.1.refs_2_.refs_1_), channel_id=1, source_target_pairs={{0,6},{1,7},{2,4},{3,5},{4,2},{5,3},{6,0},{7,1},{8,14},{9,15},{10,... | collective-permute-start | bytes 393224 | tf_op jit(solution)/shard_map/ppermute | solution.py:453
  22.6 0.0 collective-permute-start.7
  22.6 0.6 %collective-permute-start.6 = (bf16[32,2048]{1,0:T(8,128)(2,1)S(1)}, bf16[32,2048]{1,0:T(8,128)(2,1)S(1)}, u32[]{:S(2)}, u32[]{:S(2)}) collective-permute-start(bf16[32,2048]{1,0:T(8,128)(2,1)S(1)} %combine.1.refs_2_.refs_1_), channel_id=1, source_target_pairs={{0,2},{1,3},{2,0},{3,1},{4,6},{5,7},{6,4},{7,5},{8,10},{9,11},{10,... | collective-permute-start | bytes 393224 | tf_op jit(solution)/shard_map/ppermute | solution.py:453
  23.3 0.0 collective-permute-done.refs_1_
  23.3 1.7 %collective-permute-start.3 = (bf16[1,48,2048]{2,1,0:T(8,128)(2,1)S(1)}, bf16[1,48,2048]{2,1,0:T(8,128)(2,1)S(1)}, u32[]{:S(2)}, u32[]{:S(2)}) collective-permute-start(bf16[1,48,2048]{2,1,0:T(8,128)(2,1)S(1)} %middle.4.refs_2_), channel_id=1, source_target_pairs={{0,16},{1,9},{2,18},{3,11},{4,20},{5,13},{6,22},{7,15},{8,24},{9,1... | collective-permute-start | bytes 589832 | tf_op jit(solution)/shard_map/ppermute | solution.py:485
  25.0 2.1 %collective-permute-done.4.refs_1_.refs_4_ = bf16[2,80,2048]{2,1,0:T(8,128)(2,1)S(1)} collective-permute-done((bf16[2,80,2048]{2,1,0:T(8,128)(2,1)S(1)}, bf16[2,80,2048]{2,1,0:T(8,128)(2,1)S(1)}, u32[]{:S(2)}, u32[]{:S(2)}) %collective-permute-start.4) | collective-permute-done | bytes 655392 | tf_op jit(solution)/shard_map/ppermute | solution.py:485
  27.2 0.1 middle.5.refs_5_
  27.3 1.5 %collective-permute-start.5 = (bf16[1,80,2048]{2,1,0:T(8,128)(2,1)S(1)}, bf16[1,80,2048]{2,1,0:T(8,128)(2,1)S(1)}, u32[]{:S(2)}, u32[]{:S(2)}) collective-permute-start(bf16[1,80,2048]{2,1,0:T(8,128)(2,1)S(1)} %middle.5.refs_5_), channel_id=1, source_target_pairs={{0,8},{1,17},{2,10},{3,19},{4,12},{5,21},{6,14},{7,23},{8,0},{9,25... | collective-permute-start | bytes 983048 | tf_op jit(solution)/shard_map/ppermute | solution.py:485
  28.7 0.0 collective-permute-done.8.refs_4_
  28.7 3.8 %collective-permute-done.7.refs_3_ = bf16[32,2048]{1,0:T(8,128)(2,1)S(1)} collective-permute-done((bf16[32,2048]{1,0:T(8,128)(2,1)S(1)}, bf16[32,2048]{1,0:T(8,128)(2,1)S(1)}, u32[]{:S(2)}, u32[]{:S(2)}) %collective-permute-start.7) | collective-permute-done | bytes 131104 | tf_op jit(solution)/shard_map/ppermute | solution.py:453
  32.5 0.0 collective-permute-done.6.refs_2_
  32.5 0.3 stack_targets.1.mine_ref
  32.8 0.1 collective-permute-start.9
  32.9 0.0 collective-permute-done.3.refs_2_
  32.9 1.5 %collective-permute-done.5.refs_5_ = bf16[1,80,2048]{2,1,0:T(8,128)(2,1)S(1)} collective-permute-done((bf16[1,80,2048]{2,1,0:T(8,128)(2,1)S(1)}, bf16[1,80,2048]{2,1,0:T(8,128)(2,1)S(1)}, u32[]{:S(2)}, u32[]{:S(2)}) %collective-permute-start.5) | collective-permute-done | bytes 327712 | tf_op jit(solution)/shard_map/ppermute | solution.py:485
  34.4 0.4 join.1
  34.8 0.1 collective-permute-done.9.other_ref
  34.9 0.0 copy-start.1
  34.9 0.5 %gram.1 = (f32[72,128]{1,0:T(8,128)S(1)}, bf16[80,128]{1,0:T(8,128)(2,1)S(1)}, bf16[80,128]{1,0:T(8,128)(2,1)S(1)}, bf16[80,128]{1,0:T(8,128)(2,1)S(1)}) custom-call(s32[1]{0:T(128)} %bitcast.2.feat_ref.refs_0_, bf16[128,2048]{1,0:T(8,128)(2,1)S(1)} %get-tuple-element.24.t1_ref, f32[8,128]{1,0:T(8,128)S(1)} %get-tuple-element.25.norms_ref, ...), custom_call_target="tpu_custom_call" | custom-call | flops 10000000000 | tf_op jit(solution)/shard_map/gram/pallas_call | solution.py:70
  35.4 1.4 %collective-permute-start.10 = (bf16[80,128]{1,0:T(8,128)(2,1)S(1)}, bf16[80,128]{1,0:T(8,128)(2,1)S(1)}, u32[]{:S(2)}, u32[]{:S(2)}) collective-permute-start(bf16[80,128]{1,0:T(8,128)(2,1)S(1)} %get-tuple-element.27), channel_id=1, source_target_pairs={{0,24},{8,16},{16,8},{24,0},{1,25},{9,17},{17,9},{25,1},{2,26},{10... | collective-permute-start | bytes 61448 | tf_op jit(solution)/shard_map/ppermute | solution.py:453
  36.8 0.6 %collective-permute-start.11 = (bf16[80,128]{1,0:T(8,128)(2,1)S(1)}, bf16[80,128]{1,0:T(8,128)(2,1)S(1)}, u32[]{:S(2)}, u32[]{:S(2)}) collective-permute-start(bf16[80,128]{1,0:T(8,128)(2,1)S(1)} %get-tuple-element.28), channel_id=1, source_target_pairs={{0,8},{8,0},{16,24},{24,16},{1,9},{9,1},{17,25},{25,17},{2,10},{10... | collective-permute-start | bytes 61448 | tf_op jit(solution)/shard_map/ppermute | solution.py:453
  37.4 1.6 %collective-permute-start.12 = (bf16[80,128]{1,0:T(8,128)(2,1)S(1)}, bf16[80,128]{1,0:T(8,128)(2,1)S(1)}, u32[]{:S(2)}, u32[]{:S(2)}) collective-permute-start(bf16[80,128]{1,0:T(8,128)(2,1)S(1)} %get-tuple-element.29), channel_id=1, source_target_pairs={{0,16},{8,24},{16,0},{24,8},{1,17},{9,25},{17,1},{25,9},{2,18},{10... | collective-permute-start | bytes 61448 | tf_op jit(solution)/shard_map/ppermute | solution.py:453
  38.9 0.0 copy-done.1
  38.9 0.4 inner_transform.1.projected_ref
  39.3 0.8 %collective-permute-done.10.refs_1_ = bf16[80,128]{1,0:T(8,128)(2,1)S(1)} collective-permute-done((bf16[80,128]{1,0:T(8,128)(2,1)S(1)}, bf16[80,128]{1,0:T(8,128)(2,1)S(1)}, u32[]{:S(2)}, u32[]{:S(2)}) %collective-permute-start.10) | collective-permute-done | bytes 20512 | tf_op jit(solution)/shard_map/ppermute | solution.py:453
  40.1 0.5 %collective-permute-done.11.refs_2_ = bf16[80,128]{1,0:T(8,128)(2,1)S(1)} collective-permute-done((bf16[80,128]{1,0:T(8,128)(2,1)S(1)}, bf16[80,128]{1,0:T(8,128)(2,1)S(1)}, u32[]{:S(2)}, u32[]{:S(2)}) %collective-permute-start.11) | collective-permute-done | bytes 20512 | tf_op jit(solution)/shard_map/ppermute | solution.py:453
  40.6 0.6 %collective-permute-done.12.refs_3_ = bf16[80,128]{1,0:T(8,128)(2,1)S(1)} collective-permute-done((bf16[80,128]{1,0:T(8,128)(2,1)S(1)}, bf16[80,128]{1,0:T(8,128)(2,1)S(1)}, u32[]{:S(2)}, u32[]{:S(2)}) %collective-permute-start.12) | collective-permute-done | bytes 20512 | tf_op jit(solution)/shard_map/ppermute | solution.py:453
  41.1 1.0 %finish.1 = (bf16[128,2048]{1,0:T(8,128)(2,1)}, f32[64,128]{1,0:T(8,128)}) custom-call(s32[1]{0:T(128)} %bitcast.ex_ref, bf16[128,2048]{1,0:T(8,128)(2,1)S(1)} %inner_transform.1.projected_ref, f32[72,128]{1,0:T(8,128)S(1)} %get-tuple-element.26.refs_0_, bf16[80,128]{1,0:T(8,128)(2,1)S(1)} %collective-permute-done.10.refs_1_, ...), custom_call_target="tpu_custom_call" | custom-call | flops 10000000000 | tf_op jit(solution)/shard_map/finish/pallas_call | solution.py:70
  (2 shorter events, 0.1 us)
Async XLA Ops:
  0.6 7.1 %copy-start = (bf16[128,65536]{1,0:T(8,128)(2,1)S(1)}, bf16[128,65536]{1,0:T(8,128)(2,1)}, u32[]{:S(2)}) copy-start(bf16[128,65536]{1,0:T(8,128)(2,1)} %refs_2_.1) | copy-start | bytes 50331652
  4.4 8.0 %collective-permute-start.1 = (bf16[2,32,2048]{2,1,0:T(8,128)(2,1)S(1)}, bf16[2,32,2048]{2,1,0:T(8,128)(2,1)S(1)}, u32[]{:S(2)}, u32[]{:S(2)}) collective-permute-start(bf16[2,32,2048]{2,1,0:T(8,128)(2,1)S(1)} %get-tuple-element.21), channel_id=1, source_target_pairs={{0,8},{1,17},{2,10},{3,19},{4,12},{5,21},{6,14},{7,23},{8,0},{9,25... | collective-permute-start | bytes 786440 | tf_op jit(solution)/shard_map/ppermute | solution.py:485
  9.4 13.9 %collective-permute-start = (bf16[2,48,2048]{2,1,0:T(8,128)(2,1)S(1)}, bf16[2,48,2048]{2,1,0:T(8,128)(2,1)S(1)}, u32[]{:S(2)}, u32[]{:S(2)}) collective-permute-start(bf16[2,48,2048]{2,1,0:T(8,128)(2,1)S(1)} %get-tuple-element.19.refs_2_), channel_id=1, source_target_pairs={{0,8},{1,17},{2,10},{3,19},{4,12},{5,21},{6,14},{7,23},{8,0},{9,25... | collective-permute-start | bytes 1179656 | tf_op jit(solution)/shard_map/ppermute | solution.py:485
  12.4 6.3 %collective-permute-start.2 = (bf16[1,32,2048]{2,1,0:T(8,128)(2,1)S(1)}, bf16[1,32,2048]{2,1,0:T(8,128)(2,1)S(1)}, u32[]{:S(2)}, u32[]{:S(2)}) collective-permute-start(bf16[1,32,2048]{2,1,0:T(8,128)(2,1)S(1)} %middle.3.refs_3_), channel_id=1, source_target_pairs={{0,16},{1,9},{2,18},{3,11},{4,20},{5,13},{6,22},{7,15},{8,24},{9,1... | collective-permute-start | bytes 393224 | tf_op jit(solution)/shard_map/ppermute | solution.py:485
  16.5 10.7 %collective-permute-start.4 = (bf16[2,80,2048]{2,1,0:T(8,128)(2,1)S(1)}, bf16[2,80,2048]{2,1,0:T(8,128)(2,1)S(1)}, u32[]{:S(2)}, u32[]{:S(2)}) collective-permute-start(bf16[2,80,2048]{2,1,0:T(8,128)(2,1)S(1)} %get-tuple-element.22.refs_3_), channel_id=1, source_target_pairs={{0,16},{1,9},{2,18},{3,11},{4,20},{5,13},{6,22},{7,15},{8,24},{9,1... | collective-permute-start | bytes 1966088 | tf_op jit(solution)/shard_map/ppermute | solution.py:485
  18.7 10.0 %collective-permute-start.8 = (bf16[32,2048]{1,0:T(8,128)(2,1)S(1)}, bf16[32,2048]{1,0:T(8,128)(2,1)S(1)}, u32[]{:S(2)}, u32[]{:S(2)}) collective-permute-start(bf16[32,2048]{1,0:T(8,128)(2,1)S(1)} %combine.1.refs_2_.refs_1_), channel_id=1, source_target_pairs={{0,6},{1,7},{2,4},{3,5},{4,2},{5,3},{6,0},{7,1},{8,14},{9,15},{10,... | collective-permute-start | bytes 393224 | tf_op jit(solution)/shard_map/ppermute | solution.py:453
  22.6 9.9 %collective-permute-start.7 = (bf16[32,2048]{1,0:T(8,128)(2,1)S(1)}, bf16[32,2048]{1,0:T(8,128)(2,1)S(1)}, u32[]{:S(2)}, u32[]{:S(2)}) collective-permute-start(bf16[32,2048]{1,0:T(8,128)(2,1)S(1)} %combine.1.refs_2_.refs_1_), channel_id=1, source_target_pairs={{0,4},{1,5},{2,6},{3,7},{4,0},{5,1},{6,2},{7,3},{8,12},{9,13},{10,... | collective-permute-start | bytes 393224 | tf_op jit(solution)/shard_map/ppermute | solution.py:453
  22.6 9.9 %collective-permute-start.6 = (bf16[32,2048]{1,0:T(8,128)(2,1)S(1)}, bf16[32,2048]{1,0:T(8,128)(2,1)S(1)}, u32[]{:S(2)}, u32[]{:S(2)}) collective-permute-start(bf16[32,2048]{1,0:T(8,128)(2,1)S(1)} %combine.1.refs_2_.refs_1_), channel_id=1, source_target_pairs={{0,2},{1,3},{2,0},{3,1},{4,6},{5,7},{6,4},{7,5},{8,10},{9,11},{10,... | collective-permute-start | bytes 393224 | tf_op jit(solution)/shard_map/ppermute | solution.py:453
  23.3 9.6 %collective-permute-start.3 = (bf16[1,48,2048]{2,1,0:T(8,128)(2,1)S(1)}, bf16[1,48,2048]{2,1,0:T(8,128)(2,1)S(1)}, u32[]{:S(2)}, u32[]{:S(2)}) collective-permute-start(bf16[1,48,2048]{2,1,0:T(8,128)(2,1)S(1)} %middle.4.refs_2_), channel_id=1, source_target_pairs={{0,16},{1,9},{2,18},{3,11},{4,20},{5,13},{6,22},{7,15},{8,24},{9,1... | collective-permute-start | bytes 589832 | tf_op jit(solution)/shard_map/ppermute | solution.py:485
  27.3 7.1 %collective-permute-start.5 = (bf16[1,80,2048]{2,1,0:T(8,128)(2,1)S(1)}, bf16[1,80,2048]{2,1,0:T(8,128)(2,1)S(1)}, u32[]{:S(2)}, u32[]{:S(2)}) collective-permute-start(bf16[1,80,2048]{2,1,0:T(8,128)(2,1)S(1)} %middle.5.refs_5_), channel_id=1, source_target_pairs={{0,8},{1,17},{2,10},{3,19},{4,12},{5,21},{6,14},{7,23},{8,0},{9,25... | collective-permute-start | bytes 983048 | tf_op jit(solution)/shard_map/ppermute | solution.py:485
  32.8 2.1 %collective-permute-start.9 = (bf16[144,2048]{1,0:T(8,128)(2,1)S(1)}, bf16[144,2048]{1,0:T(8,128)(2,1)S(1)}, u32[]{:S(2)}, u32[]{:S(2)}) collective-permute-start(bf16[144,2048]{1,0:T(8,128)(2,1)S(1)} %stack_targets.1.mine_ref), channel_id=1, source_target_pairs={{0,1},{1,0},{2,3},{3,2},{4,5},{5,4},{6,7},{7,6},{8,9},{9,8},{10,11... | collective-permute-start | bytes 1769480 | tf_op jit(solution)/shard_map/ppermute | solution.py:453
  34.9 4.0 %copy-start.1 = (bf16[256,256]{1,0:T(8,128)(2,1)S(1)}, bf16[256,256]{1,0:T(8,128)(2,1)}, u32[]{:S(2)}) copy-start(bf16[256,256]{1,0:T(8,128)(2,1)} %constant.23.clone.table_ref) | copy-start | bytes 393220
  35.4 4.7 %collective-permute-start.10 = (bf16[80,128]{1,0:T(8,128)(2,1)S(1)}, bf16[80,128]{1,0:T(8,128)(2,1)S(1)}, u32[]{:S(2)}, u32[]{:S(2)}) collective-permute-start(bf16[80,128]{1,0:T(8,128)(2,1)S(1)} %get-tuple-element.27), channel_id=1, source_target_pairs={{0,24},{8,16},{16,8},{24,0},{1,25},{9,17},{17,9},{25,1},{2,26},{10... | collective-permute-start | bytes 61448 | tf_op jit(solution)/shard_map/ppermute | solution.py:453
  36.8 3.8 %collective-permute-start.11 = (bf16[80,128]{1,0:T(8,128)(2,1)S(1)}, bf16[80,128]{1,0:T(8,128)(2,1)S(1)}, u32[]{:S(2)}, u32[]{:S(2)}) collective-permute-start(bf16[80,128]{1,0:T(8,128)(2,1)S(1)} %get-tuple-element.28), channel_id=1, source_target_pairs={{0,8},{8,0},{16,24},{24,16},{1,9},{9,1},{17,25},{25,17},{2,10},{10... | collective-permute-start | bytes 61448 | tf_op jit(solution)/shard_map/ppermute | solution.py:453
  37.4 3.8 %collective-permute-start.12 = (bf16[80,128]{1,0:T(8,128)(2,1)S(1)}, bf16[80,128]{1,0:T(8,128)(2,1)S(1)}, u32[]{:S(2)}, u32[]{:S(2)}) collective-permute-start(bf16[80,128]{1,0:T(8,128)(2,1)S(1)} %get-tuple-element.29), channel_id=1, source_target_pairs={{0,16},{8,24},{16,0},{24,8},{1,17},{9,25},{17,1},{25,9},{2,18},{10... | collective-permute-start | bytes 61448 | tf_op jit(solution)/shard_map/ppermute | solution.py:453

commit v3 on v1

--- a/solution.py
+++ b/solution.py
@@ -10,7 +10,7 @@
 from jax.sharding import PartitionSpec as P
 
 ROWS = 16
-LANES = 256
+LANES = 512
 CHUNKS = (48, 80)
 EPS = 1e-06
 MIB = 1 << 20
@@ -120,9 +120,12 @@
                     for p in range(blocks):
                         spread[p, :, span] = make_sign(p, span)
                 total = None
-                for p in range(blocks):
-                    piece = tile[:, pl.ds(pl.multiple_of(p * width + places[h] + start, lanes), lanes)]
-                    term = wide(piece * spread[p, :, span])
+                for p in range(0, blocks, 2):
+                    pair = [
+                        tile[:, pl.ds(pl.multiple_of(q * width + places[h] + start, lanes), lanes)] * spread[q, :, span]
+                        for q in range(p, min(p + 2, blocks))
+                    ]
+                    term = wide(sum(pair[1:], pair[0]))
                     total = term if total is None else total + term
                 sums.append(total)
             for d, value in enumerate(butterfly(sums)):
@@ -323,81 +326,89 @@
     return jnp.sum(value * value, axis=1, keepdims=True)
 
 
-def join_kernel(counts, *refs):
-    parts, (t1_ref, norms_ref) = refs[: sum(counts)], refs[sum(counts) :]
-    row, norms = 0, []
-    for count in counts:
-        chunk, parts = parts[:count], parts[count:]
-        total = narrow(add_parts(chunk, 0, 1)[0])
-        t1_ref[pl.ds(row, total.shape[0]), :] = total
-        row += total.shape[0]
-        norms.append(square_sums(total))
-    norms = as_row(jnp.concatenate(norms, axis=0))
-    norms_ref[...] = jnp.concatenate([norms, jnp.zeros((7, row), jnp.float32)], axis=0)
-
-
-def join(chunks):
-    parts = [part for chunk in chunks for part in chunk]
-    rows = sum(chunk[0].shape[1] for chunk in chunks)
-    return call(
-        functools.partial(join_kernel, [len(chunk) for chunk in chunks]),
-        [
-            jax.ShapeDtypeStruct((rows, parts[0].shape[2]), jnp.bfloat16),
-            jax.ShapeDtypeStruct((8, rows), jnp.float32),
-        ],
+def join_kernel(*refs):
+    refs[-1][...] = narrow(add_parts(refs[:-1], 0, 1)[0])
+
+
+def join(parts):
+    return call(
+        join_kernel,
+        jax.ShapeDtypeStruct(parts[0].shape[1:], jnp.bfloat16),
         parts,
         [VMEM] * len(parts),
         "join",
     )
 
 
-def gram_kernel(per, feat_ref, t1_ref, norms_ref, mine_ref, other_ref, *refs):
-    outs, products = refs[:-1], refs[-1]
+def gram_kernel(per, feat_ref, core_ref, mine_ref, other_ref, first_ref, *refs):
+    parts, last_ref, outs, products = refs[0], refs[1], refs[2], refs[3]
     feat = feat_ref[0]
-    rows = t1_ref.shape[0]
+    last = narrow(add_parts(parts, 0, 1)[0])
+    last_ref[...] = last
+    train = jnp.concatenate([first_ref[...], last], axis=0)
+    rows = train.shape[0]
     height = mine_ref.shape[0] - ROWS
     share = height // len(outs)
     target_norms = []
     for i, ref in enumerate((mine_ref, other_ref)):
         products[pl.ds(i * height, height), :] = lax.dot_general(
-            ref[pl.ds(0, height), :], t1_ref[...], (((1,), (1,)), ((), ())), preferred_element_type=jnp.float32
+            ref[pl.ds(0, height), :], train, (((1,), (1,)), ((), ())), preferred_element_type=jnp.float32
         )
         pieces = wide(ref[pl.ds(height, ROWS), pl.ds(0, height)])
         target_norms.append(pieces[0:1] + pieces[1:2] + pieces[2:3])
+    norms = as_row(square_sums(train))
+    count = len(outs).bit_length() - 1
     for d, out in enumerate(outs):
+        turned = reverse_bits(d, count)
+        number = jnp.where(core_ref[0] == 0, d, turned)
         for i in range(0, 2 * share, per):
-            first = pl.multiple_of((i * len(outs)) + (d ^ feat) * per, per)
+            first = pl.multiple_of((i * len(outs)) + (number ^ feat) * per, per)
             out[pl.ds(i, per), :] = products[pl.ds(first, per), :]
-        span = slice(d * share, (d + 1) * share)
+        straight, crossed = (
+            jnp.concatenate([x[:, i * share : (i + 1) * share] for x in target_norms], axis=1) for i in (d, turned)
+        )
         here = jnp.concatenate(
-            [x[:, span] for x in target_norms] + [jnp.zeros((1, rows - 2 * share), jnp.float32)], axis=1
+            [jnp.where(core_ref[0] == 0, straight, crossed), jnp.zeros((1, rows - 2 * share), jnp.float32)], axis=1
         )
-        out[pl.ds(2 * share, 8), :] = jnp.concatenate([norms_ref[0:1, :], here, jnp.zeros((6, rows), jnp.float32)], axis=0)
-
-
-def gram(feat_count, per, feat, t1, norms, mine, other):
+        out[pl.ds(2 * share, 8), :] = jnp.concatenate([norms, here, jnp.zeros((6, rows), jnp.float32)], axis=0)
+
+
+def gram(feat_count, per, feat, core, mine, other, first, parts):
     total = 2 * (mine.shape[0] - ROWS)
-    rows = t1.shape[0]
-    return call(
-        functools.partial(gram_kernel, per),
-        [jax.ShapeDtypeStruct((total // feat_count + 8, rows), jnp.float32)] * feat_count,
-        [feat, t1, norms, mine, other],
-        [SMEM] + [VMEM] * 4,
+    unused, last_rows, inner = parts[0].shape
+    rows = first.shape[0] + last_rows
+
+    def kernel(*refs):
+        split = 5 + len(parts)
+        gram_kernel(per, *refs[:5], refs[5:split], refs[split], refs[split + 1 : -1], refs[-1])
+
+    last, *outs = call(
+        kernel,
+        [jax.ShapeDtypeStruct((last_rows, inner), jnp.bfloat16)]
+        + [jax.ShapeDtypeStruct((total // feat_count + 8, rows), jnp.float32)] * feat_count,
+        [feat, core, mine, other, first, *parts],
+        [SMEM, SMEM] + [VMEM] * (3 + len(parts)),
         "gram",
         scratch=[pltpu.VMEM((total, rows), jnp.float32)],
     )
-
-
-def inner_kernel(scale, table_ref, t1_ref, out_ref):
-    out_ref[...] = inner_part(scale, table_ref[...], t1_ref[...])
-
-
-def inner_transform(scale, table, t1):
+    return last, outs
+
+
+def inner_kernel(scale, table_ref, *refs):
+    row = 0
+    for ref in refs[:-1]:
+        rows = ref.shape[0]
+        refs[-1][pl.ds(row, rows), :] = inner_part(scale, table_ref[...], ref[...])
+        row += rows
+
+
+def inner_transform(scale, table, chunks):
+    rows = sum(chunk.shape[0] for chunk in chunks)
     return call(
         functools.partial(inner_kernel, scale),
-        jax.ShapeDtypeStruct(t1.shape, jnp.bfloat16),
-        [table, t1],
-        [VMEM, VMEM],
+        jax.ShapeDtypeStruct((rows, chunks[0].shape[1]), jnp.bfloat16),
+        [table, *chunks],
+        [VMEM] * (1 + len(chunks)),
         "inner_transform",
         limit=16,
     )
@@ -494,11 +505,11 @@
     state[1], mark = proceed(orders[1], state[1], mark)
     mine = stack_targets(feat_count, per, feat, around, mark)
     other = swap(mine, "ex", 1)
-    t1, norms = join(state)
-    sums = gram(feat_count, per, feat, t1, norms, mine, other)
+    first = join(state[0])
+    last, sums = gram(feat_count, per, feat, core, mine, other, first, state[1])
     far = sorted(range(1, feat_count), key=lambda d: -d.bit_count())
-    sums = [sums[0]] + [swap(sums[d], "feat", d) for d in far]
-    projected = inner_transform(scale, table256, t1)
+    sums = [sums[0]] + [turn(sums[d], d) for d in far]
+    projected = inner_transform(scale, table256, [first, last])
     features, cosines = finish(mean_scale, per, ex.reshape(1), projected, sums)
     return features, cosines.reshape(groups, per, train_rows).transpose(2, 0, 1)
 

time: 42.8 us -> 41.9 us (0.979)
  Pallas kernels: 10.7 us -> 9.6 us
    ppermute x7 -> x10, starting transfers between devices: 12 us -> 15.8 us  [turn(): return lax.ppermute(value, ('feat', 'ex'), pairs)]
    ppermute x7 -> x4, starting transfers between devices: 8.08 us -> 4.52 us  [swap(): lax.ppermute(value, axis, [(i, i ^ distance) for i in range(lax.axis_size...]
    ppermute x7 -> x4, waiting for transfers between devices: 5.61 us -> 2.61 us  [swap(): lax.ppermute(value, axis, [(i, i ^ distance) for i in range(lax.axis_size...]
    ppermute x7 -> x10, waiting for transfers between devices: 5.52 us -> 8.51 us  [turn(): return lax.ppermute(value, ('feat', 'ex'), pairs)]
    pallas_call x11, Pallas kernels: 10.7 us -> 9.6 us  [call(): pl.pallas_call(body, out_shape=out_shape, in_specs=specs, out_specs=jax.t...]
  transfers between devices with their start and end apart: 14 -> 14, of which waited for: 6 -> 6; matrix products, arithmetic and copies ran while one was open for 0% -> 0% of each run, Pallas kernels for 13% -> 11%
where the time goes in v3:
time: 41.9 us; the launch traced here: 41.7 us
  starting transfers between devices  20.3 us (48%)
  waiting for transfers between devices  11.1 us (26%)
  Pallas kernels  9.6 us (23%)
  between operations  0.75 us (2%)
    ppermute x10, starting transfers between devices, turn(): return lax.ppermute(value, ('feat', 'ex'), pairs)  15.8 us
    pallas_call x11, Pallas kernels, call(): pl.pallas_call(body, out_shape=out_shape, in_specs=specs, out_specs=jax.t...  9.6 us
    ppermute x10, waiting for transfers between devices, turn(): return lax.ppermute(value, ('feat', 'ex'), pairs)  8.51 us
    ppermute x4, starting transfers between devices, swap(): lax.ppermute(value, axis, [(i, i ^ distance) for i in range(lax.axis_size...  4.52 us
    ppermute x4, waiting for transfers between devices, swap(): lax.ppermute(value, axis, [(i, i ^ distance) for i in range(lax.axis_size...  2.61 us
  transfers between devices with their start and end apart: 14, of which 6 were waited for; matrix products, arithmetic and copies ran while one was open for 0% of the time, Pallas kernels for 11%

profile of v3, /device:TPU:0, one launch (start us, length us, event | category | flops | bytes accessed | tf_op | source)
XLA Modules:
  0.0 41.7 jit_solution(11365044545462024037)
XLA Ops:
  0.6 0.0 copy-start
  0.7 3.4 %first_terms.1 = (bf16[32,2048]{1,0:T(8,128)(2,1)S(1)}, bf16[32,2048]{1,0:T(8,128)(2,1)S(1)}, bf16[32,2048]{1,0:T(8,128)(2,1)S(1)}, bf16[32,2048]{1,0:T(8,128)(2,1)S(1)}, bf16[8,16,8192]{2,1,0:T(8,128)(2,1)S(1)}) custom-call(s32[1]{0:T(128)} %bitcast.2.feat_ref.refs_0_, s32[1]{0:T(128)} %bitcast.1.core_ref.refs_0_.refs_1_, s32[32]{0:T(128)} %order_hbm.1, ...), custom_call_target="tpu_custom_call" | custom-call | flops 20000000000 | tf_op jit(solution)/shard_map/first_terms/pallas_call | solution.py:70
  4.0 3.0 %collective-permute-start.1 = (bf16[32,2048]{1,0:T(8,128)(2,1)S(1)}, bf16[32,2048]{1,0:T(8,128)(2,1)S(1)}, u32[]{:S(2)}, u32[]{:S(2)}) collective-permute-start(bf16[32,2048]{1,0:T(8,128)(2,1)S(1)} %get-tuple-element.22), channel_id=1, source_target_pairs={{0,8},{1,17},{2,10},{3,19},{4,12},{5,21},{6,14},{7,23},{8,0},{9,25... | collective-permute-start | bytes 393224 | tf_op jit(solution)/shard_map/ppermute | solution.py:479
  7.0 1.5 %collective-permute-start.2 = (bf16[32,2048]{1,0:T(8,128)(2,1)S(1)}, bf16[32,2048]{1,0:T(8,128)(2,1)S(1)}, u32[]{:S(2)}, u32[]{:S(2)}) collective-permute-start(bf16[32,2048]{1,0:T(8,128)(2,1)S(1)} %get-tuple-element.23), channel_id=1, source_target_pairs={{0,16},{1,9},{2,18},{3,11},{4,20},{5,13},{6,22},{7,15},{8,24},{9,1... | collective-permute-start | bytes 393224 | tf_op jit(solution)/shard_map/ppermute | solution.py:479
  8.6 0.0 collective-permute-start.3
  8.6 0.0 copy-done
  8.6 1.4 %terms.2 = (bf16[2,48,2048]{2,1,0:T(8,128)(2,1)S(1)}, bf16[2,48,2048]{2,1,0:T(8,128)(2,1)S(1)}) custom-call(s32[1]{0:T(128)} %bitcast.1.core_ref.refs_0_.refs_1_, bf16[8,16,8192]{2,1,0:T(8,128)(2,1)S(1)} %get-tuple-element.18.spread.refs_1_, bf16[128,65536]{1,0:T(8,128)(2,1)S(1)} %copy-done), custom_call_target="tpu_custom_call" | custom-call | flops 10000000000 | tf_op jit(solution)/shard_map/terms/pallas_call | solution.py:70
  10.0 2.2 %collective-permute-start = (bf16[2,48,2048]{2,1,0:T(8,128)(2,1)S(1)}, bf16[2,48,2048]{2,1,0:T(8,128)(2,1)S(1)}, u32[]{:S(2)}, u32[]{:S(2)}) collective-permute-start(bf16[2,48,2048]{2,1,0:T(8,128)(2,1)S(1)} %get-tuple-element.20.refs_3_), channel_id=1, source_target_pairs={{0,8},{1,17},{2,10},{3,19},{4,12},{5,21},{6,14},{7,23},{8,0},{9,25... | collective-permute-start | bytes 1179656 | tf_op jit(solution)/shard_map/ppermute | solution.py:479
  12.1 2.3 %terms.3 = (bf16[2,80,2048]{2,1,0:T(8,128)(2,1)S(1)}, bf16[2,80,2048]{2,1,0:T(8,128)(2,1)S(1)}) custom-call(s32[1]{0:T(128)} %bitcast.1.core_ref.refs_0_.refs_1_, bf16[8,16,8192]{2,1,0:T(8,128)(2,1)S(1)} %get-tuple-element.18.spread.refs_1_, bf16[128,65536]{1,0:T(8,128)(2,1)S(1)} %copy-done, bf16[2,48,2048]{2,1,0:T(8,128)(2,1)S(1)} %get-tuple-element.20.refs_3_), custom_call_target="tpu_custom_call" | custom-call | flops 10000000000 | tf_op jit(solution)/shard_map/terms/pallas_call | solution.py:70
  14.4 1.6 %collective-permute-start.8 = (bf16[2,80,2048]{2,1,0:T(8,128)(2,1)S(1)}, bf16[2,80,2048]{2,1,0:T(8,128)(2,1)S(1)}, u32[]{:S(2)}, u32[]{:S(2)}) collective-permute-start(bf16[2,80,2048]{2,1,0:T(8,128)(2,1)S(1)} %get-tuple-element.25.refs_4_), channel_id=1, source_target_pairs={{0,16},{1,9},{2,18},{3,11},{4,20},{5,13},{6,22},{7,15},{8,24},{9,1... | collective-permute-start | bytes 1966088 | tf_op jit(solution)/shard_map/ppermute | solution.py:479
  16.0 0.0 collective-permute-done.1.refs_1_
  16.0 0.0 collective-permute-done.2.refs_2_
  16.0 0.0 collective-permute-done.3.refs_3_
  16.0 0.1 combine.1.refs_2_.refs_1_
  16.1 3.7 %collective-permute-start.7 = (bf16[32,2048]{1,0:T(8,128)(2,1)S(1)}, bf16[32,2048]{1,0:T(8,128)(2,1)S(1)}, u32[]{:S(2)}, u32[]{:S(2)}) collective-permute-start(bf16[32,2048]{1,0:T(8,128)(2,1)S(1)} %combine.1.refs_2_.refs_1_), channel_id=1, source_target_pairs={{0,6},{1,7},{2,4},{3,5},{4,2},{5,3},{6,0},{7,1},{8,14},{9,15},{10,... | collective-permute-start | bytes 393224 | tf_op jit(solution)/shard_map/ppermute | solution.py:447
  19.7 0.0 collective-permute-start.6
  19.7 0.8 %collective-permute-start.5 = (bf16[32,2048]{1,0:T(8,128)(2,1)S(1)}, bf16[32,2048]{1,0:T(8,128)(2,1)S(1)}, u32[]{:S(2)}, u32[]{:S(2)}) collective-permute-start(bf16[32,2048]{1,0:T(8,128)(2,1)S(1)} %combine.1.refs_2_.refs_1_), channel_id=1, source_target_pairs={{0,2},{1,3},{2,0},{3,1},{4,6},{5,7},{6,4},{7,5},{8,10},{9,11},{10,... | collective-permute-start | bytes 393224 | tf_op jit(solution)/shard_map/ppermute | solution.py:447
  20.5 0.0 collective-permute-done.refs_1_
  20.6 2.4 %collective-permute-start.4 = (bf16[1,48,2048]{2,1,0:T(8,128)(2,1)S(1)}, bf16[1,48,2048]{2,1,0:T(8,128)(2,1)S(1)}, u32[]{:S(2)}, u32[]{:S(2)}) collective-permute-start(bf16[1,48,2048]{2,1,0:T(8,128)(2,1)S(1)} %middle.2.refs_2_), channel_id=1, source_target_pairs={{0,16},{1,9},{2,18},{3,11},{4,20},{5,13},{6,22},{7,15},{8,24},{9,1... | collective-permute-start | bytes 589832 | tf_op jit(solution)/shard_map/ppermute | solution.py:479
  23.0 3.1 %collective-permute-done.8.refs_1_.refs_6_ = bf16[2,80,2048]{2,1,0:T(8,128)(2,1)S(1)} collective-permute-done((bf16[2,80,2048]{2,1,0:T(8,128)(2,1)S(1)}, bf16[2,80,2048]{2,1,0:T(8,128)(2,1)S(1)}, u32[]{:S(2)}, u32[]{:S(2)}) %collective-permute-start.8) | collective-permute-done | bytes 655392 | tf_op jit(solution)/shard_map/ppermute | solution.py:479
  26.1 0.1 middle.3.refs_5_
  26.1 1.5 %collective-permute-start.10 = (bf16[1,80,2048]{2,1,0:T(8,128)(2,1)S(1)}, bf16[1,80,2048]{2,1,0:T(8,128)(2,1)S(1)}, u32[]{:S(2)}, u32[]{:S(2)}) collective-permute-start(bf16[1,80,2048]{2,1,0:T(8,128)(2,1)S(1)} %middle.3.refs_5_), channel_id=1, source_target_pairs={{0,8},{1,17},{2,10},{3,19},{4,12},{5,21},{6,14},{7,23},{8,0},{9,25... | collective-permute-start | bytes 983048 | tf_op jit(solution)/shard_map/ppermute | solution.py:479
  27.7 0.0 collective-permute-done.7.refs_4_
  27.7 2.6 %collective-permute-done.6.refs_3_ = bf16[32,2048]{1,0:T(8,128)(2,1)S(1)} collective-permute-done((bf16[32,2048]{1,0:T(8,128)(2,1)S(1)}, bf16[32,2048]{1,0:T(8,128)(2,1)S(1)}, u32[]{:S(2)}, u32[]{:S(2)}) %collective-permute-start.6) | collective-permute-done | bytes 131104 | tf_op jit(solution)/shard_map/ppermute | solution.py:447
  30.3 0.0 collective-permute-done.5.refs_2_
  30.3 0.3 stack_targets.1.refs_2_
  30.6 0.1 collective-permute-start.9
  30.6 0.0 collective-permute-done.4.refs_2_
  30.7 0.1 join.1.refs_4_.refs_0_
  30.7 0.0 copy-start.1
  30.8 2.5 %collective-permute-done.10.refs_7_ = bf16[1,80,2048]{2,1,0:T(8,128)(2,1)S(1)} collective-permute-done((bf16[1,80,2048]{2,1,0:T(8,128)(2,1)S(1)}, bf16[1,80,2048]{2,1,0:T(8,128)(2,1)S(1)}, u32[]{:S(2)}, u32[]{:S(2)}) %collective-permute-start.10) | collective-permute-done | bytes 327712 | tf_op jit(solution)/shard_map/ppermute | solution.py:479
  33.3 0.0 collective-permute-done.9.refs_3_
  33.3 0.5 %gram.1 = (bf16[80,2048]{1,0:T(8,128)(2,1)S(1)}, f32[72,128]{1,0:T(8,128)S(1)}, f32[72,128]{1,0:T(8,128)S(1)}, f32[72,128]{1,0:T(8,128)S(1)}, f32[72,128]{1,0:T(8,128)S(1)}) custom-call(s32[1]{0:T(128)} %bitcast.2.feat_ref.refs_0_, s32[1]{0:T(128)} %bitcast.1.core_ref.refs_0_.refs_1_, bf16[144,2048]{1,0:T(8,128)(2,1)S(1)} %stack_targets.1.refs_2_, ...), custom_call_target="tpu_custom_call" | custom-call | flops 10000000000 | tf_op jit(solution)/shard_map/gram/pallas_call | solution.py:70
  33.8 2.4 %collective-permute-start.11 = (f32[72,128]{1,0:T(8,128)S(1)}, f32[72,128]{1,0:T(8,128)S(1)}, u32[]{:S(2)}, u32[]{:S(2)}) collective-permute-start(f32[72,128]{1,0:T(8,128)S(1)} %get-tuple-element.29), channel_id=1, source_target_pairs={{0,24},{1,25},{2,26},{3,27},{4,28},{5,29},{6,30},{7,31},{8,16},{9,... | collective-permute-start | bytes 110600 | tf_op jit(solution)/shard_map/ppermute | solution.py:479
  36.1 0.7 %collective-permute-start.12 = (f32[72,128]{1,0:T(8,128)S(1)}, f32[72,128]{1,0:T(8,128)S(1)}, u32[]{:S(2)}, u32[]{:S(2)}) collective-permute-start(f32[72,128]{1,0:T(8,128)S(1)} %get-tuple-element.30), channel_id=1, source_target_pairs={{0,8},{1,17},{2,10},{3,19},{4,12},{5,21},{6,14},{7,23},{8,0},{9,25... | collective-permute-start | bytes 110600 | tf_op jit(solution)/shard_map/ppermute | solution.py:479
  36.8 0.5 %collective-permute-start.13 = (f32[72,128]{1,0:T(8,128)S(1)}, f32[72,128]{1,0:T(8,128)S(1)}, u32[]{:S(2)}, u32[]{:S(2)}) collective-permute-start(f32[72,128]{1,0:T(8,128)S(1)} %get-tuple-element.31), channel_id=1, source_target_pairs={{0,16},{1,9},{2,18},{3,11},{4,20},{5,13},{6,22},{7,15},{8,24},{9,1... | collective-permute-start | bytes 110600 | tf_op jit(solution)/shard_map/ppermute | solution.py:479
  37.3 0.0 copy-done.1
  37.3 0.5 %inner_transform.1.projected_ref = bf16[128,2048]{1,0:T(8,128)(2,1)S(1)} custom-call(bf16[256,256]{1,0:T(8,128)(2,1)S(1)} %copy-done.1, bf16[48,2048]{1,0:T(8,128)(2,1)S(1)} %join.1.refs_4_.refs_0_, bf16[80,2048]{1,0:T(8,128)(2,1)S(1)} %get-tuple-element.27.refs_1_), custom_call_target="tpu_custom_call" | custom-call | flops 10000000000 | tf_op jit(solution)/shard_map/inner_transform/pallas_call | solution.py:70
  37.9 0.9 %collective-permute-done.11.refs_1_ = f32[72,128]{1,0:T(8,128)S(1)} collective-permute-done((f32[72,128]{1,0:T(8,128)S(1)}, f32[72,128]{1,0:T(8,128)S(1)}, u32[]{:S(2)}, u32[]{:S(2)}) %collective-permute-start.11) | collective-permute-done | bytes 36896 | tf_op jit(solution)/shard_map/ppermute | solution.py:479
  38.8 1.3 %collective-permute-done.12.refs_2_ = f32[72,128]{1,0:T(8,128)S(1)} collective-permute-done((f32[72,128]{1,0:T(8,128)S(1)}, f32[72,128]{1,0:T(8,128)S(1)}, u32[]{:S(2)}, u32[]{:S(2)}) %collective-permute-start.12) | collective-permute-done | bytes 36896 | tf_op jit(solution)/shard_map/ppermute | solution.py:479
  40.1 0.7 %collective-permute-done.13.refs_3_ = f32[72,128]{1,0:T(8,128)S(1)} collective-permute-done((f32[72,128]{1,0:T(8,128)S(1)}, f32[72,128]{1,0:T(8,128)S(1)}, u32[]{:S(2)}, u32[]{:S(2)}) %collective-permute-start.13) | collective-permute-done | bytes 36896 | tf_op jit(solution)/shard_map/ppermute | solution.py:479
  40.8 1.0 %finish.1 = (bf16[128,2048]{1,0:T(8,128)(2,1)}, f32[64,128]{1,0:T(8,128)}) custom-call(s32[1]{0:T(128)} %bitcast.ex_ref, bf16[128,2048]{1,0:T(8,128)(2,1)S(1)} %inner_transform.1.projected_ref, f32[72,128]{1,0:T(8,128)S(1)} %get-tuple-element.28.refs_0_, f32[72,128]{1,0:T(8,128)S(1)} %collective-permute-done.11.refs_1_, ...), custom_call_target="tpu_custom_call" | custom-call | flops 10000000000 | tf_op jit(solution)/shard_map/finish/pallas_call | solution.py:70
  (1 shorter events, 0.0 us)
Async XLA Ops:
  0.6 7.9 %copy-start = (bf16[128,65536]{1,0:T(8,128)(2,1)S(1)}, bf16[128,65536]{1,0:T(8,128)(2,1)}, u32[]{:S(2)}) copy-start(bf16[128,65536]{1,0:T(8,128)(2,1)} %refs_2_.1) | copy-start | bytes 50331652
  4.0 12.0 %collective-permute-start.1 = (bf16[32,2048]{1,0:T(8,128)(2,1)S(1)}, bf16[32,2048]{1,0:T(8,128)(2,1)S(1)}, u32[]{:S(2)}, u32[]{:S(2)}) collective-permute-start(bf16[32,2048]{1,0:T(8,128)(2,1)S(1)} %get-tuple-element.22), channel_id=1, source_target_pairs={{0,8},{1,17},{2,10},{3,19},{4,12},{5,21},{6,14},{7,23},{8,0},{9,25... | collective-permute-start | bytes 393224 | tf_op jit(solution)/shard_map/ppermute | solution.py:479
  7.0 8.9 %collective-permute-start.2 = (bf16[32,2048]{1,0:T(8,128)(2,1)S(1)}, bf16[32,2048]{1,0:T(8,128)(2,1)S(1)}, u32[]{:S(2)}, u32[]{:S(2)}) collective-permute-start(bf16[32,2048]{1,0:T(8,128)(2,1)S(1)} %get-tuple-element.23), channel_id=1, source_target_pairs={{0,16},{1,9},{2,18},{3,11},{4,20},{5,13},{6,22},{7,15},{8,24},{9,1... | collective-permute-start | bytes 393224 | tf_op jit(solution)/shard_map/ppermute | solution.py:479
  8.6 7.4 %collective-permute-start.3 = (bf16[32,2048]{1,0:T(8,128)(2,1)S(1)}, bf16[32,2048]{1,0:T(8,128)(2,1)S(1)}, u32[]{:S(2)}, u32[]{:S(2)}) collective-permute-start(bf16[32,2048]{1,0:T(8,128)(2,1)S(1)} %get-tuple-element.24), channel_id=1, source_target_pairs={{0,24},{1,25},{2,26},{3,27},{4,28},{5,29},{6,30},{7,31},{8,16},{9,... | collective-permute-start | bytes 393224 | tf_op jit(solution)/shard_map/ppermute | solution.py:479
  10.0 10.6 %collective-permute-start = (bf16[2,48,2048]{2,1,0:T(8,128)(2,1)S(1)}, bf16[2,48,2048]{2,1,0:T(8,128)(2,1)S(1)}, u32[]{:S(2)}, u32[]{:S(2)}) collective-permute-start(bf16[2,48,2048]{2,1,0:T(8,128)(2,1)S(1)} %get-tuple-element.20.refs_3_), channel_id=1, source_target_pairs={{0,8},{1,17},{2,10},{3,19},{4,12},{5,21},{6,14},{7,23},{8,0},{9,25... | collective-permute-start | bytes 1179656 | tf_op jit(solution)/shard_map/ppermute | solution.py:479
  14.4 11.7 %collective-permute-start.8 = (bf16[2,80,2048]{2,1,0:T(8,128)(2,1)S(1)}, bf16[2,80,2048]{2,1,0:T(8,128)(2,1)S(1)}, u32[]{:S(2)}, u32[]{:S(2)}) collective-permute-start(bf16[2,80,2048]{2,1,0:T(8,128)(2,1)S(1)} %get-tuple-element.25.refs_4_), channel_id=1, source_target_pairs={{0,16},{1,9},{2,18},{3,11},{4,20},{5,13},{6,22},{7,15},{8,24},{9,1... | collective-permute-start | bytes 1966088 | tf_op jit(solution)/shard_map/ppermute | solution.py:479
  16.1 11.6 %collective-permute-start.7 = (bf16[32,2048]{1,0:T(8,128)(2,1)S(1)}, bf16[32,2048]{1,0:T(8,128)(2,1)S(1)}, u32[]{:S(2)}, u32[]{:S(2)}) collective-permute-start(bf16[32,2048]{1,0:T(8,128)(2,1)S(1)} %combine.1.refs_2_.refs_1_), channel_id=1, source_target_pairs={{0,6},{1,7},{2,4},{3,5},{4,2},{5,3},{6,0},{7,1},{8,14},{9,15},{10,... | collective-permute-start | bytes 393224 | tf_op jit(solution)/shard_map/ppermute | solution.py:447
  19.7 10.5 %collective-permute-start.6 = (bf16[32,2048]{1,0:T(8,128)(2,1)S(1)}, bf16[32,2048]{1,0:T(8,128)(2,1)S(1)}, u32[]{:S(2)}, u32[]{:S(2)}) collective-permute-start(bf16[32,2048]{1,0:T(8,128)(2,1)S(1)} %combine.1.refs_2_.refs_1_), channel_id=1, source_target_pairs={{0,4},{1,5},{2,6},{3,7},{4,0},{5,1},{6,2},{7,3},{8,12},{9,13},{10,... | collective-permute-start | bytes 393224 | tf_op jit(solution)/shard_map/ppermute | solution.py:447
  19.7 10.5 %collective-permute-start.5 = (bf16[32,2048]{1,0:T(8,128)(2,1)S(1)}, bf16[32,2048]{1,0:T(8,128)(2,1)S(1)}, u32[]{:S(2)}, u32[]{:S(2)}) collective-permute-start(bf16[32,2048]{1,0:T(8,128)(2,1)S(1)} %combine.1.refs_2_.refs_1_), channel_id=1, source_target_pairs={{0,2},{1,3},{2,0},{3,1},{4,6},{5,7},{6,4},{7,5},{8,10},{9,11},{10,... | collective-permute-start | bytes 393224 | tf_op jit(solution)/shard_map/ppermute | solution.py:447
  20.6 10.1 %collective-permute-start.4 = (bf16[1,48,2048]{2,1,0:T(8,128)(2,1)S(1)}, bf16[1,48,2048]{2,1,0:T(8,128)(2,1)S(1)}, u32[]{:S(2)}, u32[]{:S(2)}) collective-permute-start(bf16[1,48,2048]{2,1,0:T(8,128)(2,1)S(1)} %middle.2.refs_2_), channel_id=1, source_target_pairs={{0,16},{1,9},{2,18},{3,11},{4,20},{5,13},{6,22},{7,15},{8,24},{9,1... | collective-permute-start | bytes 589832 | tf_op jit(solution)/shard_map/ppermute | solution.py:479
  26.1 7.1 %collective-permute-start.10 = (bf16[1,80,2048]{2,1,0:T(8,128)(2,1)S(1)}, bf16[1,80,2048]{2,1,0:T(8,128)(2,1)S(1)}, u32[]{:S(2)}, u32[]{:S(2)}) collective-permute-start(bf16[1,80,2048]{2,1,0:T(8,128)(2,1)S(1)} %middle.3.refs_5_), channel_id=1, source_target_pairs={{0,8},{1,17},{2,10},{3,19},{4,12},{5,21},{6,14},{7,23},{8,0},{9,25... | collective-permute-start | bytes 983048 | tf_op jit(solution)/shard_map/ppermute | solution.py:479
  30.6 2.7 %collective-permute-start.9 = (bf16[144,2048]{1,0:T(8,128)(2,1)S(1)}, bf16[144,2048]{1,0:T(8,128)(2,1)S(1)}, u32[]{:S(2)}, u32[]{:S(2)}) collective-permute-start(bf16[144,2048]{1,0:T(8,128)(2,1)S(1)} %stack_targets.1.refs_2_), channel_id=1, source_target_pairs={{0,1},{1,0},{2,3},{3,2},{4,5},{5,4},{6,7},{7,6},{8,9},{9,8},{10,11... | collective-permute-start | bytes 1769480 | tf_op jit(solution)/shard_map/ppermute | solution.py:447
  30.7 6.6 %copy-start.1 = (bf16[256,256]{1,0:T(8,128)(2,1)S(1)}, bf16[256,256]{1,0:T(8,128)(2,1)}, u32[]{:S(2)}) copy-start(bf16[256,256]{1,0:T(8,128)(2,1)} %constant.23.clone.table_ref) | copy-start | bytes 393220
  33.8 5.0 %collective-permute-start.11 = (f32[72,128]{1,0:T(8,128)S(1)}, f32[72,128]{1,0:T(8,128)S(1)}, u32[]{:S(2)}, u32[]{:S(2)}) collective-permute-start(f32[72,128]{1,0:T(8,128)S(1)} %get-tuple-element.29), channel_id=1, source_target_pairs={{0,24},{1,25},{2,26},{3,27},{4,28},{5,29},{6,30},{7,31},{8,16},{9,... | collective-permute-start | bytes 110600 | tf_op jit(solution)/shard_map/ppermute | solution.py:479
  36.1 4.0 %collective-permute-start.12 = (f32[72,128]{1,0:T(8,128)S(1)}, f32[72,128]{1,0:T(8,128)S(1)}, u32[]{:S(2)}, u32[]{:S(2)}) collective-permute-start(f32[72,128]{1,0:T(8,128)S(1)} %get-tuple-element.30), channel_id=1, source_target_pairs={{0,8},{1,17},{2,10},{3,19},{4,12},{5,21},{6,14},{7,23},{8,0},{9,25... | collective-permute-start | bytes 110600 | tf_op jit(solution)/shard_map/ppermute | solution.py:479
  36.8 4.0 %collective-permute-start.13 = (f32[72,128]{1,0:T(8,128)S(1)}, f32[72,128]{1,0:T(8,128)S(1)}, u32[]{:S(2)}, u32[]{:S(2)}) collective-permute-start(f32[72,128]{1,0:T(8,128)S(1)} %get-tuple-element.31), channel_id=1, source_target_pairs={{0,16},{1,9},{2,18},{3,11},{4,20},{5,13},{6,22},{7,15},{8,24},{9,1... | collective-permute-start | bytes 110600 | tf_op jit(solution)/shard_map/ppermute | solution.py:479

commit v4 on v3

--- a/solution.py
+++ b/solution.py
@@ -13,6 +13,7 @@
 LANES = 512
 CHUNKS = (48, 80)
 EPS = 1e-06
+SHRINK = 1.0 / 32.0
 MIB = 1 << 20
 HBM = pl.BlockSpec(memory_space=pltpu.HBM)
 SMEM = pl.BlockSpec(memory_space=pltpu.SMEM)
@@ -120,12 +121,9 @@
                     for p in range(blocks):
                         spread[p, :, span] = make_sign(p, span)
                 total = None
-                for p in range(0, blocks, 2):
-                    pair = [
-                        tile[:, pl.ds(pl.multiple_of(q * width + places[h] + start, lanes), lanes)] * spread[q, :, span]
-                        for q in range(p, min(p + 2, blocks))
-                    ]
-                    term = wide(sum(pair[1:], pair[0]))
+                for p in range(blocks):
+                    piece = tile[:, pl.ds(pl.multiple_of(p * width + places[h] + start, lanes), lanes)]
+                    term = wide(piece * spread[p, :, span])
                     total = term if total is None else total + term
                 sums.append(total)
             for d, value in enumerate(butterfly(sums)):
@@ -156,7 +154,7 @@
         for shift in range(feat_count.bit_length() - 1):
             odd = odd ^ ((bits >> shift) & 1)
         span = pl.ds(h * inner, inner)
-        mine[:, span] = wide(signs[:, span] * (1 - 2 * odd))
+        mine[:, span] = wide(signs[:, span] * (1 - 2 * odd)) * SHRINK
 
     def make_sign(p, span):
         return narrow(jnp.broadcast_to(mine[pl.ds(p, 1), span], (ROWS, span.size)))
@@ -461,8 +459,8 @@
     train_rows, target_rows = train_grads.shape[0], target_grads.shape[0]
     per = target_rows // feat_count
     inner = width // feat_count
-    mean_scale = 1.0 / (block_total * width * feat_count)
-    scale = 1.0 / math.sqrt(block_total * width)
+    mean_scale = 1.0 / (block_total * width * feat_count * SHRINK**2)
+    scale = 1.0 / (math.sqrt(block_total * width) * SHRINK)
     table256 = inner_table(inner)
     bits = list(range(feat_count.bit_length() - 1))
     assert sum(CHUNKS) == train_rows

time: 41.9 us -> 42 us (level)
  transfers between devices with their start and end apart: 14 -> 14, of which waited for: 6 -> 6; matrix products, arithmetic and copies ran while one was open for 0% -> 0% of each run, Pallas kernels for 11% -> 12%
where the time goes in v4:
time: 42 us; the launch traced here: 41.9 us
  starting transfers between devices  20 us (48%)
  waiting for transfers between devices  11.3 us (27%)
  Pallas kernels  9.85 us (23%)
  between operations  0.75 us (2%)
    ppermute x10, starting transfers between devices, turn(): return lax.ppermute(value, ('feat', 'ex'), pairs)  15.4 us
    pallas_call x11, Pallas kernels, call(): pl.pallas_call(body, out_shape=out_shape, in_specs=specs, out_specs=jax.t...  9.85 us
    ppermute x10, waiting for transfers between devices, turn(): return lax.ppermute(value, ('feat', 'ex'), pairs)  8.63 us
    ppermute x4, starting transfers between devices, swap(): lax.ppermute(value, axis, [(i, i ^ distance) for i in range(lax.axis_size...  4.52 us
    ppermute x4, waiting for transfers between devices, swap(): lax.ppermute(value, axis, [(i, i ^ distance) for i in range(lax.axis_size...  2.65 us
  transfers between devices with their start and end apart: 14, of which 6 were waited for; matrix products, arithmetic and copies ran while one was open for 0% of the time, Pallas kernels for 12%

profile of v4, /device:TPU:0, one launch (start us, length us, event | category | flops | bytes accessed | tf_op | source)
XLA Modules:
  0.0 41.9 jit_solution(6942170462408951849)
XLA Ops:
  0.6 0.0 copy-start
  0.7 3.5 %first_terms.1 = (bf16[32,2048]{1,0:T(8,128)(2,1)S(1)}, bf16[32,2048]{1,0:T(8,128)(2,1)S(1)}, bf16[32,2048]{1,0:T(8,128)(2,1)S(1)}, bf16[32,2048]{1,0:T(8,128)(2,1)S(1)}, bf16[8,16,8192]{2,1,0:T(8,128)(2,1)S(1)}) custom-call(s32[1]{0:T(128)} %bitcast.2.feat_ref.refs_0_, s32[1]{0:T(128)} %bitcast.1.core_ref.refs_0_.refs_1_, s32[32]{0:T(128)} %order_hbm.1, ...), custom_call_target="tpu_custom_call" | custom-call | flops 20000000000 | tf_op jit(solution)/shard_map/first_terms/pallas_call | solution.py:71
  4.1 3.0 %collective-permute-start.1 = (bf16[32,2048]{1,0:T(8,128)(2,1)S(1)}, bf16[32,2048]{1,0:T(8,128)(2,1)S(1)}, u32[]{:S(2)}, u32[]{:S(2)}) collective-permute-start(bf16[32,2048]{1,0:T(8,128)(2,1)S(1)} %get-tuple-element.22), channel_id=1, source_target_pairs={{0,8},{1,17},{2,10},{3,19},{4,12},{5,21},{6,14},{7,23},{8,0},{9,25... | collective-permute-start | bytes 393224 | tf_op jit(solution)/shard_map/ppermute | solution.py:477
  7.1 1.5 %collective-permute-start.2 = (bf16[32,2048]{1,0:T(8,128)(2,1)S(1)}, bf16[32,2048]{1,0:T(8,128)(2,1)S(1)}, u32[]{:S(2)}, u32[]{:S(2)}) collective-permute-start(bf16[32,2048]{1,0:T(8,128)(2,1)S(1)} %get-tuple-element.23), channel_id=1, source_target_pairs={{0,16},{1,9},{2,18},{3,11},{4,20},{5,13},{6,22},{7,15},{8,24},{9,1... | collective-permute-start | bytes 393224 | tf_op jit(solution)/shard_map/ppermute | solution.py:477
  8.7 0.0 collective-permute-start.3
  8.7 0.0 copy-done
  8.7 1.4 %terms.2 = (bf16[2,48,2048]{2,1,0:T(8,128)(2,1)S(1)}, bf16[2,48,2048]{2,1,0:T(8,128)(2,1)S(1)}) custom-call(s32[1]{0:T(128)} %bitcast.1.core_ref.refs_0_.refs_1_, bf16[8,16,8192]{2,1,0:T(8,128)(2,1)S(1)} %get-tuple-element.18.spread.refs_1_, bf16[128,65536]{1,0:T(8,128)(2,1)S(1)} %copy-done), custom_call_target="tpu_custom_call" | custom-call | flops 10000000000 | tf_op jit(solution)/shard_map/terms/pallas_call | solution.py:71
  10.1 2.1 %collective-permute-start = (bf16[2,48,2048]{2,1,0:T(8,128)(2,1)S(1)}, bf16[2,48,2048]{2,1,0:T(8,128)(2,1)S(1)}, u32[]{:S(2)}, u32[]{:S(2)}) collective-permute-start(bf16[2,48,2048]{2,1,0:T(8,128)(2,1)S(1)} %get-tuple-element.20.refs_3_), channel_id=1, source_target_pairs={{0,8},{1,17},{2,10},{3,19},{4,12},{5,21},{6,14},{7,23},{8,0},{9,25... | collective-permute-start | bytes 1179656 | tf_op jit(solution)/shard_map/ppermute | solution.py:477
  12.2 2.4 %terms.3 = (bf16[2,80,2048]{2,1,0:T(8,128)(2,1)S(1)}, bf16[2,80,2048]{2,1,0:T(8,128)(2,1)S(1)}) custom-call(s32[1]{0:T(128)} %bitcast.1.core_ref.refs_0_.refs_1_, bf16[8,16,8192]{2,1,0:T(8,128)(2,1)S(1)} %get-tuple-element.18.spread.refs_1_, bf16[128,65536]{1,0:T(8,128)(2,1)S(1)} %copy-done, bf16[2,48,2048]{2,1,0:T(8,128)(2,1)S(1)} %get-tuple-element.20.refs_3_), custom_call_target="tpu_custom_call" | custom-call | flops 10000000000 | tf_op jit(solution)/shard_map/terms/pallas_call | solution.py:71
  14.6 1.6 %collective-permute-start.8 = (bf16[2,80,2048]{2,1,0:T(8,128)(2,1)S(1)}, bf16[2,80,2048]{2,1,0:T(8,128)(2,1)S(1)}, u32[]{:S(2)}, u32[]{:S(2)}) collective-permute-start(bf16[2,80,2048]{2,1,0:T(8,128)(2,1)S(1)} %get-tuple-element.25.refs_4_), channel_id=1, source_target_pairs={{0,16},{1,9},{2,18},{3,11},{4,20},{5,13},{6,22},{7,15},{8,24},{9,1... | collective-permute-start | bytes 1966088 | tf_op jit(solution)/shard_map/ppermute | solution.py:477
  16.1 0.0 collective-permute-done.1.refs_1_
  16.1 0.0 collective-permute-done.2.refs_2_
  16.1 0.0 collective-permute-done.3.refs_3_
  16.1 0.1 combine.1.refs_2_.refs_1_
  16.2 3.7 %collective-permute-start.7 = (bf16[32,2048]{1,0:T(8,128)(2,1)S(1)}, bf16[32,2048]{1,0:T(8,128)(2,1)S(1)}, u32[]{:S(2)}, u32[]{:S(2)}) collective-permute-start(bf16[32,2048]{1,0:T(8,128)(2,1)S(1)} %combine.1.refs_2_.refs_1_), channel_id=1, source_target_pairs={{0,6},{1,7},{2,4},{3,5},{4,2},{5,3},{6,0},{7,1},{8,14},{9,15},{10,... | collective-permute-start | bytes 393224 | tf_op jit(solution)/shard_map/ppermute | solution.py:445
  19.9 0.0 collective-permute-start.6
  19.9 0.8 %collective-permute-start.5 = (bf16[32,2048]{1,0:T(8,128)(2,1)S(1)}, bf16[32,2048]{1,0:T(8,128)(2,1)S(1)}, u32[]{:S(2)}, u32[]{:S(2)}) collective-permute-start(bf16[32,2048]{1,0:T(8,128)(2,1)S(1)} %combine.1.refs_2_.refs_1_), channel_id=1, source_target_pairs={{0,2},{1,3},{2,0},{3,1},{4,6},{5,7},{6,4},{7,5},{8,10},{9,11},{10,... | collective-permute-start | bytes 393224 | tf_op jit(solution)/shard_map/ppermute | solution.py:445
  20.7 0.0 collective-permute-done.refs_1_
  20.7 2.2 %collective-permute-start.4 = (bf16[1,48,2048]{2,1,0:T(8,128)(2,1)S(1)}, bf16[1,48,2048]{2,1,0:T(8,128)(2,1)S(1)}, u32[]{:S(2)}, u32[]{:S(2)}) collective-permute-start(bf16[1,48,2048]{2,1,0:T(8,128)(2,1)S(1)} %middle.2.refs_2_), channel_id=1, source_target_pairs={{0,16},{1,9},{2,18},{3,11},{4,20},{5,13},{6,22},{7,15},{8,24},{9,1... | collective-permute-start | bytes 589832 | tf_op jit(solution)/shard_map/ppermute | solution.py:477
  22.9 3.2 %collective-permute-done.8.refs_1_.refs_6_ = bf16[2,80,2048]{2,1,0:T(8,128)(2,1)S(1)} collective-permute-done((bf16[2,80,2048]{2,1,0:T(8,128)(2,1)S(1)}, bf16[2,80,2048]{2,1,0:T(8,128)(2,1)S(1)}, u32[]{:S(2)}, u32[]{:S(2)}) %collective-permute-start.8) | collective-permute-done | bytes 655392 | tf_op jit(solution)/shard_map/ppermute | solution.py:477
  26.2 0.1 middle.3.refs_5_
  26.2 1.5 %collective-permute-start.10 = (bf16[1,80,2048]{2,1,0:T(8,128)(2,1)S(1)}, bf16[1,80,2048]{2,1,0:T(8,128)(2,1)S(1)}, u32[]{:S(2)}, u32[]{:S(2)}) collective-permute-start(bf16[1,80,2048]{2,1,0:T(8,128)(2,1)S(1)} %middle.3.refs_5_), channel_id=1, source_target_pairs={{0,8},{1,17},{2,10},{3,19},{4,12},{5,21},{6,14},{7,23},{8,0},{9,25... | collective-permute-start | bytes 983048 | tf_op jit(solution)/shard_map/ppermute | solution.py:477
  27.8 0.0 collective-permute-done.7.refs_4_
  27.8 2.6 %collective-permute-done.6.refs_3_ = bf16[32,2048]{1,0:T(8,128)(2,1)S(1)} collective-permute-done((bf16[32,2048]{1,0:T(8,128)(2,1)S(1)}, bf16[32,2048]{1,0:T(8,128)(2,1)S(1)}, u32[]{:S(2)}, u32[]{:S(2)}) %collective-permute-start.6) | collective-permute-done | bytes 131104 | tf_op jit(solution)/shard_map/ppermute | solution.py:445
  30.4 0.0 collective-permute-done.5.refs_2_
  30.4 0.3 stack_targets.1.refs_2_
  30.7 0.1 collective-permute-start.9
  30.8 0.0 collective-permute-done.4.refs_2_
  30.8 0.1 join.1.refs_4_.refs_0_
  30.9 0.0 copy-start.1
  30.9 2.5 %collective-permute-done.10.refs_7_ = bf16[1,80,2048]{2,1,0:T(8,128)(2,1)S(1)} collective-permute-done((bf16[1,80,2048]{2,1,0:T(8,128)(2,1)S(1)}, bf16[1,80,2048]{2,1,0:T(8,128)(2,1)S(1)}, u32[]{:S(2)}, u32[]{:S(2)}) %collective-permute-start.10) | collective-permute-done | bytes 327712 | tf_op jit(solution)/shard_map/ppermute | solution.py:477
  33.4 0.0 collective-permute-done.9.refs_3_
  33.4 0.5 %gram.1 = (bf16[80,2048]{1,0:T(8,128)(2,1)S(1)}, f32[72,128]{1,0:T(8,128)S(1)}, f32[72,128]{1,0:T(8,128)S(1)}, f32[72,128]{1,0:T(8,128)S(1)}, f32[72,128]{1,0:T(8,128)S(1)}) custom-call(s32[1]{0:T(128)} %bitcast.2.feat_ref.refs_0_, s32[1]{0:T(128)} %bitcast.1.core_ref.refs_0_.refs_1_, bf16[144,2048]{1,0:T(8,128)(2,1)S(1)} %stack_targets.1.refs_2_, ...), custom_call_target="tpu_custom_call" | custom-call | flops 10000000000 | tf_op jit(solution)/shard_map/gram/pallas_call | solution.py:71
  33.9 2.4 %collective-permute-start.11 = (f32[72,128]{1,0:T(8,128)S(1)}, f32[72,128]{1,0:T(8,128)S(1)}, u32[]{:S(2)}, u32[]{:S(2)}) collective-permute-start(f32[72,128]{1,0:T(8,128)S(1)} %get-tuple-element.29), channel_id=1, source_target_pairs={{0,24},{1,25},{2,26},{3,27},{4,28},{5,29},{6,30},{7,31},{8,16},{9,... | collective-permute-start | bytes 110600 | tf_op jit(solution)/shard_map/ppermute | solution.py:477
  36.2 0.7 %collective-permute-start.12 = (f32[72,128]{1,0:T(8,128)S(1)}, f32[72,128]{1,0:T(8,128)S(1)}, u32[]{:S(2)}, u32[]{:S(2)}) collective-permute-start(f32[72,128]{1,0:T(8,128)S(1)} %get-tuple-element.30), channel_id=1, source_target_pairs={{0,8},{1,17},{2,10},{3,19},{4,12},{5,21},{6,14},{7,23},{8,0},{9,25... | collective-permute-start | bytes 110600 | tf_op jit(solution)/shard_map/ppermute | solution.py:477
  36.9 0.5 %collective-permute-start.13 = (f32[72,128]{1,0:T(8,128)S(1)}, f32[72,128]{1,0:T(8,128)S(1)}, u32[]{:S(2)}, u32[]{:S(2)}) collective-permute-start(f32[72,128]{1,0:T(8,128)S(1)} %get-tuple-element.31), channel_id=1, source_target_pairs={{0,16},{1,9},{2,18},{3,11},{4,20},{5,13},{6,22},{7,15},{8,24},{9,1... | collective-permute-start | bytes 110600 | tf_op jit(solution)/shard_map/ppermute | solution.py:477
  37.4 0.0 copy-done.1
  37.4 0.5 %inner_transform.1.projected_ref = bf16[128,2048]{1,0:T(8,128)(2,1)S(1)} custom-call(bf16[256,256]{1,0:T(8,128)(2,1)S(1)} %copy-done.1, bf16[48,2048]{1,0:T(8,128)(2,1)S(1)} %join.1.refs_4_.refs_0_, bf16[80,2048]{1,0:T(8,128)(2,1)S(1)} %get-tuple-element.27.refs_1_), custom_call_target="tpu_custom_call" | custom-call | flops 10000000000 | tf_op jit(solution)/shard_map/inner_transform/pallas_call | solution.py:71
  38.0 0.9 %collective-permute-done.11.refs_1_ = f32[72,128]{1,0:T(8,128)S(1)} collective-permute-done((f32[72,128]{1,0:T(8,128)S(1)}, f32[72,128]{1,0:T(8,128)S(1)}, u32[]{:S(2)}, u32[]{:S(2)}) %collective-permute-start.11) | collective-permute-done | bytes 36896 | tf_op jit(solution)/shard_map/ppermute | solution.py:477
  38.9 1.3 %collective-permute-done.12.refs_2_ = f32[72,128]{1,0:T(8,128)S(1)} collective-permute-done((f32[72,128]{1,0:T(8,128)S(1)}, f32[72,128]{1,0:T(8,128)S(1)}, u32[]{:S(2)}, u32[]{:S(2)}) %collective-permute-start.12) | collective-permute-done | bytes 36896 | tf_op jit(solution)/shard_map/ppermute | solution.py:477
  40.2 0.7 %collective-permute-done.13.refs_3_ = f32[72,128]{1,0:T(8,128)S(1)} collective-permute-done((f32[72,128]{1,0:T(8,128)S(1)}, f32[72,128]{1,0:T(8,128)S(1)}, u32[]{:S(2)}, u32[]{:S(2)}) %collective-permute-start.13) | collective-permute-done | bytes 36896 | tf_op jit(solution)/shard_map/ppermute | solution.py:477
  40.9 1.0 %finish.1 = (bf16[128,2048]{1,0:T(8,128)(2,1)}, f32[64,128]{1,0:T(8,128)}) custom-call(s32[1]{0:T(128)} %bitcast.ex_ref, bf16[128,2048]{1,0:T(8,128)(2,1)S(1)} %inner_transform.1.projected_ref, f32[72,128]{1,0:T(8,128)S(1)} %get-tuple-element.28.refs_0_, f32[72,128]{1,0:T(8,128)S(1)} %collective-permute-done.11.refs_1_, ...), custom_call_target="tpu_custom_call" | custom-call | flops 10000000000 | tf_op jit(solution)/shard_map/finish/pallas_call | solution.py:71
  (1 shorter events, 0.0 us)
Async XLA Ops:
  0.6 8.0 %copy-start = (bf16[128,65536]{1,0:T(8,128)(2,1)S(1)}, bf16[128,65536]{1,0:T(8,128)(2,1)}, u32[]{:S(2)}) copy-start(bf16[128,65536]{1,0:T(8,128)(2,1)} %refs_2_.1) | copy-start | bytes 50331652
  4.1 12.0 %collective-permute-start.1 = (bf16[32,2048]{1,0:T(8,128)(2,1)S(1)}, bf16[32,2048]{1,0:T(8,128)(2,1)S(1)}, u32[]{:S(2)}, u32[]{:S(2)}) collective-permute-start(bf16[32,2048]{1,0:T(8,128)(2,1)S(1)} %get-tuple-element.22), channel_id=1, source_target_pairs={{0,8},{1,17},{2,10},{3,19},{4,12},{5,21},{6,14},{7,23},{8,0},{9,25... | collective-permute-start | bytes 393224 | tf_op jit(solution)/shard_map/ppermute | solution.py:477
  7.1 9.0 %collective-permute-start.2 = (bf16[32,2048]{1,0:T(8,128)(2,1)S(1)}, bf16[32,2048]{1,0:T(8,128)(2,1)S(1)}, u32[]{:S(2)}, u32[]{:S(2)}) collective-permute-start(bf16[32,2048]{1,0:T(8,128)(2,1)S(1)} %get-tuple-element.23), channel_id=1, source_target_pairs={{0,16},{1,9},{2,18},{3,11},{4,20},{5,13},{6,22},{7,15},{8,24},{9,1... | collective-permute-start | bytes 393224 | tf_op jit(solution)/shard_map/ppermute | solution.py:477
  8.7 7.5 %collective-permute-start.3 = (bf16[32,2048]{1,0:T(8,128)(2,1)S(1)}, bf16[32,2048]{1,0:T(8,128)(2,1)S(1)}, u32[]{:S(2)}, u32[]{:S(2)}) collective-permute-start(bf16[32,2048]{1,0:T(8,128)(2,1)S(1)} %get-tuple-element.24), channel_id=1, source_target_pairs={{0,24},{1,25},{2,26},{3,27},{4,28},{5,29},{6,30},{7,31},{8,16},{9,... | collective-permute-start | bytes 393224 | tf_op jit(solution)/shard_map/ppermute | solution.py:477
  10.1 10.6 %collective-permute-start = (bf16[2,48,2048]{2,1,0:T(8,128)(2,1)S(1)}, bf16[2,48,2048]{2,1,0:T(8,128)(2,1)S(1)}, u32[]{:S(2)}, u32[]{:S(2)}) collective-permute-start(bf16[2,48,2048]{2,1,0:T(8,128)(2,1)S(1)} %get-tuple-element.20.refs_3_), channel_id=1, source_target_pairs={{0,8},{1,17},{2,10},{3,19},{4,12},{5,21},{6,14},{7,23},{8,0},{9,25... | collective-permute-start | bytes 1179656 | tf_op jit(solution)/shard_map/ppermute | solution.py:477
  14.6 11.6 %collective-permute-start.8 = (bf16[2,80,2048]{2,1,0:T(8,128)(2,1)S(1)}, bf16[2,80,2048]{2,1,0:T(8,128)(2,1)S(1)}, u32[]{:S(2)}, u32[]{:S(2)}) collective-permute-start(bf16[2,80,2048]{2,1,0:T(8,128)(2,1)S(1)} %get-tuple-element.25.refs_4_), channel_id=1, source_target_pairs={{0,16},{1,9},{2,18},{3,11},{4,20},{5,13},{6,22},{7,15},{8,24},{9,1... | collective-permute-start | bytes 1966088 | tf_op jit(solution)/shard_map/ppermute | solution.py:477
  16.2 11.5 %collective-permute-start.7 = (bf16[32,2048]{1,0:T(8,128)(2,1)S(1)}, bf16[32,2048]{1,0:T(8,128)(2,1)S(1)}, u32[]{:S(2)}, u32[]{:S(2)}) collective-permute-start(bf16[32,2048]{1,0:T(8,128)(2,1)S(1)} %combine.1.refs_2_.refs_1_), channel_id=1, source_target_pairs={{0,6},{1,7},{2,4},{3,5},{4,2},{5,3},{6,0},{7,1},{8,14},{9,15},{10,... | collective-permute-start | bytes 393224 | tf_op jit(solution)/shard_map/ppermute | solution.py:445
  19.9 10.5 %collective-permute-start.6 = (bf16[32,2048]{1,0:T(8,128)(2,1)S(1)}, bf16[32,2048]{1,0:T(8,128)(2,1)S(1)}, u32[]{:S(2)}, u32[]{:S(2)}) collective-permute-start(bf16[32,2048]{1,0:T(8,128)(2,1)S(1)} %combine.1.refs_2_.refs_1_), channel_id=1, source_target_pairs={{0,4},{1,5},{2,6},{3,7},{4,0},{5,1},{6,2},{7,3},{8,12},{9,13},{10,... | collective-permute-start | bytes 393224 | tf_op jit(solution)/shard_map/ppermute | solution.py:445
  19.9 10.5 %collective-permute-start.5 = (bf16[32,2048]{1,0:T(8,128)(2,1)S(1)}, bf16[32,2048]{1,0:T(8,128)(2,1)S(1)}, u32[]{:S(2)}, u32[]{:S(2)}) collective-permute-start(bf16[32,2048]{1,0:T(8,128)(2,1)S(1)} %combine.1.refs_2_.refs_1_), channel_id=1, source_target_pairs={{0,2},{1,3},{2,0},{3,1},{4,6},{5,7},{6,4},{7,5},{8,10},{9,11},{10,... | collective-permute-start | bytes 393224 | tf_op jit(solution)/shard_map/ppermute | solution.py:445
  20.7 10.1 %collective-permute-start.4 = (bf16[1,48,2048]{2,1,0:T(8,128)(2,1)S(1)}, bf16[1,48,2048]{2,1,0:T(8,128)(2,1)S(1)}, u32[]{:S(2)}, u32[]{:S(2)}) collective-permute-start(bf16[1,48,2048]{2,1,0:T(8,128)(2,1)S(1)} %middle.2.refs_2_), channel_id=1, source_target_pairs={{0,16},{1,9},{2,18},{3,11},{4,20},{5,13},{6,22},{7,15},{8,24},{9,1... | collective-permute-start | bytes 589832 | tf_op jit(solution)/shard_map/ppermute | solution.py:477
  26.2 7.1 %collective-permute-start.10 = (bf16[1,80,2048]{2,1,0:T(8,128)(2,1)S(1)}, bf16[1,80,2048]{2,1,0:T(8,128)(2,1)S(1)}, u32[]{:S(2)}, u32[]{:S(2)}) collective-permute-start(bf16[1,80,2048]{2,1,0:T(8,128)(2,1)S(1)} %middle.3.refs_5_), channel_id=1, source_target_pairs={{0,8},{1,17},{2,10},{3,19},{4,12},{5,21},{6,14},{7,23},{8,0},{9,25... | collective-permute-start | bytes 983048 | tf_op jit(solution)/shard_map/ppermute | solution.py:477
  30.7 2.7 %collective-permute-start.9 = (bf16[144,2048]{1,0:T(8,128)(2,1)S(1)}, bf16[144,2048]{1,0:T(8,128)(2,1)S(1)}, u32[]{:S(2)}, u32[]{:S(2)}) collective-permute-start(bf16[144,2048]{1,0:T(8,128)(2,1)S(1)} %stack_targets.1.refs_2_), channel_id=1, source_target_pairs={{0,1},{1,0},{2,3},{3,2},{4,5},{5,4},{6,7},{7,6},{8,9},{9,8},{10,11... | collective-permute-start | bytes 1769480 | tf_op jit(solution)/shard_map/ppermute | solution.py:445
  30.9 6.5 %copy-start.1 = (bf16[256,256]{1,0:T(8,128)(2,1)S(1)}, bf16[256,256]{1,0:T(8,128)(2,1)}, u32[]{:S(2)}) copy-start(bf16[256,256]{1,0:T(8,128)(2,1)} %constant.23.clone.table_ref) | copy-start | bytes 393220
  33.9 5.0 %collective-permute-start.11 = (f32[72,128]{1,0:T(8,128)S(1)}, f32[72,128]{1,0:T(8,128)S(1)}, u32[]{:S(2)}, u32[]{:S(2)}) collective-permute-start(f32[72,128]{1,0:T(8,128)S(1)} %get-tuple-element.29), channel_id=1, source_target_pairs={{0,24},{1,25},{2,26},{3,27},{4,28},{5,29},{6,30},{7,31},{8,16},{9,... | collective-permute-start | bytes 110600 | tf_op jit(solution)/shard_map/ppermute | solution.py:477
  36.2 4.0 %collective-permute-start.12 = (f32[72,128]{1,0:T(8,128)S(1)}, f32[72,128]{1,0:T(8,128)S(1)}, u32[]{:S(2)}, u32[]{:S(2)}) collective-permute-start(f32[72,128]{1,0:T(8,128)S(1)} %get-tuple-element.30), channel_id=1, source_target_pairs={{0,8},{1,17},{2,10},{3,19},{4,12},{5,21},{6,14},{7,23},{8,0},{9,25... | collective-permute-start | bytes 110600 | tf_op jit(solution)/shard_map/ppermute | solution.py:477
  36.9 4.0 %collective-permute-start.13 = (f32[72,128]{1,0:T(8,128)S(1)}, f32[72,128]{1,0:T(8,128)S(1)}, u32[]{:S(2)}, u32[]{:S(2)}) collective-permute-start(f32[72,128]{1,0:T(8,128)S(1)} %get-tuple-element.31), channel_id=1, source_target_pairs={{0,16},{1,9},{2,18},{3,11},{4,20},{5,13},{6,22},{7,15},{8,24},{9,1... | collective-permute-start | bytes 110600 | tf_op jit(solution)/shard_map/ppermute | solution.py:477

commit v5 on v3

--- a/solution.py
+++ b/solution.py
@@ -13,6 +13,7 @@
 LANES = 512
 CHUNKS = (48, 80)
 EPS = 1e-06
+SHRINK = 1.0 / 32.0
 MIB = 1 << 20
 HBM = pl.BlockSpec(memory_space=pltpu.HBM)
 SMEM = pl.BlockSpec(memory_space=pltpu.SMEM)
@@ -156,7 +157,7 @@
         for shift in range(feat_count.bit_length() - 1):
             odd = odd ^ ((bits >> shift) & 1)
         span = pl.ds(h * inner, inner)
-        mine[:, span] = wide(signs[:, span] * (1 - 2 * odd))
+        mine[:, span] = wide(signs[:, span] * (1 - 2 * odd)) * SHRINK
 
     def make_sign(p, span):
         return narrow(jnp.broadcast_to(mine[pl.ds(p, 1), span], (ROWS, span.size)))
@@ -461,8 +462,8 @@
     train_rows, target_rows = train_grads.shape[0], target_grads.shape[0]
     per = target_rows // feat_count
     inner = width // feat_count
-    mean_scale = 1.0 / (block_total * width * feat_count)
-    scale = 1.0 / math.sqrt(block_total * width)
+    mean_scale = 1.0 / (block_total * width * feat_count * SHRINK**2)
+    scale = 1.0 / (math.sqrt(block_total * width) * SHRINK)
     table256 = inner_table(inner)
     bits = list(range(feat_count.bit_length() - 1))
     assert sum(CHUNKS) == train_rows

time: 41.9 us -> 41.9 us (level)
  no operation moved by 1% of the time
where the time goes in v5:
time: 41.9 us; the launch traced here: 41.8 us
  starting transfers between devices  20.3 us (48%)
  waiting for transfers between devices  11.1 us (26%)
  Pallas kernels  9.61 us (23%)
  between operations  0.75 us (2%)
    ppermute x10, starting transfers between devices, turn(): return lax.ppermute(value, ('feat', 'ex'), pairs)  15.7 us
    pallas_call x11, Pallas kernels, call(): pl.pallas_call(body, out_shape=out_shape, in_specs=specs, out_specs=jax.t...  9.61 us
    ppermute x10, waiting for transfers between devices, turn(): return lax.ppermute(value, ('feat', 'ex'), pairs)  8.52 us
    ppermute x4, starting transfers between devices, swap(): lax.ppermute(value, axis, [(i, i ^ distance) for i in range(lax.axis_size...  4.52 us
    ppermute x4, waiting for transfers between devices, swap(): lax.ppermute(value, axis, [(i, i ^ distance) for i in range(lax.axis_size...  2.6 us
  transfers between devices with their start and end apart: 14, of which 6 were waited for; matrix products, arithmetic and copies ran while one was open for 0% of the time, Pallas kernels for 11%

profile of v5, /device:TPU:0, one launch (start us, length us, event | category | flops | bytes accessed | tf_op | source)
XLA Modules:
  0.0 41.8 jit_solution(12767110765647759734)
XLA Ops:
  0.6 0.0 copy-start
  0.7 3.4 %first_terms.1 = (bf16[32,2048]{1,0:T(8,128)(2,1)S(1)}, bf16[32,2048]{1,0:T(8,128)(2,1)S(1)}, bf16[32,2048]{1,0:T(8,128)(2,1)S(1)}, bf16[32,2048]{1,0:T(8,128)(2,1)S(1)}, bf16[8,16,8192]{2,1,0:T(8,128)(2,1)S(1)}) custom-call(s32[1]{0:T(128)} %bitcast.2.feat_ref.refs_0_, s32[1]{0:T(128)} %bitcast.1.core_ref.refs_0_.refs_1_, s32[32]{0:T(128)} %order_hbm.1, ...), custom_call_target="tpu_custom_call" | custom-call | flops 20000000000 | tf_op jit(solution)/shard_map/first_terms/pallas_call | solution.py:71
  4.0 3.0 %collective-permute-start.1 = (bf16[32,2048]{1,0:T(8,128)(2,1)S(1)}, bf16[32,2048]{1,0:T(8,128)(2,1)S(1)}, u32[]{:S(2)}, u32[]{:S(2)}) collective-permute-start(bf16[32,2048]{1,0:T(8,128)(2,1)S(1)} %get-tuple-element.22), channel_id=1, source_target_pairs={{0,8},{1,17},{2,10},{3,19},{4,12},{5,21},{6,14},{7,23},{8,0},{9,25... | collective-permute-start | bytes 393224 | tf_op jit(solution)/shard_map/ppermute | solution.py:480
  7.1 1.5 %collective-permute-start.2 = (bf16[32,2048]{1,0:T(8,128)(2,1)S(1)}, bf16[32,2048]{1,0:T(8,128)(2,1)S(1)}, u32[]{:S(2)}, u32[]{:S(2)}) collective-permute-start(bf16[32,2048]{1,0:T(8,128)(2,1)S(1)} %get-tuple-element.23), channel_id=1, source_target_pairs={{0,16},{1,9},{2,18},{3,11},{4,20},{5,13},{6,22},{7,15},{8,24},{9,1... | collective-permute-start | bytes 393224 | tf_op jit(solution)/shard_map/ppermute | solution.py:480
  8.6 0.0 collective-permute-start.3
  8.6 0.0 copy-done
  8.6 1.4 %terms.2 = (bf16[2,48,2048]{2,1,0:T(8,128)(2,1)S(1)}, bf16[2,48,2048]{2,1,0:T(8,128)(2,1)S(1)}) custom-call(s32[1]{0:T(128)} %bitcast.1.core_ref.refs_0_.refs_1_, bf16[8,16,8192]{2,1,0:T(8,128)(2,1)S(1)} %get-tuple-element.18.spread.refs_1_, bf16[128,65536]{1,0:T(8,128)(2,1)S(1)} %copy-done), custom_call_target="tpu_custom_call" | custom-call | flops 10000000000 | tf_op jit(solution)/shard_map/terms/pallas_call | solution.py:71
  10.0 2.2 %collective-permute-start = (bf16[2,48,2048]{2,1,0:T(8,128)(2,1)S(1)}, bf16[2,48,2048]{2,1,0:T(8,128)(2,1)S(1)}, u32[]{:S(2)}, u32[]{:S(2)}) collective-permute-start(bf16[2,48,2048]{2,1,0:T(8,128)(2,1)S(1)} %get-tuple-element.20.refs_3_), channel_id=1, source_target_pairs={{0,8},{1,17},{2,10},{3,19},{4,12},{5,21},{6,14},{7,23},{8,0},{9,25... | collective-permute-start | bytes 1179656 | tf_op jit(solution)/shard_map/ppermute | solution.py:480
  12.1 2.3 %terms.3 = (bf16[2,80,2048]{2,1,0:T(8,128)(2,1)S(1)}, bf16[2,80,2048]{2,1,0:T(8,128)(2,1)S(1)}) custom-call(s32[1]{0:T(128)} %bitcast.1.core_ref.refs_0_.refs_1_, bf16[8,16,8192]{2,1,0:T(8,128)(2,1)S(1)} %get-tuple-element.18.spread.refs_1_, bf16[128,65536]{1,0:T(8,128)(2,1)S(1)} %copy-done, bf16[2,48,2048]{2,1,0:T(8,128)(2,1)S(1)} %get-tuple-element.20.refs_3_), custom_call_target="tpu_custom_call" | custom-call | flops 10000000000 | tf_op jit(solution)/shard_map/terms/pallas_call | solution.py:71
  14.4 1.6 %collective-permute-start.8 = (bf16[2,80,2048]{2,1,0:T(8,128)(2,1)S(1)}, bf16[2,80,2048]{2,1,0:T(8,128)(2,1)S(1)}, u32[]{:S(2)}, u32[]{:S(2)}) collective-permute-start(bf16[2,80,2048]{2,1,0:T(8,128)(2,1)S(1)} %get-tuple-element.25.refs_4_), channel_id=1, source_target_pairs={{0,16},{1,9},{2,18},{3,11},{4,20},{5,13},{6,22},{7,15},{8,24},{9,1... | collective-permute-start | bytes 1966088 | tf_op jit(solution)/shard_map/ppermute | solution.py:480
  16.0 0.0 collective-permute-done.1.refs_1_
  16.0 0.0 collective-permute-done.2.refs_2_
  16.0 0.0 collective-permute-done.3.refs_3_
  16.0 0.1 combine.1.refs_2_.refs_1_
  16.1 3.7 %collective-permute-start.7 = (bf16[32,2048]{1,0:T(8,128)(2,1)S(1)}, bf16[32,2048]{1,0:T(8,128)(2,1)S(1)}, u32[]{:S(2)}, u32[]{:S(2)}) collective-permute-start(bf16[32,2048]{1,0:T(8,128)(2,1)S(1)} %combine.1.refs_2_.refs_1_), channel_id=1, source_target_pairs={{0,6},{1,7},{2,4},{3,5},{4,2},{5,3},{6,0},{7,1},{8,14},{9,15},{10,... | collective-permute-start | bytes 393224 | tf_op jit(solution)/shard_map/ppermute | solution.py:448
  19.7 0.0 collective-permute-start.6
  19.7 0.8 %collective-permute-start.5 = (bf16[32,2048]{1,0:T(8,128)(2,1)S(1)}, bf16[32,2048]{1,0:T(8,128)(2,1)S(1)}, u32[]{:S(2)}, u32[]{:S(2)}) collective-permute-start(bf16[32,2048]{1,0:T(8,128)(2,1)S(1)} %combine.1.refs_2_.refs_1_), channel_id=1, source_target_pairs={{0,2},{1,3},{2,0},{3,1},{4,6},{5,7},{6,4},{7,5},{8,10},{9,11},{10,... | collective-permute-start | bytes 393224 | tf_op jit(solution)/shard_map/ppermute | solution.py:448
  20.5 0.0 collective-permute-done.refs_1_
  20.6 2.4 %collective-permute-start.4 = (bf16[1,48,2048]{2,1,0:T(8,128)(2,1)S(1)}, bf16[1,48,2048]{2,1,0:T(8,128)(2,1)S(1)}, u32[]{:S(2)}, u32[]{:S(2)}) collective-permute-start(bf16[1,48,2048]{2,1,0:T(8,128)(2,1)S(1)} %middle.2.refs_2_), channel_id=1, source_target_pairs={{0,16},{1,9},{2,18},{3,11},{4,20},{5,13},{6,22},{7,15},{8,24},{9,1... | collective-permute-start | bytes 589832 | tf_op jit(solution)/shard_map/ppermute | solution.py:480
  23.0 3.1 %collective-permute-done.8.refs_1_.refs_6_ = bf16[2,80,2048]{2,1,0:T(8,128)(2,1)S(1)} collective-permute-done((bf16[2,80,2048]{2,1,0:T(8,128)(2,1)S(1)}, bf16[2,80,2048]{2,1,0:T(8,128)(2,1)S(1)}, u32[]{:S(2)}, u32[]{:S(2)}) %collective-permute-start.8) | collective-permute-done | bytes 655392 | tf_op jit(solution)/shard_map/ppermute | solution.py:480
  26.1 0.1 middle.3.refs_5_
  26.1 1.5 %collective-permute-start.10 = (bf16[1,80,2048]{2,1,0:T(8,128)(2,1)S(1)}, bf16[1,80,2048]{2,1,0:T(8,128)(2,1)S(1)}, u32[]{:S(2)}, u32[]{:S(2)}) collective-permute-start(bf16[1,80,2048]{2,1,0:T(8,128)(2,1)S(1)} %middle.3.refs_5_), channel_id=1, source_target_pairs={{0,8},{1,17},{2,10},{3,19},{4,12},{5,21},{6,14},{7,23},{8,0},{9,25... | collective-permute-start | bytes 983048 | tf_op jit(solution)/shard_map/ppermute | solution.py:480
  27.7 0.0 collective-permute-done.7.refs_4_
  27.7 2.6 %collective-permute-done.6.refs_3_ = bf16[32,2048]{1,0:T(8,128)(2,1)S(1)} collective-permute-done((bf16[32,2048]{1,0:T(8,128)(2,1)S(1)}, bf16[32,2048]{1,0:T(8,128)(2,1)S(1)}, u32[]{:S(2)}, u32[]{:S(2)}) %collective-permute-start.6) | collective-permute-done | bytes 131104 | tf_op jit(solution)/shard_map/ppermute | solution.py:448
  30.3 0.0 collective-permute-done.5.refs_2_
  30.3 0.3 stack_targets.1.refs_2_
  30.6 0.1 collective-permute-start.9
  30.6 0.0 collective-permute-done.4.refs_2_
  30.7 0.1 join.1.refs_4_.refs_0_
  30.7 0.0 copy-start.1
  30.8 2.5 %collective-permute-done.10.refs_7_ = bf16[1,80,2048]{2,1,0:T(8,128)(2,1)S(1)} collective-permute-done((bf16[1,80,2048]{2,1,0:T(8,128)(2,1)S(1)}, bf16[1,80,2048]{2,1,0:T(8,128)(2,1)S(1)}, u32[]{:S(2)}, u32[]{:S(2)}) %collective-permute-start.10) | collective-permute-done | bytes 327712 | tf_op jit(solution)/shard_map/ppermute | solution.py:480
  33.3 0.0 collective-permute-done.9.refs_3_
  33.3 0.5 %gram.1 = (bf16[80,2048]{1,0:T(8,128)(2,1)S(1)}, f32[72,128]{1,0:T(8,128)S(1)}, f32[72,128]{1,0:T(8,128)S(1)}, f32[72,128]{1,0:T(8,128)S(1)}, f32[72,128]{1,0:T(8,128)S(1)}) custom-call(s32[1]{0:T(128)} %bitcast.2.feat_ref.refs_0_, s32[1]{0:T(128)} %bitcast.1.core_ref.refs_0_.refs_1_, bf16[144,2048]{1,0:T(8,128)(2,1)S(1)} %stack_targets.1.refs_2_, ...), custom_call_target="tpu_custom_call" | custom-call | flops 10000000000 | tf_op jit(solution)/shard_map/gram/pallas_call | solution.py:71
  33.8 2.4 %collective-permute-start.11 = (f32[72,128]{1,0:T(8,128)S(1)}, f32[72,128]{1,0:T(8,128)S(1)}, u32[]{:S(2)}, u32[]{:S(2)}) collective-permute-start(f32[72,128]{1,0:T(8,128)S(1)} %get-tuple-element.29), channel_id=1, source_target_pairs={{0,24},{1,25},{2,26},{3,27},{4,28},{5,29},{6,30},{7,31},{8,16},{9,... | collective-permute-start | bytes 110600 | tf_op jit(solution)/shard_map/ppermute | solution.py:480
  36.1 0.7 %collective-permute-start.12 = (f32[72,128]{1,0:T(8,128)S(1)}, f32[72,128]{1,0:T(8,128)S(1)}, u32[]{:S(2)}, u32[]{:S(2)}) collective-permute-start(f32[72,128]{1,0:T(8,128)S(1)} %get-tuple-element.30), channel_id=1, source_target_pairs={{0,8},{1,17},{2,10},{3,19},{4,12},{5,21},{6,14},{7,23},{8,0},{9,25... | collective-permute-start | bytes 110600 | tf_op jit(solution)/shard_map/ppermute | solution.py:480
  36.8 0.5 %collective-permute-start.13 = (f32[72,128]{1,0:T(8,128)S(1)}, f32[72,128]{1,0:T(8,128)S(1)}, u32[]{:S(2)}, u32[]{:S(2)}) collective-permute-start(f32[72,128]{1,0:T(8,128)S(1)} %get-tuple-element.31), channel_id=1, source_target_pairs={{0,16},{1,9},{2,18},{3,11},{4,20},{5,13},{6,22},{7,15},{8,24},{9,1... | collective-permute-start | bytes 110600 | tf_op jit(solution)/shard_map/ppermute | solution.py:480
  37.3 0.0 copy-done.1
  37.3 0.5 %inner_transform.1.projected_ref = bf16[128,2048]{1,0:T(8,128)(2,1)S(1)} custom-call(bf16[256,256]{1,0:T(8,128)(2,1)S(1)} %copy-done.1, bf16[48,2048]{1,0:T(8,128)(2,1)S(1)} %join.1.refs_4_.refs_0_, bf16[80,2048]{1,0:T(8,128)(2,1)S(1)} %get-tuple-element.27.refs_1_), custom_call_target="tpu_custom_call" | custom-call | flops 10000000000 | tf_op jit(solution)/shard_map/inner_transform/pallas_call | solution.py:71
  37.9 0.9 %collective-permute-done.11.refs_1_ = f32[72,128]{1,0:T(8,128)S(1)} collective-permute-done((f32[72,128]{1,0:T(8,128)S(1)}, f32[72,128]{1,0:T(8,128)S(1)}, u32[]{:S(2)}, u32[]{:S(2)}) %collective-permute-start.11) | collective-permute-done | bytes 36896 | tf_op jit(solution)/shard_map/ppermute | solution.py:480
  38.8 1.3 %collective-permute-done.12.refs_2_ = f32[72,128]{1,0:T(8,128)S(1)} collective-permute-done((f32[72,128]{1,0:T(8,128)S(1)}, f32[72,128]{1,0:T(8,128)S(1)}, u32[]{:S(2)}, u32[]{:S(2)}) %collective-permute-start.12) | collective-permute-done | bytes 36896 | tf_op jit(solution)/shard_map/ppermute | solution.py:480
  40.1 0.7 %collective-permute-done.13.refs_3_ = f32[72,128]{1,0:T(8,128)S(1)} collective-permute-done((f32[72,128]{1,0:T(8,128)S(1)}, f32[72,128]{1,0:T(8,128)S(1)}, u32[]{:S(2)}, u32[]{:S(2)}) %collective-permute-start.13) | collective-permute-done | bytes 36896 | tf_op jit(solution)/shard_map/ppermute | solution.py:480
  40.8 1.0 %finish.1 = (bf16[128,2048]{1,0:T(8,128)(2,1)}, f32[64,128]{1,0:T(8,128)}) custom-call(s32[1]{0:T(128)} %bitcast.ex_ref, bf16[128,2048]{1,0:T(8,128)(2,1)S(1)} %inner_transform.1.projected_ref, f32[72,128]{1,0:T(8,128)S(1)} %get-tuple-element.28.refs_0_, f32[72,128]{1,0:T(8,128)S(1)} %collective-permute-done.11.refs_1_, ...), custom_call_target="tpu_custom_call" | custom-call | flops 10000000000 | tf_op jit(solution)/shard_map/finish/pallas_call | solution.py:71
  (1 shorter events, 0.0 us)
Async XLA Ops:
  0.6 8.0 %copy-start = (bf16[128,65536]{1,0:T(8,128)(2,1)S(1)}, bf16[128,65536]{1,0:T(8,128)(2,1)}, u32[]{:S(2)}) copy-start(bf16[128,65536]{1,0:T(8,128)(2,1)} %refs_2_.1) | copy-start | bytes 50331652
  4.0 11.9 %collective-permute-start.1 = (bf16[32,2048]{1,0:T(8,128)(2,1)S(1)}, bf16[32,2048]{1,0:T(8,128)(2,1)S(1)}, u32[]{:S(2)}, u32[]{:S(2)}) collective-permute-start(bf16[32,2048]{1,0:T(8,128)(2,1)S(1)} %get-tuple-element.22), channel_id=1, source_target_pairs={{0,8},{1,17},{2,10},{3,19},{4,12},{5,21},{6,14},{7,23},{8,0},{9,25... | collective-permute-start | bytes 393224 | tf_op jit(solution)/shard_map/ppermute | solution.py:480
  7.1 8.9 %collective-permute-start.2 = (bf16[32,2048]{1,0:T(8,128)(2,1)S(1)}, bf16[32,2048]{1,0:T(8,128)(2,1)S(1)}, u32[]{:S(2)}, u32[]{:S(2)}) collective-permute-start(bf16[32,2048]{1,0:T(8,128)(2,1)S(1)} %get-tuple-element.23), channel_id=1, source_target_pairs={{0,16},{1,9},{2,18},{3,11},{4,20},{5,13},{6,22},{7,15},{8,24},{9,1... | collective-permute-start | bytes 393224 | tf_op jit(solution)/shard_map/ppermute | solution.py:480
  8.6 7.4 %collective-permute-start.3 = (bf16[32,2048]{1,0:T(8,128)(2,1)S(1)}, bf16[32,2048]{1,0:T(8,128)(2,1)S(1)}, u32[]{:S(2)}, u32[]{:S(2)}) collective-permute-start(bf16[32,2048]{1,0:T(8,128)(2,1)S(1)} %get-tuple-element.24), channel_id=1, source_target_pairs={{0,24},{1,25},{2,26},{3,27},{4,28},{5,29},{6,30},{7,31},{8,16},{9,... | collective-permute-start | bytes 393224 | tf_op jit(solution)/shard_map/ppermute | solution.py:480
  10.0 10.6 %collective-permute-start = (bf16[2,48,2048]{2,1,0:T(8,128)(2,1)S(1)}, bf16[2,48,2048]{2,1,0:T(8,128)(2,1)S(1)}, u32[]{:S(2)}, u32[]{:S(2)}) collective-permute-start(bf16[2,48,2048]{2,1,0:T(8,128)(2,1)S(1)} %get-tuple-element.20.refs_3_), channel_id=1, source_target_pairs={{0,8},{1,17},{2,10},{3,19},{4,12},{5,21},{6,14},{7,23},{8,0},{9,25... | collective-permute-start | bytes 1179656 | tf_op jit(solution)/shard_map/ppermute | solution.py:480
  14.4 11.7 %collective-permute-start.8 = (bf16[2,80,2048]{2,1,0:T(8,128)(2,1)S(1)}, bf16[2,80,2048]{2,1,0:T(8,128)(2,1)S(1)}, u32[]{:S(2)}, u32[]{:S(2)}) collective-permute-start(bf16[2,80,2048]{2,1,0:T(8,128)(2,1)S(1)} %get-tuple-element.25.refs_4_), channel_id=1, source_target_pairs={{0,16},{1,9},{2,18},{3,11},{4,20},{5,13},{6,22},{7,15},{8,24},{9,1... | collective-permute-start | bytes 1966088 | tf_op jit(solution)/shard_map/ppermute | solution.py:480
  16.1 11.6 %collective-permute-start.7 = (bf16[32,2048]{1,0:T(8,128)(2,1)S(1)}, bf16[32,2048]{1,0:T(8,128)(2,1)S(1)}, u32[]{:S(2)}, u32[]{:S(2)}) collective-permute-start(bf16[32,2048]{1,0:T(8,128)(2,1)S(1)} %combine.1.refs_2_.refs_1_), channel_id=1, source_target_pairs={{0,6},{1,7},{2,4},{3,5},{4,2},{5,3},{6,0},{7,1},{8,14},{9,15},{10,... | collective-permute-start | bytes 393224 | tf_op jit(solution)/shard_map/ppermute | solution.py:448
  19.7 10.5 %collective-permute-start.6 = (bf16[32,2048]{1,0:T(8,128)(2,1)S(1)}, bf16[32,2048]{1,0:T(8,128)(2,1)S(1)}, u32[]{:S(2)}, u32[]{:S(2)}) collective-permute-start(bf16[32,2048]{1,0:T(8,128)(2,1)S(1)} %combine.1.refs_2_.refs_1_), channel_id=1, source_target_pairs={{0,4},{1,5},{2,6},{3,7},{4,0},{5,1},{6,2},{7,3},{8,12},{9,13},{10,... | collective-permute-start | bytes 393224 | tf_op jit(solution)/shard_map/ppermute | solution.py:448
  19.7 10.5 %collective-permute-start.5 = (bf16[32,2048]{1,0:T(8,128)(2,1)S(1)}, bf16[32,2048]{1,0:T(8,128)(2,1)S(1)}, u32[]{:S(2)}, u32[]{:S(2)}) collective-permute-start(bf16[32,2048]{1,0:T(8,128)(2,1)S(1)} %combine.1.refs_2_.refs_1_), channel_id=1, source_target_pairs={{0,2},{1,3},{2,0},{3,1},{4,6},{5,7},{6,4},{7,5},{8,10},{9,11},{10,... | collective-permute-start | bytes 393224 | tf_op jit(solution)/shard_map/ppermute | solution.py:448
  20.6 10.1 %collective-permute-start.4 = (bf16[1,48,2048]{2,1,0:T(8,128)(2,1)S(1)}, bf16[1,48,2048]{2,1,0:T(8,128)(2,1)S(1)}, u32[]{:S(2)}, u32[]{:S(2)}) collective-permute-start(bf16[1,48,2048]{2,1,0:T(8,128)(2,1)S(1)} %middle.2.refs_2_), channel_id=1, source_target_pairs={{0,16},{1,9},{2,18},{3,11},{4,20},{5,13},{6,22},{7,15},{8,24},{9,1... | collective-permute-start | bytes 589832 | tf_op jit(solution)/shard_map/ppermute | solution.py:480
  26.1 7.1 %collective-permute-start.10 = (bf16[1,80,2048]{2,1,0:T(8,128)(2,1)S(1)}, bf16[1,80,2048]{2,1,0:T(8,128)(2,1)S(1)}, u32[]{:S(2)}, u32[]{:S(2)}) collective-permute-start(bf16[1,80,2048]{2,1,0:T(8,128)(2,1)S(1)} %middle.3.refs_5_), channel_id=1, source_target_pairs={{0,8},{1,17},{2,10},{3,19},{4,12},{5,21},{6,14},{7,23},{8,0},{9,25... | collective-permute-start | bytes 983048 | tf_op jit(solution)/shard_map/ppermute | solution.py:480
  30.6 2.7 %collective-permute-start.9 = (bf16[144,2048]{1,0:T(8,128)(2,1)S(1)}, bf16[144,2048]{1,0:T(8,128)(2,1)S(1)}, u32[]{:S(2)}, u32[]{:S(2)}) collective-permute-start(bf16[144,2048]{1,0:T(8,128)(2,1)S(1)} %stack_targets.1.refs_2_), channel_id=1, source_target_pairs={{0,1},{1,0},{2,3},{3,2},{4,5},{5,4},{6,7},{7,6},{8,9},{9,8},{10,11... | collective-permute-start | bytes 1769480 | tf_op jit(solution)/shard_map/ppermute | solution.py:448
  30.7 6.6 %copy-start.1 = (bf16[256,256]{1,0:T(8,128)(2,1)S(1)}, bf16[256,256]{1,0:T(8,128)(2,1)}, u32[]{:S(2)}) copy-start(bf16[256,256]{1,0:T(8,128)(2,1)} %constant.23.clone.table_ref) | copy-start | bytes 393220
  33.8 5.0 %collective-permute-start.11 = (f32[72,128]{1,0:T(8,128)S(1)}, f32[72,128]{1,0:T(8,128)S(1)}, u32[]{:S(2)}, u32[]{:S(2)}) collective-permute-start(f32[72,128]{1,0:T(8,128)S(1)} %get-tuple-element.29), channel_id=1, source_target_pairs={{0,24},{1,25},{2,26},{3,27},{4,28},{5,29},{6,30},{7,31},{8,16},{9,... | collective-permute-start | bytes 110600 | tf_op jit(solution)/shard_map/ppermute | solution.py:480
  36.1 4.0 %collective-permute-start.12 = (f32[72,128]{1,0:T(8,128)S(1)}, f32[72,128]{1,0:T(8,128)S(1)}, u32[]{:S(2)}, u32[]{:S(2)}) collective-permute-start(f32[72,128]{1,0:T(8,128)S(1)} %get-tuple-element.30), channel_id=1, source_target_pairs={{0,8},{1,17},{2,10},{3,19},{4,12},{5,21},{6,14},{7,23},{8,0},{9,25... | collective-permute-start | bytes 110600 | tf_op jit(solution)/shard_map/ppermute | solution.py:480
  36.8 4.0 %collective-permute-start.13 = (f32[72,128]{1,0:T(8,128)S(1)}, f32[72,128]{1,0:T(8,128)S(1)}, u32[]{:S(2)}, u32[]{:S(2)}) collective-permute-start(f32[72,128]{1,0:T(8,128)S(1)} %get-tuple-element.31), channel_id=1, source_target_pairs={{0,16},{1,9},{2,18},{3,11},{4,20},{5,13},{6,22},{7,15},{8,24},{9,1... | collective-permute-start | bytes 110600 | tf_op jit(solution)/shard_map/ppermute | solution.py:480

commit v6 on v5

--- a/solution.py
+++ b/solution.py
@@ -322,6 +322,15 @@
     )
 
 
+def pieces_of(row):
+    pieces = []
+    for unused in range(3):
+        piece = wide(narrow(row))
+        row = row - piece
+        pieces.append(piece)
+    return pieces
+
+
 def square_sums(value):
     value = wide(value)
     return jnp.sum(value * value, axis=1, keepdims=True)
@@ -362,16 +371,21 @@
     for d, out in enumerate(outs):
         turned = reverse_bits(d, count)
         number = jnp.where(core_ref[0] == 0, d, turned)
+        picked = []
         for i in range(0, 2 * share, per):
             first = pl.multiple_of((i * len(outs)) + (number ^ feat) * per, per)
-            out[pl.ds(i, per), :] = products[pl.ds(first, per), :]
+            picked.append(products[pl.ds(first, per), :])
         straight, crossed = (
             jnp.concatenate([x[:, i * share : (i + 1) * share] for x in target_norms], axis=1) for i in (d, turned)
         )
         here = jnp.concatenate(
             [jnp.where(core_ref[0] == 0, straight, crossed), jnp.zeros((1, rows - 2 * share), jnp.float32)], axis=1
         )
-        out[pl.ds(2 * share, 8), :] = jnp.concatenate([norms, here, jnp.zeros((6, rows), jnp.float32)], axis=0)
+        sums = [norms, here]
+        if d > 0:
+            sums = [piece for row in sums for piece in pieces_of(row)]
+        sums.append(jnp.zeros((out.shape[0] - 2 * share - len(sums), rows), jnp.float32))
+        out[...] = jnp.concatenate([*picked, *sums], axis=0).astype(out.dtype)
 
 
 def gram(feat_count, per, feat, core, mine, other, first, parts):
@@ -386,7 +400,8 @@
     last, *outs = call(
         kernel,
         [jax.ShapeDtypeStruct((last_rows, inner), jnp.bfloat16)]
-        + [jax.ShapeDtypeStruct((total // feat_count + 8, rows), jnp.float32)] * feat_count,
+        + [jax.ShapeDtypeStruct((total // feat_count + 8, rows), jnp.float32)]
+        + [jax.ShapeDtypeStruct((total // feat_count + ROWS, rows), jnp.bfloat16)] * (feat_count - 1),
         [feat, core, mine, other, first, *parts],
         [SMEM, SMEM] + [VMEM] * (3 + len(parts)),
         "gram",
@@ -420,11 +435,16 @@
     count = cosines_ref.shape[0]
     share = count // 2
     sums = parts[0][...]
+    products, train_sums, target_sums = sums[:count], sums[count : count + 1], sums[count + 1 : count + 2]
     for part in parts[1:]:
-        sums = sums + part[...]
-    train_scale = lax.rsqrt(sums[count : count + 1] * mean_scale + EPS)
-    target_scale = lax.rsqrt(sums[count + 1 : count + 2, :count] * mean_scale + EPS)
-    cosines = sums[:count] * train_scale * as_column(target_scale) * mean_scale
+        got = wide(part[...])
+        products = products + got[:count]
+        for i in range(count, count + 3):
+            train_sums = train_sums + got[i : i + 1]
+            target_sums = target_sums + got[i + 3 : i + 4]
+    train_scale = lax.rsqrt(train_sums * mean_scale + EPS)
+    target_scale = lax.rsqrt(target_sums[:, :count] * mean_scale + EPS)
+    cosines = products * train_scale * as_column(target_scale) * mean_scale
     for i in range(count // per):
         group = ex_ref[0] ^ (i * 2 if i * per < share else i * 2 - count // per + 1)
         cosines_ref[pl.ds(pl.multiple_of(group * per, per), per), :] = cosines[i * per : (i + 1) * per]
@@ -481,7 +501,8 @@
 
     target_parts, table = first_terms(feat_count, feat, core, block_order, signs, target_grads)
     own = pltpu.with_memory_space_constraint(target_parts[0], pltpu.VMEM)
-    got = [own] + [turn(target_parts[d], d) for d in range(1, feat_count)]
+    far = sorted(range(1, feat_count), key=lambda d: -d.bit_count())
+    got = [own] + [turn(target_parts[d], d) for d in far]
 
     orders = [bits if i % 2 == 0 else bits[::-1] for i in range(len(CHUNKS))]
     firsts = [sum(CHUNKS[:i]) for i in range(len(CHUNKS))]
@@ -508,7 +529,6 @@
     other = swap(mine, "ex", 1)
     first = join(state[0])
     last, sums = gram(feat_count, per, feat, core, mine, other, first, state[1])
-    far = sorted(range(1, feat_count), key=lambda d: -d.bit_count())
     sums = [sums[0]] + [turn(sums[d], d) for d in far]
     projected = inner_transform(scale, table256, [first, last])
     features, cosines = finish(mean_scale, per, ex.reshape(1), projected, sums)

time: 41.9 us -> 41.4 us (0.988)
    ppermute x10, waiting for transfers between devices: 8.52 us -> 7.81 us  [turn(): return lax.ppermute(value, ('feat', 'ex'), pairs)]
  transfers between devices with their start and end apart: 14 -> 14, of which waited for: 6 -> 7; matrix products, arithmetic and copies ran while one was open for 0% -> 0% of each run, Pallas kernels for 11% -> 12%
where the time goes in v6:
time: 41.4 us; the launch traced here: 41.3 us
  starting transfers between devices  20.2 us (49%)
  waiting for transfers between devices  10.7 us (26%)
  Pallas kernels  9.62 us (23%)
  between operations  0.75 us (2%)
    ppermute x10, starting transfers between devices, turn(): return lax.ppermute(value, ('feat', 'ex'), pairs)  15.7 us
    pallas_call x11, Pallas kernels, call(): pl.pallas_call(body, out_shape=out_shape, in_specs=specs, out_specs=jax.t...  9.62 us
    ppermute x10, waiting for transfers between devices, turn(): return lax.ppermute(value, ('feat', 'ex'), pairs)  7.81 us
    ppermute x4, starting transfers between devices, swap(): lax.ppermute(value, axis, [(i, i ^ distance) for i in range(lax.axis_size...  4.52 us
    ppermute x4, waiting for transfers between devices, swap(): lax.ppermute(value, axis, [(i, i ^ distance) for i in range(lax.axis_size...  2.89 us
  transfers between devices with their start and end apart: 14, of which 7 were waited for; matrix products, arithmetic and copies ran while one was open for 0% of the time, Pallas kernels for 12%

profile of v6, /device:TPU:0, one launch (start us, length us, event | category | flops | bytes accessed | tf_op | source)
XLA Modules:
  0.0 41.3 jit_solution(3070020846579022154)
XLA Ops:
  0.6 0.0 copy-start
  0.7 3.4 %first_terms.1 = (bf16[32,2048]{1,0:T(8,128)(2,1)S(1)}, bf16[32,2048]{1,0:T(8,128)(2,1)S(1)}, bf16[32,2048]{1,0:T(8,128)(2,1)S(1)}, bf16[32,2048]{1,0:T(8,128)(2,1)S(1)}, bf16[8,16,8192]{2,1,0:T(8,128)(2,1)S(1)}) custom-call(s32[1]{0:T(128)} %bitcast.2.feat_ref.refs_0_, s32[1]{0:T(128)} %bitcast.1.core_ref.refs_0_.refs_1_, s32[32]{0:T(128)} %order_hbm.1, ...), custom_call_target="tpu_custom_call" | custom-call | flops 20000000000 | tf_op jit(solution)/shard_map/first_terms/pallas_call | solution.py:71
  4.0 4.0 %collective-permute-start.1 = (bf16[32,2048]{1,0:T(8,128)(2,1)S(1)}, bf16[32,2048]{1,0:T(8,128)(2,1)S(1)}, u32[]{:S(2)}, u32[]{:S(2)}) collective-permute-start(bf16[32,2048]{1,0:T(8,128)(2,1)S(1)} %get-tuple-element.22), channel_id=1, source_target_pairs={{0,24},{1,25},{2,26},{3,27},{4,28},{5,29},{6,30},{7,31},{8,16},{9,... | collective-permute-start | bytes 393224 | tf_op jit(solution)/shard_map/ppermute | solution.py:500
  8.0 0.5 %collective-permute-start.2 = (bf16[32,2048]{1,0:T(8,128)(2,1)S(1)}, bf16[32,2048]{1,0:T(8,128)(2,1)S(1)}, u32[]{:S(2)}, u32[]{:S(2)}) collective-permute-start(bf16[32,2048]{1,0:T(8,128)(2,1)S(1)} %get-tuple-element.23), channel_id=1, source_target_pairs={{0,8},{1,17},{2,10},{3,19},{4,12},{5,21},{6,14},{7,23},{8,0},{9,25... | collective-permute-start | bytes 393224 | tf_op jit(solution)/shard_map/ppermute | solution.py:500
  8.5 0.1 collective-permute-start.3
  8.6 0.0 copy-done
  8.7 1.4 %terms.2 = (bf16[2,48,2048]{2,1,0:T(8,128)(2,1)S(1)}, bf16[2,48,2048]{2,1,0:T(8,128)(2,1)S(1)}) custom-call(s32[1]{0:T(128)} %bitcast.1.core_ref.refs_0_.refs_1_, bf16[8,16,8192]{2,1,0:T(8,128)(2,1)S(1)} %get-tuple-element.18.spread.refs_1_, bf16[128,65536]{1,0:T(8,128)(2,1)S(1)} %copy-done), custom_call_target="tpu_custom_call" | custom-call | flops 10000000000 | tf_op jit(solution)/shard_map/terms/pallas_call | solution.py:71
  10.0 2.1 %collective-permute-start = (bf16[2,48,2048]{2,1,0:T(8,128)(2,1)S(1)}, bf16[2,48,2048]{2,1,0:T(8,128)(2,1)S(1)}, u32[]{:S(2)}, u32[]{:S(2)}) collective-permute-start(bf16[2,48,2048]{2,1,0:T(8,128)(2,1)S(1)} %get-tuple-element.20.refs_3_), channel_id=1, source_target_pairs={{0,8},{1,17},{2,10},{3,19},{4,12},{5,21},{6,14},{7,23},{8,0},{9,25... | collective-permute-start | bytes 1179656 | tf_op jit(solution)/shard_map/ppermute | solution.py:500
  12.1 2.3 %terms.3 = (bf16[2,80,2048]{2,1,0:T(8,128)(2,1)S(1)}, bf16[2,80,2048]{2,1,0:T(8,128)(2,1)S(1)}) custom-call(s32[1]{0:T(128)} %bitcast.1.core_ref.refs_0_.refs_1_, bf16[8,16,8192]{2,1,0:T(8,128)(2,1)S(1)} %get-tuple-element.18.spread.refs_1_, bf16[128,65536]{1,0:T(8,128)(2,1)S(1)} %copy-done, bf16[2,48,2048]{2,1,0:T(8,128)(2,1)S(1)} %get-tuple-element.20.refs_3_), custom_call_target="tpu_custom_call" | custom-call | flops 10000000000 | tf_op jit(solution)/shard_map/terms/pallas_call | solution.py:71
  14.4 1.6 %collective-permute-start.8 = (bf16[2,80,2048]{2,1,0:T(8,128)(2,1)S(1)}, bf16[2,80,2048]{2,1,0:T(8,128)(2,1)S(1)}, u32[]{:S(2)}, u32[]{:S(2)}) collective-permute-start(bf16[2,80,2048]{2,1,0:T(8,128)(2,1)S(1)} %get-tuple-element.25.refs_4_), channel_id=1, source_target_pairs={{0,16},{1,9},{2,18},{3,11},{4,20},{5,13},{6,22},{7,15},{8,24},{9,1... | collective-permute-start | bytes 1966088 | tf_op jit(solution)/shard_map/ppermute | solution.py:500
  16.0 0.0 collective-permute-done.1.refs_1_
  16.0 0.0 collective-permute-done.2.refs_2_
  16.0 0.0 collective-permute-done.3.refs_3_
  16.0 0.1 combine.1.refs_2_.refs_1_
  16.1 3.7 %collective-permute-start.7 = (bf16[32,2048]{1,0:T(8,128)(2,1)S(1)}, bf16[32,2048]{1,0:T(8,128)(2,1)S(1)}, u32[]{:S(2)}, u32[]{:S(2)}) collective-permute-start(bf16[32,2048]{1,0:T(8,128)(2,1)S(1)} %combine.1.refs_2_.refs_1_), channel_id=1, source_target_pairs={{0,6},{1,7},{2,4},{3,5},{4,2},{5,3},{6,0},{7,1},{8,14},{9,15},{10,... | collective-permute-start | bytes 393224 | tf_op jit(solution)/shard_map/ppermute | solution.py:468
  19.7 0.0 collective-permute-start.6
  19.7 0.8 %collective-permute-start.5 = (bf16[32,2048]{1,0:T(8,128)(2,1)S(1)}, bf16[32,2048]{1,0:T(8,128)(2,1)S(1)}, u32[]{:S(2)}, u32[]{:S(2)}) collective-permute-start(bf16[32,2048]{1,0:T(8,128)(2,1)S(1)} %combine.1.refs_2_.refs_1_), channel_id=1, source_target_pairs={{0,2},{1,3},{2,0},{3,1},{4,6},{5,7},{6,4},{7,5},{8,10},{9,11},{10,... | collective-permute-start | bytes 393224 | tf_op jit(solution)/shard_map/ppermute | solution.py:468
  20.5 0.3 collective-permute-done.refs_1_
  20.9 2.1 %collective-permute-start.4 = (bf16[1,48,2048]{2,1,0:T(8,128)(2,1)S(1)}, bf16[1,48,2048]{2,1,0:T(8,128)(2,1)S(1)}, u32[]{:S(2)}, u32[]{:S(2)}) collective-permute-start(bf16[1,48,2048]{2,1,0:T(8,128)(2,1)S(1)} %middle.2.refs_2_), channel_id=1, source_target_pairs={{0,16},{1,9},{2,18},{3,11},{4,20},{5,13},{6,22},{7,15},{8,24},{9,1... | collective-permute-start | bytes 589832 | tf_op jit(solution)/shard_map/ppermute | solution.py:500
  23.0 2.6 %collective-permute-done.8.refs_1_.refs_6_ = bf16[2,80,2048]{2,1,0:T(8,128)(2,1)S(1)} collective-permute-done((bf16[2,80,2048]{2,1,0:T(8,128)(2,1)S(1)}, bf16[2,80,2048]{2,1,0:T(8,128)(2,1)S(1)}, u32[]{:S(2)}, u32[]{:S(2)}) %collective-permute-start.8) | collective-permute-done | bytes 655392 | tf_op jit(solution)/shard_map/ppermute | solution.py:500
  25.5 0.1 middle.3.refs_5_
  25.6 1.7 %collective-permute-start.10 = (bf16[1,80,2048]{2,1,0:T(8,128)(2,1)S(1)}, bf16[1,80,2048]{2,1,0:T(8,128)(2,1)S(1)}, u32[]{:S(2)}, u32[]{:S(2)}) collective-permute-start(bf16[1,80,2048]{2,1,0:T(8,128)(2,1)S(1)} %middle.3.refs_5_), channel_id=1, source_target_pairs={{0,8},{1,17},{2,10},{3,19},{4,12},{5,21},{6,14},{7,23},{8,0},{9,25... | collective-permute-start | bytes 983048 | tf_op jit(solution)/shard_map/ppermute | solution.py:500
  27.4 0.0 collective-permute-done.7.refs_4_
  27.4 2.9 %collective-permute-done.6.refs_3_ = bf16[32,2048]{1,0:T(8,128)(2,1)S(1)} collective-permute-done((bf16[32,2048]{1,0:T(8,128)(2,1)S(1)}, bf16[32,2048]{1,0:T(8,128)(2,1)S(1)}, u32[]{:S(2)}, u32[]{:S(2)}) %collective-permute-start.6) | collective-permute-done | bytes 131104 | tf_op jit(solution)/shard_map/ppermute | solution.py:468
  30.3 0.0 collective-permute-done.5.refs_2_
  30.3 0.3 stack_targets.1.refs_2_
  30.6 0.1 collective-permute-start.9
  30.6 0.0 collective-permute-done.4.refs_2_
  30.7 0.1 join.1.refs_4_.refs_0_
  30.7 0.0 copy-start.1
  30.8 2.0 %collective-permute-done.10.refs_7_ = bf16[1,80,2048]{2,1,0:T(8,128)(2,1)S(1)} collective-permute-done((bf16[1,80,2048]{2,1,0:T(8,128)(2,1)S(1)}, bf16[1,80,2048]{2,1,0:T(8,128)(2,1)S(1)}, u32[]{:S(2)}, u32[]{:S(2)}) %collective-permute-start.10) | collective-permute-done | bytes 327712 | tf_op jit(solution)/shard_map/ppermute | solution.py:500
  32.8 0.0 collective-permute-done.9.refs_3_
  32.8 0.5 %gram.1 = (bf16[80,2048]{1,0:T(8,128)(2,1)S(1)}, f32[72,128]{1,0:T(8,128)S(1)}, bf16[80,128]{1,0:T(8,128)(2,1)S(1)}, bf16[80,128]{1,0:T(8,128)(2,1)S(1)}, bf16[80,128]{1,0:T(8,128)(2,1)S(1)}) custom-call(s32[1]{0:T(128)} %bitcast.2.feat_ref.refs_0_, s32[1]{0:T(128)} %bitcast.1.core_ref.refs_0_.refs_1_, bf16[144,2048]{1,0:T(8,128)(2,1)S(1)} %stack_targets.1.refs_2_, ...), custom_call_target="tpu_custom_call" | custom-call | flops 10000000000 | tf_op jit(solution)/shard_map/gram/pallas_call | solution.py:71
  33.3 1.9 %collective-permute-start.11 = (bf16[80,128]{1,0:T(8,128)(2,1)S(1)}, bf16[80,128]{1,0:T(8,128)(2,1)S(1)}, u32[]{:S(2)}, u32[]{:S(2)}) collective-permute-start(bf16[80,128]{1,0:T(8,128)(2,1)S(1)} %get-tuple-element.29), channel_id=1, source_target_pairs={{0,24},{1,25},{2,26},{3,27},{4,28},{5,29},{6,30},{7,31},{8,16},{9,... | collective-permute-start | bytes 61448 | tf_op jit(solution)/shard_map/ppermute | solution.py:500
  35.2 1.4 %collective-permute-start.12 = (bf16[80,128]{1,0:T(8,128)(2,1)S(1)}, bf16[80,128]{1,0:T(8,128)(2,1)S(1)}, u32[]{:S(2)}, u32[]{:S(2)}) collective-permute-start(bf16[80,128]{1,0:T(8,128)(2,1)S(1)} %get-tuple-element.30), channel_id=1, source_target_pairs={{0,8},{1,17},{2,10},{3,19},{4,12},{5,21},{6,14},{7,23},{8,0},{9,25... | collective-permute-start | bytes 61448 | tf_op jit(solution)/shard_map/ppermute | solution.py:500
  36.5 0.3 collective-permute-start.13
  36.8 0.0 copy-done.1
  36.8 0.5 %inner_transform.1.projected_ref = bf16[128,2048]{1,0:T(8,128)(2,1)S(1)} custom-call(bf16[256,256]{1,0:T(8,128)(2,1)S(1)} %copy-done.1, bf16[48,2048]{1,0:T(8,128)(2,1)S(1)} %join.1.refs_4_.refs_0_, bf16[80,2048]{1,0:T(8,128)(2,1)S(1)} %get-tuple-element.27.refs_1_), custom_call_target="tpu_custom_call" | custom-call | flops 10000000000 | tf_op jit(solution)/shard_map/inner_transform/pallas_call | solution.py:71
  37.4 0.6 %collective-permute-done.11.refs_1_ = bf16[80,128]{1,0:T(8,128)(2,1)S(1)} collective-permute-done((bf16[80,128]{1,0:T(8,128)(2,1)S(1)}, bf16[80,128]{1,0:T(8,128)(2,1)S(1)}, u32[]{:S(2)}, u32[]{:S(2)}) %collective-permute-start.11) | collective-permute-done | bytes 20512 | tf_op jit(solution)/shard_map/ppermute | solution.py:500
  38.0 0.9 %collective-permute-done.12.refs_2_ = bf16[80,128]{1,0:T(8,128)(2,1)S(1)} collective-permute-done((bf16[80,128]{1,0:T(8,128)(2,1)S(1)}, bf16[80,128]{1,0:T(8,128)(2,1)S(1)}, u32[]{:S(2)}, u32[]{:S(2)}) %collective-permute-start.12) | collective-permute-done | bytes 20512 | tf_op jit(solution)/shard_map/ppermute | solution.py:500
  38.9 1.4 %collective-permute-done.13.refs_3_ = bf16[80,128]{1,0:T(8,128)(2,1)S(1)} collective-permute-done((bf16[80,128]{1,0:T(8,128)(2,1)S(1)}, bf16[80,128]{1,0:T(8,128)(2,1)S(1)}, u32[]{:S(2)}, u32[]{:S(2)}) %collective-permute-start.13) | collective-permute-done | bytes 20512 | tf_op jit(solution)/shard_map/ppermute | solution.py:500
  40.3 1.0 %finish.1 = (bf16[128,2048]{1,0:T(8,128)(2,1)}, f32[64,128]{1,0:T(8,128)}) custom-call(s32[1]{0:T(128)} %bitcast.ex_ref, bf16[128,2048]{1,0:T(8,128)(2,1)S(1)} %inner_transform.1.projected_ref, f32[72,128]{1,0:T(8,128)S(1)} %get-tuple-element.28.refs_0_, bf16[80,128]{1,0:T(8,128)(2,1)S(1)} %collective-permute-done.11.refs_1_, ...), custom_call_target="tpu_custom_call" | custom-call | flops 10000000000 | tf_op jit(solution)/shard_map/finish/pallas_call | solution.py:71
  (1 shorter events, 0.0 us)
Async XLA Ops:
  0.6 8.0 %copy-start = (bf16[128,65536]{1,0:T(8,128)(2,1)S(1)}, bf16[128,65536]{1,0:T(8,128)(2,1)}, u32[]{:S(2)}) copy-start(bf16[128,65536]{1,0:T(8,128)(2,1)} %refs_2_.1) | copy-start | bytes 50331652
  4.0 11.9 %collective-permute-start.1 = (bf16[32,2048]{1,0:T(8,128)(2,1)S(1)}, bf16[32,2048]{1,0:T(8,128)(2,1)S(1)}, u32[]{:S(2)}, u32[]{:S(2)}) collective-permute-start(bf16[32,2048]{1,0:T(8,128)(2,1)S(1)} %get-tuple-element.22), channel_id=1, source_target_pairs={{0,24},{1,25},{2,26},{3,27},{4,28},{5,29},{6,30},{7,31},{8,16},{9,... | collective-permute-start | bytes 393224 | tf_op jit(solution)/shard_map/ppermute | solution.py:500
  8.0 8.0 %collective-permute-start.2 = (bf16[32,2048]{1,0:T(8,128)(2,1)S(1)}, bf16[32,2048]{1,0:T(8,128)(2,1)S(1)}, u32[]{:S(2)}, u32[]{:S(2)}) collective-permute-start(bf16[32,2048]{1,0:T(8,128)(2,1)S(1)} %get-tuple-element.23), channel_id=1, source_target_pairs={{0,8},{1,17},{2,10},{3,19},{4,12},{5,21},{6,14},{7,23},{8,0},{9,25... | collective-permute-start | bytes 393224 | tf_op jit(solution)/shard_map/ppermute | solution.py:500
  8.5 7.5 %collective-permute-start.3 = (bf16[32,2048]{1,0:T(8,128)(2,1)S(1)}, bf16[32,2048]{1,0:T(8,128)(2,1)S(1)}, u32[]{:S(2)}, u32[]{:S(2)}) collective-permute-start(bf16[32,2048]{1,0:T(8,128)(2,1)S(1)} %get-tuple-element.24), channel_id=1, source_target_pairs={{0,16},{1,9},{2,18},{3,11},{4,20},{5,13},{6,22},{7,15},{8,24},{9,1... | collective-permute-start | bytes 393224 | tf_op jit(solution)/shard_map/ppermute | solution.py:500
  10.0 10.8 %collective-permute-start = (bf16[2,48,2048]{2,1,0:T(8,128)(2,1)S(1)}, bf16[2,48,2048]{2,1,0:T(8,128)(2,1)S(1)}, u32[]{:S(2)}, u32[]{:S(2)}) collective-permute-start(bf16[2,48,2048]{2,1,0:T(8,128)(2,1)S(1)} %get-tuple-element.20.refs_3_), channel_id=1, source_target_pairs={{0,8},{1,17},{2,10},{3,19},{4,12},{5,21},{6,14},{7,23},{8,0},{9,25... | collective-permute-start | bytes 1179656 | tf_op jit(solution)/shard_map/ppermute | solution.py:500
  14.4 11.1 %collective-permute-start.8 = (bf16[2,80,2048]{2,1,0:T(8,128)(2,1)S(1)}, bf16[2,80,2048]{2,1,0:T(8,128)(2,1)S(1)}, u32[]{:S(2)}, u32[]{:S(2)}) collective-permute-start(bf16[2,80,2048]{2,1,0:T(8,128)(2,1)S(1)} %get-tuple-element.25.refs_4_), channel_id=1, source_target_pairs={{0,16},{1,9},{2,18},{3,11},{4,20},{5,13},{6,22},{7,15},{8,24},{9,1... | collective-permute-start | bytes 1966088 | tf_op jit(solution)/shard_map/ppermute | solution.py:500
  16.1 11.3 %collective-permute-start.7 = (bf16[32,2048]{1,0:T(8,128)(2,1)S(1)}, bf16[32,2048]{1,0:T(8,128)(2,1)S(1)}, u32[]{:S(2)}, u32[]{:S(2)}) collective-permute-start(bf16[32,2048]{1,0:T(8,128)(2,1)S(1)} %combine.1.refs_2_.refs_1_), channel_id=1, source_target_pairs={{0,6},{1,7},{2,4},{3,5},{4,2},{5,3},{6,0},{7,1},{8,14},{9,15},{10,... | collective-permute-start | bytes 393224 | tf_op jit(solution)/shard_map/ppermute | solution.py:468
  19.7 10.5 %collective-permute-start.6 = (bf16[32,2048]{1,0:T(8,128)(2,1)S(1)}, bf16[32,2048]{1,0:T(8,128)(2,1)S(1)}, u32[]{:S(2)}, u32[]{:S(2)}) collective-permute-start(bf16[32,2048]{1,0:T(8,128)(2,1)S(1)} %combine.1.refs_2_.refs_1_), channel_id=1, source_target_pairs={{0,4},{1,5},{2,6},{3,7},{4,0},{5,1},{6,2},{7,3},{8,12},{9,13},{10,... | collective-permute-start | bytes 393224 | tf_op jit(solution)/shard_map/ppermute | solution.py:468
  19.7 10.5 %collective-permute-start.5 = (bf16[32,2048]{1,0:T(8,128)(2,1)S(1)}, bf16[32,2048]{1,0:T(8,128)(2,1)S(1)}, u32[]{:S(2)}, u32[]{:S(2)}) collective-permute-start(bf16[32,2048]{1,0:T(8,128)(2,1)S(1)} %combine.1.refs_2_.refs_1_), channel_id=1, source_target_pairs={{0,2},{1,3},{2,0},{3,1},{4,6},{5,7},{6,4},{7,5},{8,10},{9,11},{10,... | collective-permute-start | bytes 393224 | tf_op jit(solution)/shard_map/ppermute | solution.py:468
  20.9 9.8 %collective-permute-start.4 = (bf16[1,48,2048]{2,1,0:T(8,128)(2,1)S(1)}, bf16[1,48,2048]{2,1,0:T(8,128)(2,1)S(1)}, u32[]{:S(2)}, u32[]{:S(2)}) collective-permute-start(bf16[1,48,2048]{2,1,0:T(8,128)(2,1)S(1)} %middle.2.refs_2_), channel_id=1, source_target_pairs={{0,16},{1,9},{2,18},{3,11},{4,20},{5,13},{6,22},{7,15},{8,24},{9,1... | collective-permute-start | bytes 589832 | tf_op jit(solution)/shard_map/ppermute | solution.py:500
  25.6 7.1 %collective-permute-start.10 = (bf16[1,80,2048]{2,1,0:T(8,128)(2,1)S(1)}, bf16[1,80,2048]{2,1,0:T(8,128)(2,1)S(1)}, u32[]{:S(2)}, u32[]{:S(2)}) collective-permute-start(bf16[1,80,2048]{2,1,0:T(8,128)(2,1)S(1)} %middle.3.refs_5_), channel_id=1, source_target_pairs={{0,8},{1,17},{2,10},{3,19},{4,12},{5,21},{6,14},{7,23},{8,0},{9,25... | collective-permute-start | bytes 983048 | tf_op jit(solution)/shard_map/ppermute | solution.py:500
  30.6 2.2 %collective-permute-start.9 = (bf16[144,2048]{1,0:T(8,128)(2,1)S(1)}, bf16[144,2048]{1,0:T(8,128)(2,1)S(1)}, u32[]{:S(2)}, u32[]{:S(2)}) collective-permute-start(bf16[144,2048]{1,0:T(8,128)(2,1)S(1)} %stack_targets.1.refs_2_), channel_id=1, source_target_pairs={{0,1},{1,0},{2,3},{3,2},{4,5},{5,4},{6,7},{7,6},{8,9},{9,8},{10,11... | collective-permute-start | bytes 1769480 | tf_op jit(solution)/shard_map/ppermute | solution.py:468
  30.7 6.1 %copy-start.1 = (bf16[256,256]{1,0:T(8,128)(2,1)S(1)}, bf16[256,256]{1,0:T(8,128)(2,1)}, u32[]{:S(2)}) copy-start(bf16[256,256]{1,0:T(8,128)(2,1)} %constant.23.clone.table_ref) | copy-start | bytes 393220
  33.3 4.7 %collective-permute-start.11 = (bf16[80,128]{1,0:T(8,128)(2,1)S(1)}, bf16[80,128]{1,0:T(8,128)(2,1)S(1)}, u32[]{:S(2)}, u32[]{:S(2)}) collective-permute-start(bf16[80,128]{1,0:T(8,128)(2,1)S(1)} %get-tuple-element.29), channel_id=1, source_target_pairs={{0,24},{1,25},{2,26},{3,27},{4,28},{5,29},{6,30},{7,31},{8,16},{9,... | collective-permute-start | bytes 61448 | tf_op jit(solution)/shard_map/ppermute | solution.py:500
  35.2 3.8 %collective-permute-start.12 = (bf16[80,128]{1,0:T(8,128)(2,1)S(1)}, bf16[80,128]{1,0:T(8,128)(2,1)S(1)}, u32[]{:S(2)}, u32[]{:S(2)}) collective-permute-start(bf16[80,128]{1,0:T(8,128)(2,1)S(1)} %get-tuple-element.30), channel_id=1, source_target_pairs={{0,8},{1,17},{2,10},{3,19},{4,12},{5,21},{6,14},{7,23},{8,0},{9,25... | collective-permute-start | bytes 61448 | tf_op jit(solution)/shard_map/ppermute | solution.py:500
  36.5 3.8 %collective-permute-start.13 = (bf16[80,128]{1,0:T(8,128)(2,1)S(1)}, bf16[80,128]{1,0:T(8,128)(2,1)S(1)}, u32[]{:S(2)}, u32[]{:S(2)}) collective-permute-start(bf16[80,128]{1,0:T(8,128)(2,1)S(1)} %get-tuple-element.31), channel_id=1, source_target_pairs={{0,16},{1,9},{2,18},{3,11},{4,20},{5,13},{6,22},{7,15},{8,24},{9,1... | collective-permute-start | bytes 61448 | tf_op jit(solution)/shard_map/ppermute | solution.py:500
